TPU v7x, 32 devices: a whole 2x2x4 slice. The times are simulated.
32 devices in a mesh: dp: 32 (over z, y, x, core).
Axes of the slice: x: 2, y: 2, z: 4, core: 2. Of those that a mesh axis runs over, the one named last changes fastest.
Arguments:
- embeddings: float32 [65536, 1024], P('dp'), may hold values from -400 to 400
- start_block: float32 [1024, 256], replicated, may hold values from -6 to 6
Outputs:
- axes_out: float32 [1024, 256], replicated
- scores_out: float32 [65536, 256], P('dp')
All inputs are finite; a program needn't handle non-finite values.
Results may differ from a plain program's by a relative error of at most 0.0001.
Values sent between devices are 32-bit elements; how exact they have to be, the bound alone decides.
No kernel may reach another device: no remote copies, remote signals or barrier semaphores. Data moves between devices by JAX's collectives and lax.ppermute only.
A program may use at most 64 MiB of HBM per device.

v0:
```python
import math

import jax
import jax.numpy as jnp
from jax import lax
from jax.sharding import PartitionSpec as P

ITERS = 2


def exact_dot(first, second):
    return jnp.dot(
        first, second, precision=lax.Precision.HIGHEST, preferred_element_type=jnp.float32
    )


def inner_dot(first, second):
    return lax.dot_general(
        first,
        second,
        (((0,), (0,)), ((), ())),
        precision=lax.Precision.HIGHEST,
        preferred_element_type=jnp.float32,
    )


def factor(gram_matrix):
    lower_factor = jnp.linalg.cholesky(gram_matrix)
    identity = jnp.eye(gram_matrix.shape[0], dtype=jnp.float32)
    return jax.scipy.linalg.solve_triangular(lower_factor, identity, lower=True).T


def body(embeddings, start_block):
    devices = lax.axis_size("dp")
    columns = embeddings.shape[1]
    rows_total = embeddings.shape[0] * devices
    current_basis = start_block
    left_basis = None
    for iteration in range(ITERS):
        projected = exact_dot(embeddings, current_basis)
        gram_matrix = lax.psum(inner_dot(projected, projected), "dp")
        inverse = factor(gram_matrix)
        left_basis = exact_dot(projected, inverse)
        summed = lax.psum(inner_dot(embeddings, left_basis), "dp")
        cross_gram = inner_dot(summed, summed)
        current_basis = exact_dot(summed, factor(cross_gram))
    return (current_basis * math.sqrt(columns), left_basis * math.sqrt(rows_total))


def solution(mesh):
    in_specs = (P("dp", None), P())
    out_specs = (P(), P("dp", None))
    return jax.shard_map(body, mesh=mesh, in_specs=in_specs, out_specs=out_specs, check_vma=False)
```

profile of v0, /device:TPU:0, one launch (start us, length us, event | category | flops | bytes accessed | tf_op | source)
XLA Modules:
  0.0 865.9 jit_solution(14387491601591342755)
XLA Ops:
  8.4 9.0 %fusion.56 = f32[2048,256]{1,0:T(8,128)S(1)} fusion(f32[2048,1024]{1,0:T(8,128)} %param.5, f32[1024,256]{1,0:T(8,128)S(1)} %copy-done), kind=kOutput, calls=%fused_computation.125 | convolution fusion | flops 6442450944 | bytes 11534336 | tf_op jit(solution)/shard_map/dot_general | solution.py:12
  17.5 4.2 fusion.57
  22.2 127.2 %all-reduce.6.cloned.1.call-done = f32[256,256]{0,1:T(8,128)} async-done(((f32[256,256]{0,1:T(8,128)}), f32[256,256]{0,1:T(8,128)}) %all-reduce.6.cloned.1.call-update) | async-done | bytes 262160 | tf_op jit(solution)/shard_map/psum | solution.py:41
  153.0 11.7 %cholesky.214 = f32[128,128]{1,0:T(8,128)S(1)} custom-call(f32[128,128]{1,0:T(8,128)S(1)} %cholesky.346), custom_call_target="Cholesky" | custom-call | tf_op jit(solution)/shard_map/jit(cholesky)/cholesky | solution.py:28
  164.8 10.4 %custom-call.17 = f32[1,128,128]{1,2,0:T(8,128)} custom-call(f32[1,128,128]{2,1,0:T(8,128)S(1)} %get-tuple-element.89), custom_call_target="InvertDiagBlocksLowerTriangular" | custom-call | tf_op jit(solution)/shard_map/jit(cholesky)/cholesky | solution.py:28
  178.8 11.7 %cholesky.231 = f32[128,128]{1,0:T(8,128)S(1)} custom-call(f32[128,128]{1,0:T(8,128)S(1)} %convolution_subtract_fusion.7), custom_call_target="Cholesky" | custom-call | tf_op jit(solution)/shard_map/jit(cholesky)/cholesky | solution.py:28
  195.0 6.0 while.8
  201.7 20.5 %custom-call.18 = f32[2,128,128]{1,2,0:T(8,128)S(1)} custom-call(f32[2,128,128]{2,1,0:T(8,128)} %copy-done.5), custom_call_target="InvertDiagBlocksLowerTriangular" | custom-call | tf_op jit(solution)/shard_map/jit(_solve_triangular)/triangular_solve | solution.py:30
  225.7 10.3 %convolution_bitcast_fusion.1 = f32[1024,256]{0,1:T(8,128)} fusion(f32[2048,256]{1,0:T(8,128)S(1)} %fusion, f32[2048,1024]{1,0:T(8,128)} %param.5), kind=kOutput, calls=%fused_computation.9 | convolution fusion | flops 6442450944 | bytes 11534336 | tf_op jit(solution)/shard_map/dot_general | solution.py:18
  236.3 128.8 %all-reduce.8.cloned.1.call-done = f32[1024,256]{0,1:T(8,128)} async-done(((f32[1024,256]{0,1:T(8,128)}), f32[1024,256]{0,1:T(8,128)}) %all-reduce.8.cloned.1.call-update) | async-done | bytes 1048592 | tf_op jit(solution)/shard_map/psum | solution.py:44
  365.1 2.6 fusion.58
  367.9 11.7 %cholesky.248 = f32[128,128]{1,0:T(8,128)S(1)} custom-call(f32[128,128]{1,0:T(8,128)S(1)} %cholesky.349), custom_call_target="Cholesky" | custom-call | tf_op jit(solution)/shard_map/jit(cholesky)/cholesky | solution.py:28
  379.7 9.8 %custom-call.19 = f32[1,128,128]{1,2,0:T(8,128)S(1)} custom-call(f32[1,128,128]{2,1,0:T(8,128)S(1)} %get-tuple-element.85), custom_call_target="InvertDiagBlocksLowerTriangular" | custom-call | tf_op jit(solution)/shard_map/jit(cholesky)/cholesky | solution.py:28
  390.0 11.7 %cholesky.265 = f32[128,128]{1,0:T(8,128)S(1)} custom-call(f32[128,128]{1,0:T(8,128)S(1)} %convolution_subtract_fusion.6), custom_call_target="Cholesky" | custom-call | tf_op jit(solution)/shard_map/jit(cholesky)/cholesky | solution.py:28
  404.3 4.2 while.9
  408.5 19.7 %custom-call.20 = f32[2,128,128]{1,2,0:T(8,128)S(1)} custom-call(f32[2,128,128]{2,1,0:T(8,128)S(1)} %get-tuple-element.31), custom_call_target="InvertDiagBlocksLowerTriangular" | custom-call | tf_op jit(solution)/shard_map/jit(_solve_triangular)/triangular_solve | solution.py:30
  430.9 16.0 %fusion.59 = f32[256,2048]{1,0:T(8,128)S(1)} fusion(f32[1024,256]{1,0:T(8,128)S(1)} %fusion.4, f32[2048,1024]{1,0:T(8,128)} %param.5), kind=kOutput, calls=%fused_computation.128 | convolution fusion | flops 6442450944 | bytes 11534336 | tf_op jit(solution)/shard_map/dot_general | solution.py:12
  449.6 124.1 %all-reduce.10.cloned.1.call-done = f32[256,256]{0,1:T(8,128)} async-done(((f32[256,256]{0,1:T(8,128)}), f32[256,256]{0,1:T(8,128)}) %all-reduce.10.cloned.1.call-update) | async-done | bytes 262160 | tf_op jit(solution)/shard_map/psum | solution.py:41
  577.3 11.7 %cholesky.282 = f32[128,128]{1,0:T(8,128)S(1)} custom-call(f32[128,128]{1,0:T(8,128)S(1)} %cholesky.352), custom_call_target="Cholesky" | custom-call | tf_op jit(solution)/shard_map/jit(cholesky)/cholesky | solution.py:28
  589.8 9.8 %custom-call.21 = f32[1,128,128]{1,2,0:T(8,128)S(1)} custom-call(f32[1,128,128]{2,1,0:T(8,128)S(1)} %get-tuple-element.81), custom_call_target="InvertDiagBlocksLowerTriangular" | custom-call | tf_op jit(solution)/shard_map/jit(cholesky)/cholesky | solution.py:28
  602.4 11.7 %cholesky.299 = f32[128,128]{1,0:T(8,128)S(1)} custom-call(f32[128,128]{1,0:T(8,128)S(1)} %convolution_subtract_fusion.5), custom_call_target="Cholesky" | custom-call | tf_op jit(solution)/shard_map/jit(cholesky)/cholesky | solution.py:28
  619.1 6.1 while.10
  625.9 20.5 %custom-call.22 = f32[2,128,128]{1,2,0:T(8,128)S(1)} custom-call(f32[2,128,128]{2,1,0:T(8,128)} %copy-done.6), custom_call_target="InvertDiagBlocksLowerTriangular" | custom-call | tf_op jit(solution)/shard_map/jit(_solve_triangular)/triangular_solve | solution.py:30
  648.1 4.8 broadcast_multiply_fusion
  652.9 10.7 %convolution_bitcast_fusion = f32[1024,256]{0,1:T(8,128)} fusion(f32[2048,256]{1,0:T(8,128)S(1)} %get-tuple-element.99, f32[2048,1024]{1,0:T(8,128)} %param.5), kind=kOutput, calls=%fused_computation.8 | convolution fusion | flops 6442450944 | bytes 11534336 | tf_op jit(solution)/shard_map/dot_general | solution.py:18
  663.6 129.0 %all-reduce.12.cloned.1.call-done = f32[1024,256]{0,1:T(8,128)} async-done(((f32[1024,256]{0,1:T(8,128)}), f32[1024,256]{0,1:T(8,128)}) %all-reduce.12.cloned.1.call-update) | async-done | bytes 1048592 | tf_op jit(solution)/shard_map/psum | solution.py:44
  795.4 11.7 %cholesky.316 = f32[128,128]{1,0:T(8,128)S(1)} custom-call(f32[128,128]{1,0:T(8,128)S(1)} %cholesky.355), custom_call_target="Cholesky" | custom-call | tf_op jit(solution)/shard_map/jit(cholesky)/cholesky | solution.py:28
  807.2 9.8 %custom-call.23 = f32[1,128,128]{1,2,0:T(8,128)S(1)} custom-call(f32[1,128,128]{2,1,0:T(8,128)S(1)} %get-tuple-element.77), custom_call_target="InvertDiagBlocksLowerTriangular" | custom-call | tf_op jit(solution)/shard_map/jit(cholesky)/cholesky | solution.py:28
  817.5 11.7 %cholesky.333 = f32[128,128]{1,0:T(8,128)S(1)} custom-call(f32[128,128]{1,0:T(8,128)S(1)} %convolution_subtract_fusion.4), custom_call_target="Cholesky" | custom-call | tf_op jit(solution)/shard_map/jit(cholesky)/cholesky | solution.py:28
  831.8 3.8 while.11
  835.6 19.8 %custom-call.24 = f32[2,128,128]{1,2,0:T(8,128)S(1)} custom-call(f32[2,128,128]{2,1,0:T(8,128)S(1)} %get-tuple-element.33), custom_call_target="InvertDiagBlocksLowerTriangular" | custom-call | tf_op jit(solution)/shard_map/jit(_solve_triangular)/triangular_solve | solution.py:30
  856.4 2.8 convolution_multiply_fusion
  (112 shorter events, 61.8 us)
Async XLA Ops:
  7.2 1.2 copy-start
  7.2 142.3 %all-reduce.6.cloned.1.call-start = ((), (), s32[]{:S(2)}) async-start(), calls=%async_computation | async-start | bytes 524288 | tf_op jit(solution)/shard_map/psum | solution.py:41
  21.6 343.5 %all-reduce.8.cloned.1.call-start = ((), (), s32[]{:S(2)}) async-start(), calls=%async_computation.1 | async-start | bytes 2097152 | tf_op jit(solution)/shard_map/psum | solution.py:44
  152.3 0.7 copy-start.3
  201.0 0.7 copy-start.5
  236.1 337.7 %all-reduce.10.cloned.1.call-start = ((), (), s32[]{:S(2)}) async-start(), calls=%async_computation.2 | async-start | bytes 524288 | tf_op jit(solution)/shard_map/psum | solution.py:41
  367.9 61.2 %copy-start.2 = (f32[1024,256]{0,1:T(8,128)S(1)}, f32[1024,256]{0,1:T(8,128)}, u32[]{:S(2)}) copy-start(f32[1024,256]{0,1:T(8,128)} %all-reduce.8.cloned.1.call-done) | copy-start | bytes 3145732
  449.5 343.1 %all-reduce.12.cloned.1.call-start = ((), (), s32[]{:S(2)}) async-start(), calls=%async_computation.3 | async-start | bytes 2097152 | tf_op jit(solution)/shard_map/psum | solution.py:44
  576.6 0.7 copy-start.4
  625.2 0.7 copy-start.6
  795.4 61.0 %copy-start.1 = (f32[1024,256]{0,1:T(8,128)S(1)}, f32[1024,256]{0,1:T(8,128)}, u32[]{:S(2)}) copy-start(f32[1024,256]{0,1:T(8,128)} %all-reduce.12.cloned.1.call-done) | copy-start | bytes 3145732
Sparse Core Ops, SparseCore 0:
  21.8 127.6 all-reduce.5
  236.2 128.8 all-reduce.7
  449.7 124.0 all-reduce.9
  663.7 128.8 all-reduce.11
where the time goes:
time: 872 us; the launch traced here: 866 us
  waiting for transfers between devices  509 us (58%)
  other arithmetic  226 us (26%)
  matrix products  80.9 us (9%)
  local copies, waits for them, and re-layouts  28.5 us (3%)
  between operations  19.5 us (2%)
    psum x2, waiting for transfers between devices, body(): summed = lax.psum(inner_dot(embeddings, left_basis), 'dp')  258 us
    psum x2, waiting for transfers between devices, body(): gram_matrix = lax.psum(inner_dot(projected, projected), 'dp')  251 us
    another operation x27, other arithmetic, factor(): lower_factor = jnp.linalg.cholesky(gram_matrix)  140 us
    another operation x9, other arithmetic, factor(): jax.scipy.linalg.solve_triangular(lower_factor, identity, lower=True)  83.9 us
    dot_general x6, matrix products, exact_dot(): jnp.dot(first, second, precision=lax.Precision.HIGHEST, preferred_element...  36.3 us
    dot_general x6, matrix products, inner_dot(): lax.dot_general(first, second, (((0,), (0,)), ((), ())), precision=lax.Pr...  32.9 us
    another operation x29, local copies, waits for them, and re-layouts, factor(): jax.scipy.linalg.solve_triangular(lower_factor, identity, lower=True)  19.3 us
  transfers between devices with their start and end apart: 4, of which 4 were waited for; matrix products, arithmetic and copies ran while one was open for 0% of the time, Pallas kernels for 0%

commit v1 on v0

v1 whole, which is shorter than its diff:
```python
import functools
import math

import jax
import jax.numpy as jnp
from jax import lax
from jax.experimental import pallas as pl
from jax.experimental.pallas import tpu as pltpu
from jax.sharding import PartitionSpec as P

ITERS = 2
BLOCK = 32
SUB = 8
LANES = 128
TILE = 256
VMEM_LIMIT = 48 * 1024 * 1024


def dot(left, right, contract=(1, 0)):
    dims = (((contract[0],), (contract[1],)), ((), ()))
    return lax.dot_general(left, right, dims, preferred_element_type=jnp.float32)


def split2(x):
    high = x.astype(jnp.bfloat16)
    return high, (x - high.astype(jnp.float32)).astype(jnp.bfloat16)


def split3(x):
    high = x.astype(jnp.bfloat16)
    rest = x - high.astype(jnp.float32)
    middle = rest.astype(jnp.bfloat16)
    return high, middle, (rest - middle.astype(jnp.float32)).astype(jnp.bfloat16)


def dot3(left, right, contract=(1, 0)):
    left_high, left_low = left
    right_high, right_low = right
    return (
        dot(left_high, right_high, contract)
        + dot(left_high, right_low, contract)
        + dot(left_low, right_high, contract)
    )


def outer6(left, right):
    lh, lm, ll = split3(left)
    rh, rm, rl = split3(right)
    return dot(
        jnp.concatenate([lh, lh, lm, lm, lh, ll], 0),
        jnp.concatenate([rh, rm, rh, rm, rl, rh], 0),
        (0, 0),
    )


def eliminate(first, second):
    lane = lax.broadcasted_iota(jnp.int32, (1, LANES), 1)
    for base in range(0, BLOCK, SUB):
        height = BLOCK - base
        row = lax.broadcasted_iota(jnp.int32, (height, LANES), 0)
        ra, rb = first[base:], second[base:]
        cols = [
            jnp.broadcast_to(ra[:, base + k : base + k + 1], (height, LANES)) for k in range(SUB)
        ]
        for k in range(SUB):
            scale = lax.rsqrt(cols[k][k : k + 1])
            mult = jnp.where(row > k, cols[k] * scale, 0.0)
            here = lane == base + k
            pa = jnp.where(here, scale, ra[k : k + 1] * scale)
            pb = rb[k : k + 1] * scale
            for q in range(k + 1, SUB):
                cols[q] = cols[q] - mult * (cols[q][k : k + 1] * scale)
            ra = jnp.where(here & (row > k), 0.0, ra) - mult * pa
            rb = rb - mult * pb
            ra = jnp.where(row == k, pa, ra)
            rb = jnp.where(row == k, pb, rb)
        first = jnp.concatenate([first[:base], ra], 0) if base else ra
        second = jnp.concatenate([second[:base], rb], 0) if base else rb
    return first, second


def invert_factor(a_ref):
    n = a_ref.shape[0]

    def step(index, carry):
        start = pl.multiple_of(index * BLOCK, BLOCK)
        rows = pltpu.roll(a_ref[pl.ds(start, BLOCK), :], lax.rem(n - start, n), 1)
        done = jnp.concatenate(eliminate(rows[:, :LANES], rows[:, LANES:]), 1)
        lane = lax.broadcasted_iota(jnp.int32, (BLOCK, n), 1)
        row = lax.broadcasted_iota(jnp.int32, (BLOCK, n), 0)
        upper = jnp.where((lane >= BLOCK) & (lane < n - start), done, 0.0)
        done = jnp.where((lane < BLOCK) & (lane > row), 0.0, done)
        done = pltpu.roll(done, start, 1)
        update = outer6(pltpu.roll(upper, start, 1), done)
        col = lax.broadcasted_iota(jnp.int32, (n, n), 1)
        row = lax.broadcasted_iota(jnp.int32, (n, n), 0)
        gone = (row >= start + BLOCK) & (col >= start) & (col < start + BLOCK)
        a_ref[...] = jnp.where(gone, 0.0, a_ref[...]) - update
        a_ref[pl.ds(start, BLOCK), :] = done
        return carry

    lax.fori_loop(0, n // BLOCK, step, 0)
    col = lax.broadcasted_iota(jnp.int32, (n, n), 1)
    row = lax.broadcasted_iota(jnp.int32, (n, n), 0)
    a_ref[...] = jnp.where(col <= row, a_ref[...], 0.0)


def lower_blocks(blocks):
    return [(i, j) for j in range(blocks) for i in range(j, blocks)]


def moments_kernel(me_ref, e_ref, out_ref, sums):
    blocks = e_ref.shape[1] // TILE
    step = pl.program_id(0)

    @pl.when(step == 0)
    def _():
        sums[...] = jnp.zeros_like(sums)

    flipped = [split2(e_ref[:, i * TILE : (i + 1) * TILE].T) for i in range(blocks)]
    for j in range(blocks):
        right = split2(e_ref[:, j * TILE : (j + 1) * TILE])
        for i in range(j, blocks):
            place = lower_blocks(blocks).index((i, j)) * TILE
            sums[place : place + TILE, :] += dot3(flipped[i], right)

    @pl.when(step == pl.num_programs(0) - 1)
    def _():
        pieces, rows, _ = out_ref.shape
        for piece in range(pieces):
            out_ref[piece ^ me_ref[0]] = sums[piece * rows : (piece + 1) * rows, :]


def moments(embeddings, me, pieces):
    rows, columns = embeddings.shape
    blocks = columns // TILE
    packed = TILE * blocks * (blocks + 1) // 2
    step = min(512, rows)
    shape = (pieces, packed // pieces, TILE)
    return pl.pallas_call(
        moments_kernel,
        grid=(rows // step,),
        in_specs=[
            pl.BlockSpec(memory_space=pltpu.SMEM),
            pl.BlockSpec((step, columns), lambda i: (i, 0)),
        ],
        out_specs=pl.BlockSpec(shape, lambda i: (0, 0, 0)),
        out_shape=jax.ShapeDtypeStruct(shape, jnp.float32),
        scratch_shapes=[pltpu.VMEM((packed, TILE), jnp.float32)],
        compiler_params=pltpu.CompilerParams(vmem_limit_bytes=VMEM_LIMIT),
        name="moments",
    )(me, embeddings)


def exchange(x, flip, devices):
    return lax.ppermute(x, "dp", [(d, d ^ flip) for d in range(devices)])


def phases(bits):
    groups = [[0]] if bits else []
    return groups + [list(range(b, min(b + 2, bits))) for b in range(1, bits, 2)]


def spread(value, group):
    return sum(((value >> place) & 1) << bit for place, bit in enumerate(group))


def sum_over_devices(x, devices, scattered):
    bits = devices.bit_length() - 1
    pieces, rows, columns = x.shape
    for group in phases(scattered):
        size = 1 << len(group)
        x = x.reshape(-1, size, rows, columns)
        mine = x[:, 0]
        others = [exchange(x[:, d], spread(d, group), devices) for d in range(1, size)]
        for other in others:
            mine = mine + other
        x = mine
    x = x.reshape(rows, columns)
    for bit in range(scattered, bits):
        x = x + exchange(x, 1 << bit, devices)
    x = x[None]
    for group in reversed(phases(scattered)):
        size = 1 << len(group)
        parts = [x] + [exchange(x, spread(d, group), devices) for d in range(1, size)]
        x = jnp.stack(parts, 1).reshape(-1, rows, columns)
    return x


def iterate_kernel(me_ref, c_ref, start_ref, axes_ref, weights_ref, packed, c_high, c_low, basis, work, gram, cross):
    pieces, rows, _ = c_ref.shape
    columns, width = start_ref.shape
    blocks = columns // TILE
    for piece in range(pieces):
        packed[piece * rows : (piece + 1) * rows, :] = c_ref[piece ^ me_ref[0]]
    for place, (i, j) in enumerate(lower_blocks(blocks)):
        block = packed[place * TILE : (place + 1) * TILE, :]
        at_i, at_j = pl.ds(i * TILE, TILE), pl.ds(j * TILE, TILE)
        if i == j:
            row = lax.broadcasted_iota(jnp.int32, block.shape, 0)
            col = lax.broadcasted_iota(jnp.int32, block.shape, 1)
            block = jnp.where(row >= col, block, block.T)
        high, low = split2(block)
        c_high[at_i, at_j] = high
        c_low[at_i, at_j] = low
        if i != j:
            high, low = split2(block.T)
            c_high[at_j, at_i] = high
            c_low[at_j, at_i] = low
    basis[...] = start_ref[...]

    def iteration(index, carry):
        current = split2(basis[...])

        def multiply(tile, carry):
            at = pl.ds(pl.multiple_of(tile * TILE, TILE), TILE)
            work[at, :] = dot3((c_high[at, :], c_low[at, :]), current)
            return carry

        lax.fori_loop(0, blocks, multiply, 0)
        gram[...] = dot3(current, split2(work[...]), (0, 0))
        invert_factor(gram)
        inverse = split2(gram[...])
        weights_ref[...] = dot3(current, inverse, (1, 1))
        summed = dot3(split2(work[...]), inverse, (1, 1))
        parts = split2(summed)
        cross[...] = dot3(parts, parts, (0, 0))
        invert_factor(cross)
        basis[...] = dot3(parts, split2(cross[...]), (1, 1))
        return carry

    lax.fori_loop(0, ITERS, iteration, 0)
    axes_ref[...] = basis[...] * math.sqrt(columns)


def iterate(summed, start_block, me):
    columns, width = start_block.shape
    pieces, rows, _ = summed.shape
    whole = jax.ShapeDtypeStruct((columns, width), jnp.float32)
    return pl.pallas_call(
        iterate_kernel,
        in_specs=[
            pl.BlockSpec(memory_space=pltpu.SMEM),
            pl.BlockSpec(memory_space=pltpu.VMEM),
            pl.BlockSpec(memory_space=pltpu.VMEM),
        ],
        out_specs=[pl.BlockSpec(memory_space=pltpu.VMEM)] * 2,
        out_shape=[whole, whole],
        scratch_shapes=[
            pltpu.VMEM((pieces * rows, TILE), jnp.float32),
            pltpu.VMEM((columns, columns), jnp.bfloat16),
            pltpu.VMEM((columns, columns), jnp.bfloat16),
            pltpu.VMEM((columns, width), jnp.float32),
            pltpu.VMEM((columns, width), jnp.float32),
            pltpu.VMEM((width, width), jnp.float32),
            pltpu.VMEM((width, width), jnp.float32),
        ],
        compiler_params=pltpu.CompilerParams(vmem_limit_bytes=VMEM_LIMIT),
        name="iterate",
    )(me, summed, start_block)


def body(embeddings, start_block):
    devices = lax.axis_size("dp")
    rows, columns = embeddings.shape
    blocks = columns // TILE
    packed = TILE * blocks * (blocks + 1) // 2
    bits = devices.bit_length() - 1
    scattered = min(bits, ((packed // 8) & -(packed // 8)).bit_length() - 1)
    pieces = 1 << scattered
    me = (lax.axis_index("dp") % pieces).astype(jnp.int32).reshape(1)
    summed = sum_over_devices(moments(embeddings, me, pieces), devices, scattered)
    axes, weights = iterate(summed, start_block, me)
    scores = jnp.dot(
        embeddings,
        weights * math.sqrt(rows * devices),
        precision=lax.Precision.HIGH,
        preferred_element_type=jnp.float32,
    )
    return axes, scores


def solution(mesh):
    in_specs = (P("dp", None), P())
    out_specs = (P(), P("dp", None))
    return jax.shard_map(body, mesh=mesh, in_specs=in_specs, out_specs=out_specs, check_vma=False)
```

time: 872 us -> 135 us (0.15)
  waiting for transfers between devices: 509 us -> 45.8 us
  other arithmetic: 226 us -> 0.68 us
  matrix products: 80.9 us -> 7.29 us
  Pallas kernels: 0 us -> 60.2 us
  local copies, waits for them, and re-layouts: 28.5 us -> 3.04 us
  between operations: 19.5 us -> 0.75 us
  starting transfers between devices: 0.9 us -> 17.3 us
    psum x4 -> x0, waiting for transfers between devices: 509 us -> none  [the longest x2 258 us: body(): summed = lax.psum(inner_dot(embeddings, left_basis), 'dp')]
    another operation x36 -> x3, other arithmetic: 224 us -> 0.32 us  [sum_over_devices(): x = jnp.stack(parts, 1).reshape(-1, rows, columns)]
    dot_general x12 -> x1, matrix products: 69.2 us -> 7.29 us  [body(): jnp.dot(embeddings, weights * math.sqrt(rows * devices), precision=lax.Pr...]
    pallas_call x0 -> x2, Pallas kernels: none -> 60.2 us  [the longest x1 48.4 us: iterate(): pl.pallas_call(iterate_kernel, in_specs=[pl.BlockSpec(memory_space=pltpu....]
    ppermute x0 -> x14, waiting for transfers between devices: none -> 45.8 us  [exchange(): return lax.ppermute(x, 'dp', [(d, d ^ flip) for d in range(devices)])]
    another operation x37 -> x0, local copies, waits for them, and re-layouts: 20.8 us -> none  [the longest x29 19.3 us: factor(): jax.scipy.linalg.solve_triangular(lower_factor, identity, lower=True)]
    ppermute x0 -> x14, starting transfers between devices: none -> 17.3 us  [exchange(): return lax.ppermute(x, 'dp', [(d, d ^ flip) for d in range(devices)])]
    another operation x20 -> x0, matrix products: 11.7 us -> none  [the longest x8 6.54 us: factor(): lower_factor = jnp.linalg.cholesky(gram_matrix)]
  transfers between devices with their start and end apart: 4 -> 14, of which waited for: 4 -> 12; matrix products, arithmetic and copies ran while one was open for 0% -> 0% of each run, Pallas kernels for 0% -> 0%
where the time goes in v1:
time: 135 us
  Pallas kernels  60.2 us (45%)
  waiting for transfers between devices  45.8 us (34%)
  starting transfers between devices  17.3 us (13%)
  matrix products  7.29 us (5%)
  local copies, waits for them, and re-layouts  3.04 us (2%)
    pallas_call x1, Pallas kernels, iterate(): pl.pallas_call(iterate_kernel, in_specs=[pl.BlockSpec(memory_space=pltpu....  48.4 us
    ppermute x14, waiting for transfers between devices, exchange(): return lax.ppermute(x, 'dp', [(d, d ^ flip) for d in range(devices)])  45.8 us
    ppermute x14, starting transfers between devices, exchange(): return lax.ppermute(x, 'dp', [(d, d ^ flip) for d in range(devices)])  17.3 us
    pallas_call x1, Pallas kernels, moments(): pl.pallas_call(moments_kernel, grid=(rows // step,), in_specs=[pl.BlockSp...  11.7 us
    dot_general x1, matrix products, body(): jnp.dot(embeddings, weights * math.sqrt(rows * devices), precision=lax.Pr...  7.29 us
    unnamed x7, local copies, waits for them, and re-layouts  2.87 us
  transfers between devices with their start and end apart: 14, of which 12 were waited for; matrix products, arithmetic and copies ran while one was open for 0% of the time, Pallas kernels for 0%

profile of v1, /device:TPU:0, one launch (start us, length us, event | category | flops | bytes accessed | tf_op | source)
XLA Modules:
  0.0 135.1 jit_solution(5856551728711597747)
XLA Ops:
  0.6 11.7 %moments.1 = f32[32,80,256]{2,1,0:T(8,128)S(1)} custom-call(s32[1]{0:T(128)} %bitcast.me_ref, f32[2048,1024]{1,0:T(8,128)} %e_ref.1), custom_call_target="tpu_custom_call" | custom-call | tf_op jit(solution)/shard_map/moments/pallas_call | solution.py:140
  12.5 0.5 collective-permute-start
  13.0 2.7 %collective-permute-done = f32[16,80,256]{2,1,0:T(8,128)S(1)} collective-permute-done((f32[16,80,256]{2,1,0:T(8,128)S(1)}, f32[16,80,256]{2,1,0:T(8,128)S(1)}, u32[]{:S(2)}, u32[]{:S(2)}) %collective-permute-start) | collective-permute-done | bytes 1310752 | tf_op jit(solution)/shard_map/ppermute | solution.py:156
  15.7 0.2 fusion
  16.0 2.9 %collective-permute-start.1 = (f32[4,80,256]{2,1,0:T(8,128)S(1)}, f32[4,80,256]{2,1,0:T(8,128)S(1)}, u32[]{:S(2)}, u32[]{:S(2)}) collective-permute-start(f32[4,80,256]{2,1,0:T(8,128)S(1)} %get-tuple-element.8), channel_id=1, source_target_pairs={{0,2},{1,3},{2,0},{3,1},{4,6},{5,7},{6,4},{7,5},{8,10},{9,11},{10,... | collective-permute-start | bytes 983048 | tf_op jit(solution)/shard_map/ppermute | solution.py:156
  18.9 1.5 %collective-permute-start.2 = (f32[4,80,256]{2,1,0:T(8,128)S(1)}, f32[4,80,256]{2,1,0:T(8,128)S(1)}, u32[]{:S(2)}, u32[]{:S(2)}) collective-permute-start(f32[4,80,256]{2,1,0:T(8,128)S(1)} %get-tuple-element.9), channel_id=1, source_target_pairs={{0,4},{1,5},{2,6},{3,7},{4,0},{5,1},{6,2},{7,3},{8,12},{9,13},{10,... | collective-permute-start | bytes 983048 | tf_op jit(solution)/shard_map/ppermute | solution.py:156
  20.5 7.0 %collective-permute-done.1 = f32[4,80,256]{2,1,0:T(8,128)S(1)} collective-permute-done((f32[4,80,256]{2,1,0:T(8,128)S(1)}, f32[4,80,256]{2,1,0:T(8,128)S(1)}, u32[]{:S(2)}, u32[]{:S(2)}) %collective-permute-start.1) | collective-permute-done | bytes 327712 | tf_op jit(solution)/shard_map/ppermute | solution.py:156
  27.4 8.0 %collective-permute-done.2 = f32[4,80,256]{2,1,0:T(8,128)S(1)} collective-permute-done((f32[4,80,256]{2,1,0:T(8,128)S(1)}, f32[4,80,256]{2,1,0:T(8,128)S(1)}, u32[]{:S(2)}, u32[]{:S(2)}) %collective-permute-start.2) | collective-permute-done | bytes 327712 | tf_op jit(solution)/shard_map/ppermute | solution.py:156
  35.4 0.1 fusion.6
  35.5 1.6 %collective-permute-start.4 = (f32[1,80,256]{2,1,0:T(8,128)S(1)}, f32[1,80,256]{2,1,0:T(8,128)S(1)}, u32[]{:S(2)}, u32[]{:S(2)}) collective-permute-start(f32[1,80,256]{2,1,0:T(8,128)S(1)} %get-tuple-element.13), channel_id=1, source_target_pairs={{0,8},{1,9},{2,10},{3,11},{4,12},{5,13},{6,14},{7,15},{8,0},{9,1},... | collective-permute-start | bytes 245768 | tf_op jit(solution)/shard_map/ppermute | solution.py:156
  37.2 2.5 %collective-permute-start.6 = (f32[1,80,256]{2,1,0:T(8,128)S(1)}, f32[1,80,256]{2,1,0:T(8,128)S(1)}, u32[]{:S(2)}, u32[]{:S(2)}) collective-permute-start(f32[1,80,256]{2,1,0:T(8,128)S(1)} %get-tuple-element.14), channel_id=1, source_target_pairs={{0,24},{1,25},{2,26},{3,27},{4,28},{5,29},{6,30},{7,31},{8,16},{9,... | collective-permute-start | bytes 245768 | tf_op jit(solution)/shard_map/ppermute | solution.py:156
  39.7 0.1 collective-permute-start.5
  39.8 0.3 collective-permute-done.4
  40.1 3.9 %collective-permute-done.6 = f32[1,80,256]{2,1,0:T(8,128)S(1)} collective-permute-done((f32[1,80,256]{2,1,0:T(8,128)S(1)}, f32[1,80,256]{2,1,0:T(8,128)S(1)}, u32[]{:S(2)}, u32[]{:S(2)}) %collective-permute-start.6) | collective-permute-done | bytes 81952 | tf_op jit(solution)/shard_map/ppermute | solution.py:156
  43.9 2.7 %collective-permute-done.5 = f32[1,80,256]{2,1,0:T(8,128)S(1)} collective-permute-done((f32[1,80,256]{2,1,0:T(8,128)S(1)}, f32[1,80,256]{2,1,0:T(8,128)S(1)}, u32[]{:S(2)}, u32[]{:S(2)}) %collective-permute-start.5) | collective-permute-done | bytes 81952 | tf_op jit(solution)/shard_map/ppermute | solution.py:156
  46.6 2.6 %collective-permute-start.9 = (f32[1,80,256]{2,1,0:T(8,128)S(1)}, f32[1,80,256]{2,1,0:T(8,128)S(1)}, u32[]{:S(2)}, u32[]{:S(2)}) collective-permute-start(f32[1,80,256]{2,1,0:T(8,128)S(1)} %fusion.11), channel_id=1, source_target_pairs={{0,24},{1,25},{2,26},{3,27},{4,28},{5,29},{6,30},{7,31},{8,16},{9,... | collective-permute-start | bytes 245768 | tf_op jit(solution)/shard_map/ppermute | solution.py:156
  49.2 1.9 %collective-permute-start.7 = (f32[1,80,256]{2,1,0:T(8,128)S(1)}, f32[1,80,256]{2,1,0:T(8,128)S(1)}, u32[]{:S(2)}, u32[]{:S(2)}) collective-permute-start(f32[1,80,256]{2,1,0:T(8,128)S(1)} %fusion.11), channel_id=1, source_target_pairs={{0,8},{1,9},{2,10},{3,11},{4,12},{5,13},{6,14},{7,15},{8,0},{9,1},... | collective-permute-start | bytes 245768 | tf_op jit(solution)/shard_map/ppermute | solution.py:156
  51.1 2.9 %collective-permute-done.9 = f32[1,80,256]{2,1,0:T(8,128)S(1)} collective-permute-done((f32[1,80,256]{2,1,0:T(8,128)S(1)}, f32[1,80,256]{2,1,0:T(8,128)S(1)}, u32[]{:S(2)}, u32[]{:S(2)}) %collective-permute-start.9) | collective-permute-done | bytes 81952 | tf_op jit(solution)/shard_map/ppermute | solution.py:156
  54.0 1.9 %collective-permute-done.8 = f32[1,80,256]{2,1,0:T(8,128)S(1)} collective-permute-done((f32[1,80,256]{2,1,0:T(8,128)S(1)}, f32[1,80,256]{2,1,0:T(8,128)S(1)}, u32[]{:S(2)}, u32[]{:S(2)}) %collective-permute-start.8) | collective-permute-done | bytes 81952 | tf_op jit(solution)/shard_map/ppermute | solution.py:156
  55.9 1.6 %collective-permute-start.12 = (f32[4,80,256]{2,1,0:T(8,128)S(1)}, f32[4,80,256]{2,1,0:T(8,128)S(1)}, u32[]{:S(2)}, u32[]{:S(2)}) collective-permute-start(f32[4,80,256]{2,1,0:T(8,128)S(1)} %get-tuple-element.12), channel_id=1, source_target_pairs={{0,6},{1,7},{2,4},{3,5},{4,2},{5,3},{6,0},{7,1},{8,14},{9,15},{10,... | collective-permute-start | bytes 983048 | tf_op jit(solution)/shard_map/ppermute | solution.py:156
  57.5 1.5 %collective-permute-start.11 = (f32[4,80,256]{2,1,0:T(8,128)S(1)}, f32[4,80,256]{2,1,0:T(8,128)S(1)}, u32[]{:S(2)}, u32[]{:S(2)}) collective-permute-start(f32[4,80,256]{2,1,0:T(8,128)S(1)} %get-tuple-element.12), channel_id=1, source_target_pairs={{0,4},{1,5},{2,6},{3,7},{4,0},{5,1},{6,2},{7,3},{8,12},{9,13},{10,... | collective-permute-start | bytes 983048 | tf_op jit(solution)/shard_map/ppermute | solution.py:156
  59.0 0.5 collective-permute-start.10
  59.5 8.1 %collective-permute-done.12 = f32[4,80,256]{2,1,0:T(8,128)S(1)} collective-permute-done((f32[4,80,256]{2,1,0:T(8,128)S(1)}, f32[4,80,256]{2,1,0:T(8,128)S(1)}, u32[]{:S(2)}, u32[]{:S(2)}) %collective-permute-start.12) | collective-permute-done | bytes 327712 | tf_op jit(solution)/shard_map/ppermute | solution.py:156
  67.6 5.4 %collective-permute-done.11 = f32[4,80,256]{2,1,0:T(8,128)S(1)} collective-permute-done((f32[4,80,256]{2,1,0:T(8,128)S(1)}, f32[4,80,256]{2,1,0:T(8,128)S(1)}, u32[]{:S(2)}, u32[]{:S(2)}) %collective-permute-start.11) | collective-permute-done | bytes 327712 | tf_op jit(solution)/shard_map/ppermute | solution.py:156
  73.0 0.1 collective-permute-done.10
  73.1 0.1 pad_maximum_fusion.1
  73.3 3.0 %collective-permute-done.13 = f32[16,80,256]{2,1,0:T(8,128)S(1)} collective-permute-done((f32[16,80,256]{2,1,0:T(8,128)S(1)}, f32[16,80,256]{2,1,0:T(8,128)S(1)}, u32[]{:S(2)}, u32[]{:S(2)}) %collective-permute-start.13) | collective-permute-done | bytes 1310752 | tf_op jit(solution)/shard_map/ppermute | solution.py:156
  76.3 0.2 pad_maximum_fusion
  76.5 1.0 copy-done
  77.5 48.4 %iterate.1 = (f32[1024,256]{1,0:T(8,128)}, f32[1024,256]{1,0:T(8,128)S(1)}) custom-call(s32[1]{0:T(128)} %bitcast.me_ref, f32[32,80,256]{2,1,0:T(8,128)S(1)} %bitcast.75, f32[1024,256]{1,0:T(8,128)S(1)} %copy-done), custom_call_target="tpu_custom_call" | custom-call | tf_op jit(solution)/shard_map/iterate/pallas_call | solution.py:240
  126.0 7.3 %convolution_bitcast_fusion = f32[2048,256]{0,1:T(8,128)S(1)} fusion(f32[2048,1024]{1,0:T(8,128)S(1)} %bitcast.79, f32[1024,256]{1,0:T(8,128)S(1)} %get-tuple-element.5), kind=kOutput, calls=%fused_computation | convolution fusion | flops 3221487616 | bytes 11534336 | tf_op jit(solution)/shard_map/dot_general | solution.py:274
  133.3 1.8 %copy.12 = f32[2048,256]{1,0:T(8,128)} copy(f32[2048,256]{0,1:T(8,128)S(1)} %convolution_bitcast_fusion) | data formatting | bytes 4194304
  (16 shorter events, 0.3 us)
Async XLA Ops:
  12.5 3.2 %collective-permute-start = (f32[16,80,256]{2,1,0:T(8,128)S(1)}, f32[16,80,256]{2,1,0:T(8,128)S(1)}, u32[]{:S(2)}, u32[]{:S(2)}) collective-permute-start(f32[16,80,256]{2,1,0:T(8,128)S(1)} %slice_bitcast_fusion), channel_id=1, source_target_pairs={{0,1},{1,0},{2,3},{3,2},{4,5},{5,4},{6,7},{7,6},{8,9},{9,8},{10,11... | collective-permute-start | bytes 3932168 | tf_op jit(solution)/shard_map/ppermute | solution.py:156
  15.9 110.0 %slice-start = ((s8[8388608]{0:T(1024)(128)(4,1)}), s8[4194304]{0:T(1024)(128)(4,1)S(1)}, s32[]{:S(2)}) async-start(s8[8388608]{0:T(1024)(128)(4,1)} %bitcast.78), calls=%async_computation | async-start | bytes 8388608
  16.0 11.4 %collective-permute-start.1 = (f32[4,80,256]{2,1,0:T(8,128)S(1)}, f32[4,80,256]{2,1,0:T(8,128)S(1)}, u32[]{:S(2)}, u32[]{:S(2)}) collective-permute-start(f32[4,80,256]{2,1,0:T(8,128)S(1)} %get-tuple-element.8), channel_id=1, source_target_pairs={{0,2},{1,3},{2,0},{3,1},{4,6},{5,7},{6,4},{7,5},{8,10},{9,11},{10,... | collective-permute-start | bytes 983048 | tf_op jit(solution)/shard_map/ppermute | solution.py:156
  18.9 16.5 %collective-permute-start.2 = (f32[4,80,256]{2,1,0:T(8,128)S(1)}, f32[4,80,256]{2,1,0:T(8,128)S(1)}, u32[]{:S(2)}, u32[]{:S(2)}) collective-permute-start(f32[4,80,256]{2,1,0:T(8,128)S(1)} %get-tuple-element.9), channel_id=1, source_target_pairs={{0,4},{1,5},{2,6},{3,7},{4,0},{5,1},{6,2},{7,3},{8,12},{9,13},{10,... | collective-permute-start | bytes 983048 | tf_op jit(solution)/shard_map/ppermute | solution.py:156
  20.4 15.0 %collective-permute-start.3 = (f32[4,80,256]{2,1,0:T(8,128)S(1)}, f32[4,80,256]{2,1,0:T(8,128)S(1)}, u32[]{:S(2)}, u32[]{:S(2)}) collective-permute-start(f32[4,80,256]{2,1,0:T(8,128)S(1)} %get-tuple-element.10), channel_id=1, source_target_pairs={{0,6},{1,7},{2,4},{3,5},{4,2},{5,3},{6,0},{7,1},{8,14},{9,15},{10,... | collective-permute-start | bytes 983048 | tf_op jit(solution)/shard_map/ppermute | solution.py:156
  35.5 4.5 %collective-permute-start.4 = (f32[1,80,256]{2,1,0:T(8,128)S(1)}, f32[1,80,256]{2,1,0:T(8,128)S(1)}, u32[]{:S(2)}, u32[]{:S(2)}) collective-permute-start(f32[1,80,256]{2,1,0:T(8,128)S(1)} %get-tuple-element.13), channel_id=1, source_target_pairs={{0,8},{1,9},{2,10},{3,11},{4,12},{5,13},{6,14},{7,15},{8,0},{9,1},... | collective-permute-start | bytes 245768 | tf_op jit(solution)/shard_map/ppermute | solution.py:156
  37.2 6.7 %collective-permute-start.6 = (f32[1,80,256]{2,1,0:T(8,128)S(1)}, f32[1,80,256]{2,1,0:T(8,128)S(1)}, u32[]{:S(2)}, u32[]{:S(2)}) collective-permute-start(f32[1,80,256]{2,1,0:T(8,128)S(1)} %get-tuple-element.14), channel_id=1, source_target_pairs={{0,24},{1,25},{2,26},{3,27},{4,28},{5,29},{6,30},{7,31},{8,16},{9,... | collective-permute-start | bytes 245768 | tf_op jit(solution)/shard_map/ppermute | solution.py:156
  39.7 6.9 %collective-permute-start.5 = (f32[1,80,256]{2,1,0:T(8,128)S(1)}, f32[1,80,256]{2,1,0:T(8,128)S(1)}, u32[]{:S(2)}, u32[]{:S(2)}) collective-permute-start(f32[1,80,256]{2,1,0:T(8,128)S(1)} %get-tuple-element.15), channel_id=1, source_target_pairs={{0,16},{1,17},{2,18},{3,19},{4,20},{5,21},{6,22},{7,23},{8,24},{9,... | collective-permute-start | bytes 245768 | tf_op jit(solution)/shard_map/ppermute | solution.py:156
  46.6 7.3 %collective-permute-start.9 = (f32[1,80,256]{2,1,0:T(8,128)S(1)}, f32[1,80,256]{2,1,0:T(8,128)S(1)}, u32[]{:S(2)}, u32[]{:S(2)}) collective-permute-start(f32[1,80,256]{2,1,0:T(8,128)S(1)} %fusion.11), channel_id=1, source_target_pairs={{0,24},{1,25},{2,26},{3,27},{4,28},{5,29},{6,30},{7,31},{8,16},{9,... | collective-permute-start | bytes 245768 | tf_op jit(solution)/shard_map/ppermute | solution.py:156
  49.2 6.6 %collective-permute-start.8 = (f32[1,80,256]{2,1,0:T(8,128)S(1)}, f32[1,80,256]{2,1,0:T(8,128)S(1)}, u32[]{:S(2)}, u32[]{:S(2)}) collective-permute-start(f32[1,80,256]{2,1,0:T(8,128)S(1)} %fusion.11), channel_id=1, source_target_pairs={{0,16},{1,17},{2,18},{3,19},{4,20},{5,21},{6,22},{7,23},{8,24},{9,... | collective-permute-start | bytes 245768 | tf_op jit(solution)/shard_map/ppermute | solution.py:156
  49.2 6.6 %collective-permute-start.7 = (f32[1,80,256]{2,1,0:T(8,128)S(1)}, f32[1,80,256]{2,1,0:T(8,128)S(1)}, u32[]{:S(2)}, u32[]{:S(2)}) collective-permute-start(f32[1,80,256]{2,1,0:T(8,128)S(1)} %fusion.11), channel_id=1, source_target_pairs={{0,8},{1,9},{2,10},{3,11},{4,12},{5,13},{6,14},{7,15},{8,0},{9,1},... | collective-permute-start | bytes 245768 | tf_op jit(solution)/shard_map/ppermute | solution.py:156
  55.9 11.7 %collective-permute-start.12 = (f32[4,80,256]{2,1,0:T(8,128)S(1)}, f32[4,80,256]{2,1,0:T(8,128)S(1)}, u32[]{:S(2)}, u32[]{:S(2)}) collective-permute-start(f32[4,80,256]{2,1,0:T(8,128)S(1)} %get-tuple-element.12), channel_id=1, source_target_pairs={{0,6},{1,7},{2,4},{3,5},{4,2},{5,3},{6,0},{7,1},{8,14},{9,15},{10,... | collective-permute-start | bytes 983048 | tf_op jit(solution)/shard_map/ppermute | solution.py:156
  57.5 15.5 %collective-permute-start.11 = (f32[4,80,256]{2,1,0:T(8,128)S(1)}, f32[4,80,256]{2,1,0:T(8,128)S(1)}, u32[]{:S(2)}, u32[]{:S(2)}) collective-permute-start(f32[4,80,256]{2,1,0:T(8,128)S(1)} %get-tuple-element.12), channel_id=1, source_target_pairs={{0,4},{1,5},{2,6},{3,7},{4,0},{5,1},{6,2},{7,3},{8,12},{9,13},{10,... | collective-permute-start | bytes 983048 | tf_op jit(solution)/shard_map/ppermute | solution.py:156
  59.0 14.1 %collective-permute-start.10 = (f32[4,80,256]{2,1,0:T(8,128)S(1)}, f32[4,80,256]{2,1,0:T(8,128)S(1)}, u32[]{:S(2)}, u32[]{:S(2)}) collective-permute-start(f32[4,80,256]{2,1,0:T(8,128)S(1)} %get-tuple-element.12), channel_id=1, source_target_pairs={{0,2},{1,3},{2,0},{3,1},{4,6},{5,7},{6,4},{7,5},{8,10},{9,11},{10,... | collective-permute-start | bytes 983048 | tf_op jit(solution)/shard_map/ppermute | solution.py:156
  73.2 3.1 %collective-permute-start.13 = (f32[16,80,256]{2,1,0:T(8,128)S(1)}, f32[16,80,256]{2,1,0:T(8,128)S(1)}, u32[]{:S(2)}, u32[]{:S(2)}) collective-permute-start(f32[16,80,256]{2,1,0:T(8,128)S(1)} %bitcast.80), channel_id=1, source_target_pairs={{0,1},{1,0},{2,3},{3,2},{4,5},{5,4},{6,7},{7,6},{8,9},{9,8},{10,11... | collective-permute-start | bytes 3932168 | tf_op jit(solution)/shard_map/ppermute | solution.py:156
  76.3 1.2 copy-start
  76.3 49.7 %slice-start.1 = ((s8[8388608]{0:T(1024)(128)(4,1)}), s8[4194304]{0:T(1024)(128)(4,1)S(1)}, s32[]{:S(2)}) async-start(s8[8388608]{0:T(1024)(128)(4,1)} %bitcast.78), calls=%async_computation.1 | async-start | bytes 8388608

commit v2 on v1

v2 whole, which is shorter than its diff:
```python
import functools
import math

import jax
import jax.numpy as jnp
from jax import lax
from jax.experimental import pallas as pl
from jax.experimental.pallas import tpu as pltpu
from jax.sharding import PartitionSpec as P

ITERS = 2
BLOCK = 32
SUB = 8
LANES = 128
TILE = 256
HALF = TILE // 2
VMEM_LIMIT = 48 * 1024 * 1024


def dot(left, right, contract=(1, 0)):
    dims = (((contract[0],), (contract[1],)), ((), ()))
    return lax.dot_general(left, right, dims, preferred_element_type=jnp.float32)


def split2(x):
    high = x.astype(jnp.bfloat16)
    return high, (x - high.astype(jnp.float32)).astype(jnp.bfloat16)


def split3(x):
    high = x.astype(jnp.bfloat16)
    rest = x - high.astype(jnp.float32)
    middle = rest.astype(jnp.bfloat16)
    return high, middle, (rest - middle.astype(jnp.float32)).astype(jnp.bfloat16)


def dot3(left, right, contract=(1, 0)):
    left_high, left_low = left
    right_high, right_low = right
    return (
        dot(left_high, right_high, contract)
        + dot(left_high, right_low, contract)
        + dot(left_low, right_high, contract)
    )


def stack_left(x):
    high, middle, low = split3(x)
    return jnp.concatenate([high, high, middle, middle, high, low], 0)


def stack_right(x):
    high, middle, low = split3(x)
    return jnp.concatenate([high, middle, high, middle, low, high], 0)


def self_product(parts):
    high, low = parts
    half = dot(high, high * jnp.bfloat16(0.5), (0, 0)) + dot(high, low, (0, 0))
    return half + half.T


def eliminate(rows, offset):
    lane = lax.broadcasted_iota(jnp.int32, (SUB, LANES), 1)
    row = lax.broadcasted_iota(jnp.int32, (SUB, LANES), 0)
    tiles = BLOCK // SUB
    rows = [list(groups) for groups in rows]
    columns = {}

    def spread_columns(tile):
        for k in range(SUB):
            at = offset + tile * SUB + k
            columns[tile * SUB + k] = {
                i: jnp.broadcast_to(rows[i][0][:, at : at + 1], (SUB, LANES))
                for i in range(tile, tiles)
            }

    spread_columns(0)
    for tile in range(tiles):
        if tile + 1 < tiles:
            spread_columns(tile + 1)
        for k in range(SUB):
            j = tile * SUB + k
            column = columns.pop(j)
            pivot = column[tile][k : k + 1]
            inverse = 1.0 / pivot
            mult = {i: column[i] * inverse for i in range(tile, tiles)}
            for q in range(j + 1, min((tile + 2) * SUB, BLOCK)):
                entry = column[q // SUB][q % SUB : q % SUB + 1]
                for i in range(q // SUB, tiles):
                    columns[q][i] = columns[q][i] - mult[i] * entry
            scale = lax.rsqrt(pivot)
            here = lane == offset + j
            top = [jnp.where(here[:1], 1.0, rows[tile][0][k : k + 1])]
            top += [group[k : k + 1] for group in rows[tile][1:]]
            for i in range(tile, tiles):
                old = rows[i]
                new = [jnp.where(here, 0.0, old[0])] + old[1:]
                new = [x - mult[i] * y for x, y in zip(new, top)]
                if i == tile:
                    kept = [jnp.where(row == k, y * scale, x) for x, y in zip(old, top)]
                    new = [jnp.where(row > k, x, y) for x, y in zip(new, kept)]
                rows[i] = new
    return rows


def invert_factor(a_ref, beside=None):
    n = a_ref.shape[0]
    lane = lax.broadcasted_iota(jnp.int32, (BLOCK, n), 1)
    row = lax.broadcasted_iota(jnp.int32, (BLOCK, n), 0)
    panel = a_ref[0:BLOCK, :]
    for start in range(0, n, BLOCK):
        end = start + BLOCK
        if beside is not None:
            beside(start // BLOCK)
        active = start // LANES
        order = [active] + [g for g in range(n // LANES) if g != active]
        rows = [
            [panel[t : t + SUB, g * LANES : (g + 1) * LANES] for g in order]
            for t in range(0, BLOCK, SUB)
        ]
        rows = eliminate(rows, start % LANES)
        groups = [jnp.concatenate([tile[order.index(g)] for tile in rows], 0) for g in range(n // LANES)]
        upper = jnp.concatenate(groups, 1)
        done = jnp.where((lane < end) & (lane - start > row), 0.0, upper)
        a_ref[start:end, :] = jnp.where(lane < end, done, 0.0)
        if end == n:
            break
        left, right = stack_left(upper), stack_right(done)

        def updated(first, last):
            col = lax.broadcasted_iota(jnp.int32, (last - first, n), 1)
            old = jnp.where((col >= start) & (col < end), 0.0, a_ref[first:last, :])
            return old - dot(left[:, first:last], right, (0, 0))

        panel = updated(end, end + BLOCK)
        if end + BLOCK < n:
            a_ref[end + BLOCK : n, :] = updated(end + BLOCK, n)


def below_diagonal(blocks):
    return [(i, j) for j in range(blocks) for i in range(j + 1, blocks)]


def packed_rows(blocks):
    return TILE * len(below_diagonal(blocks)) + HALF * blocks + HALF * blocks // 2


def moments_kernel(me_ref, e_ref, out_ref, packed, diagonal):
    blocks = e_ref.shape[1] // TILE
    step = pl.program_id(0)

    @pl.when(step == 0)
    def _():
        packed[...] = jnp.zeros_like(packed)
        diagonal[...] = jnp.zeros_like(diagonal)

    parts = [split2(e_ref[:, i * TILE : (i + 1) * TILE]) for i in range(blocks)]
    flipped = [(high.T, low.T) for high, low in parts]
    for j in range(blocks):
        high, low = parts[j]
        diagonal[j] += dot(flipped[j][0], high * jnp.bfloat16(0.5)) + dot(flipped[j][0], low)
    for place, (i, j) in enumerate(below_diagonal(blocks)):
        packed[place * TILE : (place + 1) * TILE, :] += dot3(flipped[i], parts[j])

    @pl.when(step == pl.num_programs(0) - 1)
    def _():
        lower = TILE * len(below_diagonal(blocks))
        corner = lower + HALF * blocks
        for j in range(blocks):
            block = diagonal[j] + diagonal[j].T
            packed[lower + j * HALF : lower + (j + 1) * HALF, :] = block[HALF:]
            at = corner + j // 2 * HALF
            side = j % 2 * HALF
            packed[at : at + HALF, side : side + HALF] = block[:HALF, :HALF]
        pieces, rows, _ = out_ref.shape
        for piece in range(pieces):
            out_ref[piece ^ me_ref[0]] = packed[piece * rows : (piece + 1) * rows, :]


def moments(embeddings, me, pieces):
    rows, columns = embeddings.shape
    blocks = columns // TILE
    packed = packed_rows(blocks)
    step = min(512, rows)
    shape = (pieces, packed // pieces, TILE)
    return pl.pallas_call(
        moments_kernel,
        grid=(rows // step,),
        in_specs=[
            pl.BlockSpec(memory_space=pltpu.SMEM),
            pl.BlockSpec((step, columns), lambda i: (i, 0)),
        ],
        out_specs=pl.BlockSpec(shape, lambda i: (0, 0, 0)),
        out_shape=jax.ShapeDtypeStruct(shape, jnp.float32),
        scratch_shapes=[
            pltpu.VMEM((packed, TILE), jnp.float32),
            pltpu.VMEM((blocks, TILE, TILE), jnp.float32),
        ],
        compiler_params=pltpu.CompilerParams(vmem_limit_bytes=VMEM_LIMIT),
        name="moments",
    )(me, embeddings)


def exchange(x, flip, devices):
    return lax.ppermute(x, "dp", [(d, d ^ flip) for d in range(devices)])


def phases(bits):
    groups = [[0]] if bits else []
    return groups + [list(range(b, min(b + 2, bits))) for b in range(1, bits, 2)]


def spread(value, group):
    return sum(((value >> place) & 1) << bit for place, bit in enumerate(group))


def sum_over_devices(x, devices, scattered):
    bits = devices.bit_length() - 1
    pieces, rows, columns = x.shape
    for group in phases(scattered):
        size = 1 << len(group)
        x = x.reshape(-1, size, rows, columns)
        mine = x[:, 0]
        others = [exchange(x[:, d], spread(d, group), devices) for d in range(1, size)]
        for other in others:
            mine = mine + other
        x = mine
    x = x.reshape(rows, columns)
    for bit in range(scattered, bits):
        x = x + exchange(x, 1 << bit, devices)
    x = x[None]
    for group in reversed(phases(scattered)):
        size = 1 << len(group)
        parts = [x] + [exchange(x, spread(d, group), devices) for d in range(1, size)]
        x = jnp.stack(parts, 1).reshape(-1, rows, columns)
    return x


def iterate_kernel(
    scale, me_ref, c_ref, start_ref, e_ref, axes_ref, scores_ref,
    packed, c_high, c_low, work, gram, cross, rows_in, rows_out, sems,
):
    load = pltpu.make_async_copy(e_ref, rows_in, sems.at[0])
    load.start()
    pieces, rows, _ = c_ref.shape
    columns, width = start_ref.shape
    blocks = columns // TILE
    for piece in range(pieces):
        packed[piece * rows : (piece + 1) * rows, :] = c_ref[piece ^ me_ref[0]]

    def put(i, j, block):
        at_i, at_j = pl.ds(i * TILE, TILE), pl.ds(j * TILE, TILE)
        c_high[at_i, at_j], c_low[at_i, at_j] = split2(block)

    for place, (i, j) in enumerate(below_diagonal(blocks)):
        block = packed[place * TILE : (place + 1) * TILE, :]
        put(i, j, block)
        put(j, i, block.T)
    lower = TILE * len(below_diagonal(blocks))
    corner = lower + HALF * blocks
    for j in range(blocks):
        bottom = packed[lower + j * HALF : lower + (j + 1) * HALF, :]
        at = corner + j // 2 * HALF
        side = j % 2 * HALF
        top = [packed[at : at + HALF, side : side + HALF], bottom[:, :HALF].T]
        put(j, j, jnp.concatenate([jnp.concatenate(top, 1), bottom], 0))

    step_rows = rows_in.shape[0] * BLOCK // width
    basis = start_ref[...]
    for index in range(ITERS):
        current = split2(basis)
        work[...] = dot3((c_high[...], c_low[...]), current)
        product = split2(work[...])
        gram[...] = dot3(current, product, (0, 0))
        invert_factor(gram)
        inverse = split2(gram[...])
        summed = split2(dot3(product, inverse, (1, 1)))
        cross[...] = self_product(summed)
        if index < ITERS - 1:
            invert_factor(cross)
        else:
            weights = split2(dot3(current, inverse, (1, 1)) * scale)
            load.wait()

            def beside(step):
                at = slice(step * step_rows, (step + 1) * step_rows)
                rows_out[at, :] = dot3(split2(rows_in[at, :]), weights)

            invert_factor(cross, beside)
        basis = dot3(summed, split2(cross[...]), (1, 1))
    store = pltpu.make_async_copy(rows_out, scores_ref, sems.at[1])
    store.start()
    axes_ref[...] = basis * math.sqrt(columns)
    store.wait()


def iterate(summed, start_block, embeddings, me, scale):
    columns, width = start_block.shape
    pieces, rows, _ = summed.shape
    count = embeddings.shape[0]
    vmem = pl.BlockSpec(memory_space=pltpu.VMEM)
    anywhere = pl.BlockSpec(memory_space=pl.ANY)
    return pl.pallas_call(
        functools.partial(iterate_kernel, scale),
        in_specs=[pl.BlockSpec(memory_space=pltpu.SMEM), vmem, vmem, anywhere],
        out_specs=[vmem, anywhere],
        out_shape=[
            jax.ShapeDtypeStruct((columns, width), jnp.float32),
            jax.ShapeDtypeStruct((count, width), jnp.float32),
        ],
        scratch_shapes=[
            pltpu.VMEM((pieces * rows, TILE), jnp.float32),
            pltpu.VMEM((columns, columns), jnp.bfloat16),
            pltpu.VMEM((columns, columns), jnp.bfloat16),
            pltpu.VMEM((columns, width), jnp.float32),
            pltpu.VMEM((width, width), jnp.float32),
            pltpu.VMEM((width, width), jnp.float32),
            pltpu.VMEM((count, columns), jnp.float32),
            pltpu.VMEM((count, width), jnp.float32),
            pltpu.SemaphoreType.DMA((2,)),
        ],
        compiler_params=pltpu.CompilerParams(vmem_limit_bytes=VMEM_LIMIT),
        name="iterate",
    )(me, summed, start_block, embeddings)


def body(embeddings, start_block):
    devices = lax.axis_size("dp")
    rows, columns = embeddings.shape
    packed = packed_rows(columns // TILE)
    bits = devices.bit_length() - 1
    scattered = min(bits, ((packed // 8) & -(packed // 8)).bit_length() - 1)
    pieces = 1 << scattered
    me = (lax.axis_index("dp") % pieces).astype(jnp.int32).reshape(1)
    summed = sum_over_devices(moments(embeddings, me, pieces), devices, scattered)
    axes, scores = iterate(summed, start_block, embeddings, me, math.sqrt(rows * devices))
    return axes, scores


def solution(mesh):
    in_specs = (P("dp", None), P())
    out_specs = (P(), P("dp", None))
    return jax.shard_map(body, mesh=mesh, in_specs=in_specs, out_specs=out_specs, check_vma=False)
```

time: 135 us -> 113 us (0.84)
  Pallas kernels: 60.2 us -> 50.8 us
  matrix products: 7.29 us -> 0 us
  waiting for transfers between devices: 45.8 us -> 41.7 us
  local copies, waits for them, and re-layouts: 3.04 us -> 1.19 us
    pallas_call x1, Pallas kernels: 48.4 us -> 40.7 us  [iterate(): pl.pallas_call(functools.partial(iterate_kernel, scale), in_specs=[pl.Blo...]
    dot_general x1 -> x0, matrix products: 7.29 us -> none  [body(): jnp.dot(embeddings, weights * math.sqrt(rows * devices), precision=lax.Pr...]
    ppermute x14, waiting for transfers between devices: 45.8 us -> 41.7 us  [exchange(): return lax.ppermute(x, 'dp', [(d, d ^ flip) for d in range(devices)])]
    unnamed x7 -> x2, local copies, waits for them, and re-layouts: 2.87 us -> 1.03 us
    pallas_call x1, Pallas kernels: 11.7 us -> 10.2 us  [moments(): pl.pallas_call(moments_kernel, grid=(rows // step,), in_specs=[pl.BlockSp...]
where the time goes in v2:
time: 113 us
  Pallas kernels  50.8 us (45%)
  waiting for transfers between devices  41.7 us (37%)
  starting transfers between devices  17.3 us (15%)
  local copies, waits for them, and re-layouts  1.19 us (1%)
    ppermute x14, waiting for transfers between devices, exchange(): return lax.ppermute(x, 'dp', [(d, d ^ flip) for d in range(devices)])  41.7 us
    pallas_call x1, Pallas kernels, iterate(): pl.pallas_call(functools.partial(iterate_kernel, scale), in_specs=[pl.Blo...  40.7 us
    ppermute x14, starting transfers between devices, exchange(): return lax.ppermute(x, 'dp', [(d, d ^ flip) for d in range(devices)])  17.3 us
    pallas_call x1, Pallas kernels, moments(): pl.pallas_call(moments_kernel, grid=(rows // step,), in_specs=[pl.BlockSp...  10.2 us
  transfers between devices with their start and end apart: 14, of which 12 were waited for; matrix products, arithmetic and copies ran while one was open for 0% of the time, Pallas kernels for 0%

profile of v2, /device:TPU:0, one launch (start us, length us, event | category | flops | bytes accessed | tf_op | source)
XLA Modules:
  0.0 112.6 jit_solution(17881531334020608770)
XLA Ops:
  0.6 10.2 %moments.1 = f32[32,72,256]{2,1,0:T(8,128)S(1)} custom-call(s32[1]{0:T(128)} %bitcast.me_ref, f32[2048,1024]{1,0:T(8,128)} %e_ref.3), custom_call_target="tpu_custom_call" | custom-call | tf_op jit(solution)/shard_map/moments/pallas_call | solution.py:187
  10.8 0.1 slice_bitcast_fusion
  10.9 0.5 collective-permute-start
  11.4 2.5 %collective-permute-done = f32[16,72,256]{2,1,0:T(8,128)S(1)} collective-permute-done((f32[16,72,256]{2,1,0:T(8,128)S(1)}, f32[16,72,256]{2,1,0:T(8,128)S(1)}, u32[]{:S(2)}, u32[]{:S(2)}) %collective-permute-start) | collective-permute-done | bytes 1179680 | tf_op jit(solution)/shard_map/ppermute | solution.py:206
  13.9 0.2 fusion
  14.2 2.9 %collective-permute-start.1 = (f32[4,72,256]{2,1,0:T(8,128)S(1)}, f32[4,72,256]{2,1,0:T(8,128)S(1)}, u32[]{:S(2)}, u32[]{:S(2)}) collective-permute-start(f32[4,72,256]{2,1,0:T(8,128)S(1)} %get-tuple-element.2), channel_id=1, source_target_pairs={{0,2},{1,3},{2,0},{3,1},{4,6},{5,7},{6,4},{7,5},{8,10},{9,11},{10,... | collective-permute-start | bytes 884744 | tf_op jit(solution)/shard_map/ppermute | solution.py:206
  17.1 1.5 %collective-permute-start.2 = (f32[4,72,256]{2,1,0:T(8,128)S(1)}, f32[4,72,256]{2,1,0:T(8,128)S(1)}, u32[]{:S(2)}, u32[]{:S(2)}) collective-permute-start(f32[4,72,256]{2,1,0:T(8,128)S(1)} %get-tuple-element.3), channel_id=1, source_target_pairs={{0,4},{1,5},{2,6},{3,7},{4,0},{5,1},{6,2},{7,3},{8,12},{9,13},{10,... | collective-permute-start | bytes 884744 | tf_op jit(solution)/shard_map/ppermute | solution.py:206
  18.7 6.3 %collective-permute-done.1 = f32[4,72,256]{2,1,0:T(8,128)S(1)} collective-permute-done((f32[4,72,256]{2,1,0:T(8,128)S(1)}, f32[4,72,256]{2,1,0:T(8,128)S(1)}, u32[]{:S(2)}, u32[]{:S(2)}) %collective-permute-start.1) | collective-permute-done | bytes 294944 | tf_op jit(solution)/shard_map/ppermute | solution.py:206
  24.9 7.3 %collective-permute-done.2 = f32[4,72,256]{2,1,0:T(8,128)S(1)} collective-permute-done((f32[4,72,256]{2,1,0:T(8,128)S(1)}, f32[4,72,256]{2,1,0:T(8,128)S(1)}, u32[]{:S(2)}, u32[]{:S(2)}) %collective-permute-start.2) | collective-permute-done | bytes 294944 | tf_op jit(solution)/shard_map/ppermute | solution.py:206
  32.2 0.1 fusion.4
  32.3 1.6 %collective-permute-start.4 = (f32[1,72,256]{2,1,0:T(8,128)S(1)}, f32[1,72,256]{2,1,0:T(8,128)S(1)}, u32[]{:S(2)}, u32[]{:S(2)}) collective-permute-start(f32[1,72,256]{2,1,0:T(8,128)S(1)} %get-tuple-element.7), channel_id=1, source_target_pairs={{0,8},{1,9},{2,10},{3,11},{4,12},{5,13},{6,14},{7,15},{8,0},{9,1},... | collective-permute-start | bytes 221192 | tf_op jit(solution)/shard_map/ppermute | solution.py:206
  34.0 2.5 %collective-permute-start.6 = (f32[1,72,256]{2,1,0:T(8,128)S(1)}, f32[1,72,256]{2,1,0:T(8,128)S(1)}, u32[]{:S(2)}, u32[]{:S(2)}) collective-permute-start(f32[1,72,256]{2,1,0:T(8,128)S(1)} %get-tuple-element.8), channel_id=1, source_target_pairs={{0,24},{1,25},{2,26},{3,27},{4,28},{5,29},{6,30},{7,31},{8,16},{9,... | collective-permute-start | bytes 221192 | tf_op jit(solution)/shard_map/ppermute | solution.py:206
  36.5 0.1 collective-permute-start.5
  36.6 0.2 collective-permute-done.4
  36.8 3.6 %collective-permute-done.6 = f32[1,72,256]{2,1,0:T(8,128)S(1)} collective-permute-done((f32[1,72,256]{2,1,0:T(8,128)S(1)}, f32[1,72,256]{2,1,0:T(8,128)S(1)}, u32[]{:S(2)}, u32[]{:S(2)}) %collective-permute-start.6) | collective-permute-done | bytes 73760 | tf_op jit(solution)/shard_map/ppermute | solution.py:206
  40.4 2.5 %collective-permute-done.5 = f32[1,72,256]{2,1,0:T(8,128)S(1)} collective-permute-done((f32[1,72,256]{2,1,0:T(8,128)S(1)}, f32[1,72,256]{2,1,0:T(8,128)S(1)}, u32[]{:S(2)}, u32[]{:S(2)}) %collective-permute-start.5) | collective-permute-done | bytes 73760 | tf_op jit(solution)/shard_map/ppermute | solution.py:206
  42.9 2.5 %collective-permute-start.9 = (f32[1,72,256]{2,1,0:T(8,128)S(1)}, f32[1,72,256]{2,1,0:T(8,128)S(1)}, u32[]{:S(2)}, u32[]{:S(2)}) collective-permute-start(f32[1,72,256]{2,1,0:T(8,128)S(1)} %fusion.9), channel_id=1, source_target_pairs={{0,24},{1,25},{2,26},{3,27},{4,28},{5,29},{6,30},{7,31},{8,16},{9,... | collective-permute-start | bytes 221192 | tf_op jit(solution)/shard_map/ppermute | solution.py:206
  45.4 1.9 %collective-permute-start.7 = (f32[1,72,256]{2,1,0:T(8,128)S(1)}, f32[1,72,256]{2,1,0:T(8,128)S(1)}, u32[]{:S(2)}, u32[]{:S(2)}) collective-permute-start(f32[1,72,256]{2,1,0:T(8,128)S(1)} %fusion.9), channel_id=1, source_target_pairs={{0,8},{1,9},{2,10},{3,11},{4,12},{5,13},{6,14},{7,15},{8,0},{9,1},... | collective-permute-start | bytes 221192 | tf_op jit(solution)/shard_map/ppermute | solution.py:206
  47.3 2.7 %collective-permute-done.9 = f32[1,72,256]{2,1,0:T(8,128)S(1)} collective-permute-done((f32[1,72,256]{2,1,0:T(8,128)S(1)}, f32[1,72,256]{2,1,0:T(8,128)S(1)}, u32[]{:S(2)}, u32[]{:S(2)}) %collective-permute-start.9) | collective-permute-done | bytes 73760 | tf_op jit(solution)/shard_map/ppermute | solution.py:206
  50.0 1.7 %collective-permute-done.8 = f32[1,72,256]{2,1,0:T(8,128)S(1)} collective-permute-done((f32[1,72,256]{2,1,0:T(8,128)S(1)}, f32[1,72,256]{2,1,0:T(8,128)S(1)}, u32[]{:S(2)}, u32[]{:S(2)}) %collective-permute-start.8) | collective-permute-done | bytes 73760 | tf_op jit(solution)/shard_map/ppermute | solution.py:206
  51.7 1.6 %collective-permute-start.12 = (f32[4,72,256]{2,1,0:T(8,128)S(1)}, f32[4,72,256]{2,1,0:T(8,128)S(1)}, u32[]{:S(2)}, u32[]{:S(2)}) collective-permute-start(f32[4,72,256]{2,1,0:T(8,128)S(1)} %get-tuple-element.6), channel_id=1, source_target_pairs={{0,6},{1,7},{2,4},{3,5},{4,2},{5,3},{6,0},{7,1},{8,14},{9,15},{10,... | collective-permute-start | bytes 884744 | tf_op jit(solution)/shard_map/ppermute | solution.py:206
  53.3 1.4 %collective-permute-start.11 = (f32[4,72,256]{2,1,0:T(8,128)S(1)}, f32[4,72,256]{2,1,0:T(8,128)S(1)}, u32[]{:S(2)}, u32[]{:S(2)}) collective-permute-start(f32[4,72,256]{2,1,0:T(8,128)S(1)} %get-tuple-element.6), channel_id=1, source_target_pairs={{0,4},{1,5},{2,6},{3,7},{4,0},{5,1},{6,2},{7,3},{8,12},{9,13},{10,... | collective-permute-start | bytes 884744 | tf_op jit(solution)/shard_map/ppermute | solution.py:206
  54.7 0.5 collective-permute-start.10
  55.3 7.4 %collective-permute-done.12 = f32[4,72,256]{2,1,0:T(8,128)S(1)} collective-permute-done((f32[4,72,256]{2,1,0:T(8,128)S(1)}, f32[4,72,256]{2,1,0:T(8,128)S(1)}, u32[]{:S(2)}, u32[]{:S(2)}) %collective-permute-start.12) | collective-permute-done | bytes 294944 | tf_op jit(solution)/shard_map/ppermute | solution.py:206
  62.7 4.7 %collective-permute-done.11 = f32[4,72,256]{2,1,0:T(8,128)S(1)} collective-permute-done((f32[4,72,256]{2,1,0:T(8,128)S(1)}, f32[4,72,256]{2,1,0:T(8,128)S(1)}, u32[]{:S(2)}, u32[]{:S(2)}) %collective-permute-start.11) | collective-permute-done | bytes 294944 | tf_op jit(solution)/shard_map/ppermute | solution.py:206
  67.4 0.1 collective-permute-done.10
  67.5 0.1 pad_maximum_fusion.1
  67.6 0.1 collective-permute-start.13
  67.7 2.8 %collective-permute-done.13 = f32[16,72,256]{2,1,0:T(8,128)S(1)} collective-permute-done((f32[16,72,256]{2,1,0:T(8,128)S(1)}, f32[16,72,256]{2,1,0:T(8,128)S(1)}, u32[]{:S(2)}, u32[]{:S(2)}) %collective-permute-start.13) | collective-permute-done | bytes 1179680 | tf_op jit(solution)/shard_map/ppermute | solution.py:206
  70.5 0.2 pad_maximum_fusion
  70.7 1.0 copy-done
  71.7 40.7 %iterate.1 = (f32[1024,256]{1,0:T(8,128)}, f32[2048,256]{1,0:T(8,128)}) custom-call(s32[1]{0:T(128)} %bitcast.me_ref, f32[32,72,256]{2,1,0:T(8,128)S(1)} %bitcast.74, f32[1024,256]{1,0:T(8,128)S(1)} %copy-done, f32[2048,1024]{1,0:T(8,128)} %e_ref.3), custom_call_target="tpu_custom_call" | custom-call | tf_op jit(solution)/shard_map/iterate/pallas_call | solution.py:304
  (9 shorter events, 0.2 us)
Async XLA Ops:
  10.9 3.0 %collective-permute-start = (f32[16,72,256]{2,1,0:T(8,128)S(1)}, f32[16,72,256]{2,1,0:T(8,128)S(1)}, u32[]{:S(2)}, u32[]{:S(2)}) collective-permute-start(f32[16,72,256]{2,1,0:T(8,128)S(1)} %slice_bitcast_fusion), channel_id=1, source_target_pairs={{0,1},{1,0},{2,3},{3,2},{4,5},{5,4},{6,7},{7,6},{8,9},{9,8},{10,11... | collective-permute-start | bytes 3538952 | tf_op jit(solution)/shard_map/ppermute | solution.py:206
  14.2 10.7 %collective-permute-start.1 = (f32[4,72,256]{2,1,0:T(8,128)S(1)}, f32[4,72,256]{2,1,0:T(8,128)S(1)}, u32[]{:S(2)}, u32[]{:S(2)}) collective-permute-start(f32[4,72,256]{2,1,0:T(8,128)S(1)} %get-tuple-element.2), channel_id=1, source_target_pairs={{0,2},{1,3},{2,0},{3,1},{4,6},{5,7},{6,4},{7,5},{8,10},{9,11},{10,... | collective-permute-start | bytes 884744 | tf_op jit(solution)/shard_map/ppermute | solution.py:206
  17.1 15.1 %collective-permute-start.2 = (f32[4,72,256]{2,1,0:T(8,128)S(1)}, f32[4,72,256]{2,1,0:T(8,128)S(1)}, u32[]{:S(2)}, u32[]{:S(2)}) collective-permute-start(f32[4,72,256]{2,1,0:T(8,128)S(1)} %get-tuple-element.3), channel_id=1, source_target_pairs={{0,4},{1,5},{2,6},{3,7},{4,0},{5,1},{6,2},{7,3},{8,12},{9,13},{10,... | collective-permute-start | bytes 884744 | tf_op jit(solution)/shard_map/ppermute | solution.py:206
  18.6 13.6 %collective-permute-start.3 = (f32[4,72,256]{2,1,0:T(8,128)S(1)}, f32[4,72,256]{2,1,0:T(8,128)S(1)}, u32[]{:S(2)}, u32[]{:S(2)}) collective-permute-start(f32[4,72,256]{2,1,0:T(8,128)S(1)} %get-tuple-element.4), channel_id=1, source_target_pairs={{0,6},{1,7},{2,4},{3,5},{4,2},{5,3},{6,0},{7,1},{8,14},{9,15},{10,... | collective-permute-start | bytes 884744 | tf_op jit(solution)/shard_map/ppermute | solution.py:206
  32.3 4.4 %collective-permute-start.4 = (f32[1,72,256]{2,1,0:T(8,128)S(1)}, f32[1,72,256]{2,1,0:T(8,128)S(1)}, u32[]{:S(2)}, u32[]{:S(2)}) collective-permute-start(f32[1,72,256]{2,1,0:T(8,128)S(1)} %get-tuple-element.7), channel_id=1, source_target_pairs={{0,8},{1,9},{2,10},{3,11},{4,12},{5,13},{6,14},{7,15},{8,0},{9,1},... | collective-permute-start | bytes 221192 | tf_op jit(solution)/shard_map/ppermute | solution.py:206
  34.0 6.4 %collective-permute-start.6 = (f32[1,72,256]{2,1,0:T(8,128)S(1)}, f32[1,72,256]{2,1,0:T(8,128)S(1)}, u32[]{:S(2)}, u32[]{:S(2)}) collective-permute-start(f32[1,72,256]{2,1,0:T(8,128)S(1)} %get-tuple-element.8), channel_id=1, source_target_pairs={{0,24},{1,25},{2,26},{3,27},{4,28},{5,29},{6,30},{7,31},{8,16},{9,... | collective-permute-start | bytes 221192 | tf_op jit(solution)/shard_map/ppermute | solution.py:206
  36.5 6.4 %collective-permute-start.5 = (f32[1,72,256]{2,1,0:T(8,128)S(1)}, f32[1,72,256]{2,1,0:T(8,128)S(1)}, u32[]{:S(2)}, u32[]{:S(2)}) collective-permute-start(f32[1,72,256]{2,1,0:T(8,128)S(1)} %get-tuple-element.9), channel_id=1, source_target_pairs={{0,16},{1,17},{2,18},{3,19},{4,20},{5,21},{6,22},{7,23},{8,24},{9,... | collective-permute-start | bytes 221192 | tf_op jit(solution)/shard_map/ppermute | solution.py:206
  42.9 7.1 %collective-permute-start.9 = (f32[1,72,256]{2,1,0:T(8,128)S(1)}, f32[1,72,256]{2,1,0:T(8,128)S(1)}, u32[]{:S(2)}, u32[]{:S(2)}) collective-permute-start(f32[1,72,256]{2,1,0:T(8,128)S(1)} %fusion.9), channel_id=1, source_target_pairs={{0,24},{1,25},{2,26},{3,27},{4,28},{5,29},{6,30},{7,31},{8,16},{9,... | collective-permute-start | bytes 221192 | tf_op jit(solution)/shard_map/ppermute | solution.py:206
  45.4 6.3 %collective-permute-start.8 = (f32[1,72,256]{2,1,0:T(8,128)S(1)}, f32[1,72,256]{2,1,0:T(8,128)S(1)}, u32[]{:S(2)}, u32[]{:S(2)}) collective-permute-start(f32[1,72,256]{2,1,0:T(8,128)S(1)} %fusion.9), channel_id=1, source_target_pairs={{0,16},{1,17},{2,18},{3,19},{4,20},{5,21},{6,22},{7,23},{8,24},{9,... | collective-permute-start | bytes 221192 | tf_op jit(solution)/shard_map/ppermute | solution.py:206
  45.4 6.3 %collective-permute-start.7 = (f32[1,72,256]{2,1,0:T(8,128)S(1)}, f32[1,72,256]{2,1,0:T(8,128)S(1)}, u32[]{:S(2)}, u32[]{:S(2)}) collective-permute-start(f32[1,72,256]{2,1,0:T(8,128)S(1)} %fusion.9), channel_id=1, source_target_pairs={{0,8},{1,9},{2,10},{3,11},{4,12},{5,13},{6,14},{7,15},{8,0},{9,1},... | collective-permute-start | bytes 221192 | tf_op jit(solution)/shard_map/ppermute | solution.py:206
  51.7 11.0 %collective-permute-start.12 = (f32[4,72,256]{2,1,0:T(8,128)S(1)}, f32[4,72,256]{2,1,0:T(8,128)S(1)}, u32[]{:S(2)}, u32[]{:S(2)}) collective-permute-start(f32[4,72,256]{2,1,0:T(8,128)S(1)} %get-tuple-element.6), channel_id=1, source_target_pairs={{0,6},{1,7},{2,4},{3,5},{4,2},{5,3},{6,0},{7,1},{8,14},{9,15},{10,... | collective-permute-start | bytes 884744 | tf_op jit(solution)/shard_map/ppermute | solution.py:206
  53.3 14.1 %collective-permute-start.11 = (f32[4,72,256]{2,1,0:T(8,128)S(1)}, f32[4,72,256]{2,1,0:T(8,128)S(1)}, u32[]{:S(2)}, u32[]{:S(2)}) collective-permute-start(f32[4,72,256]{2,1,0:T(8,128)S(1)} %get-tuple-element.6), channel_id=1, source_target_pairs={{0,4},{1,5},{2,6},{3,7},{4,0},{5,1},{6,2},{7,3},{8,12},{9,13},{10,... | collective-permute-start | bytes 884744 | tf_op jit(solution)/shard_map/ppermute | solution.py:206
  54.7 12.8 %collective-permute-start.10 = (f32[4,72,256]{2,1,0:T(8,128)S(1)}, f32[4,72,256]{2,1,0:T(8,128)S(1)}, u32[]{:S(2)}, u32[]{:S(2)}) collective-permute-start(f32[4,72,256]{2,1,0:T(8,128)S(1)} %get-tuple-element.6), channel_id=1, source_target_pairs={{0,2},{1,3},{2,0},{3,1},{4,6},{5,7},{6,4},{7,5},{8,10},{9,11},{10,... | collective-permute-start | bytes 884744 | tf_op jit(solution)/shard_map/ppermute | solution.py:206
  67.6 2.9 %collective-permute-start.13 = (f32[16,72,256]{2,1,0:T(8,128)S(1)}, f32[16,72,256]{2,1,0:T(8,128)S(1)}, u32[]{:S(2)}, u32[]{:S(2)}) collective-permute-start(f32[16,72,256]{2,1,0:T(8,128)S(1)} %bitcast.77), channel_id=1, source_target_pairs={{0,1},{1,0},{2,3},{3,2},{4,5},{5,4},{6,7},{7,6},{8,9},{9,8},{10,11... | collective-permute-start | bytes 3538952 | tf_op jit(solution)/shard_map/ppermute | solution.py:206
  70.5 1.2 %copy-start = (f32[1024,256]{1,0:T(8,128)S(1)}, f32[1024,256]{1,0:T(8,128)}, u32[]{:S(2)}) copy-start(f32[1024,256]{1,0:T(8,128)} %start_ref.1) | copy-start | bytes 3145732

commit v3 on v2

--- a/solution.py
+++ b/solution.py
@@ -41,6 +41,13 @@
         dot(left_high, right_high, contract)
         + dot(left_high, right_low, contract)
         + dot(left_low, right_high, contract)
+    )
+
+
+def tall3(left, right, contract=(1, 0)):
+    tiles = range(0, left[0].shape[0], TILE)
+    return jnp.concatenate(
+        [dot3([part[t : t + TILE] for part in left], right, contract) for t in tiles], 0
     )
 
 
@@ -146,56 +153,59 @@
     return TILE * len(below_diagonal(blocks)) + HALF * blocks + HALF * blocks // 2
 
 
-def moments_kernel(me_ref, e_ref, out_ref, packed, diagonal):
+def moments_kernel(bounds, me_ref, e_ref, out_ref, rows_in, packed, diagonal, sems):
     blocks = e_ref.shape[1] // TILE
-    step = pl.program_id(0)
-
-    @pl.when(step == 0)
-    def _():
-        packed[...] = jnp.zeros_like(packed)
-        diagonal[...] = jnp.zeros_like(diagonal)
-
-    parts = [split2(e_ref[:, i * TILE : (i + 1) * TILE]) for i in range(blocks)]
-    flipped = [(high.T, low.T) for high, low in parts]
+    below = below_diagonal(blocks)
+    cuts = list(zip(bounds[:-1], bounds[1:]))
+    loads = [
+        pltpu.make_async_copy(
+            e_ref.at[first:last, :], rows_in.at[first:last, :], sems.at[index]
+        )
+        for index, (first, last) in enumerate(cuts)
+    ]
+    for load in loads:
+        load.start()
+    for index, (first, last) in enumerate(cuts):
+        loads[index].wait()
+        parts = [split2(rows_in[first:last, i * TILE : (i + 1) * TILE]) for i in range(blocks)]
+        flipped = [(high.T, low.T) for high, low in parts]
+        for j in range(blocks):
+            high, low = parts[j]
+            term = dot(flipped[j][0], high * jnp.bfloat16(0.5)) + dot(flipped[j][0], low)
+            diagonal[j] = term if index == 0 else diagonal[j] + term
+        for place, (i, j) in enumerate(below):
+            at = slice(place * TILE, (place + 1) * TILE)
+            term = dot3(flipped[i], parts[j])
+            packed[at, :] = term if index == 0 else packed[at, :] + term
+    lower = TILE * len(below)
+    corner = lower + HALF * blocks
     for j in range(blocks):
-        high, low = parts[j]
-        diagonal[j] += dot(flipped[j][0], high * jnp.bfloat16(0.5)) + dot(flipped[j][0], low)
-    for place, (i, j) in enumerate(below_diagonal(blocks)):
-        packed[place * TILE : (place + 1) * TILE, :] += dot3(flipped[i], parts[j])
-
-    @pl.when(step == pl.num_programs(0) - 1)
-    def _():
-        lower = TILE * len(below_diagonal(blocks))
-        corner = lower + HALF * blocks
-        for j in range(blocks):
-            block = diagonal[j] + diagonal[j].T
-            packed[lower + j * HALF : lower + (j + 1) * HALF, :] = block[HALF:]
-            at = corner + j // 2 * HALF
-            side = j % 2 * HALF
-            packed[at : at + HALF, side : side + HALF] = block[:HALF, :HALF]
-        pieces, rows, _ = out_ref.shape
-        for piece in range(pieces):
-            out_ref[piece ^ me_ref[0]] = packed[piece * rows : (piece + 1) * rows, :]
+        block = diagonal[j] + diagonal[j].T
+        packed[lower + j * HALF : lower + (j + 1) * HALF, :] = block[HALF:]
+        at = corner + j // 2 * HALF
+        side = j % 2 * HALF
+        packed[at : at + HALF, side : side + HALF] = block[:HALF, :HALF]
+    pieces, rows, _ = out_ref.shape
+    for piece in range(pieces):
+        out_ref[piece ^ me_ref[0]] = packed[piece * rows : (piece + 1) * rows, :]
 
 
 def moments(embeddings, me, pieces):
     rows, columns = embeddings.shape
     blocks = columns // TILE
     packed = packed_rows(blocks)
-    step = min(512, rows)
+    bounds = [0] + [rows // 8 * k for k in (1, 2, 4, 6, 8)]
     shape = (pieces, packed // pieces, TILE)
     return pl.pallas_call(
-        moments_kernel,
-        grid=(rows // step,),
-        in_specs=[
-            pl.BlockSpec(memory_space=pltpu.SMEM),
-            pl.BlockSpec((step, columns), lambda i: (i, 0)),
-        ],
-        out_specs=pl.BlockSpec(shape, lambda i: (0, 0, 0)),
+        functools.partial(moments_kernel, bounds),
+        in_specs=[pl.BlockSpec(memory_space=pltpu.SMEM), pl.BlockSpec(memory_space=pl.ANY)],
+        out_specs=pl.BlockSpec(memory_space=pltpu.VMEM),
         out_shape=jax.ShapeDtypeStruct(shape, jnp.float32),
         scratch_shapes=[
+            pltpu.VMEM((rows, columns), jnp.float32),
             pltpu.VMEM((packed, TILE), jnp.float32),
             pltpu.VMEM((blocks, TILE, TILE), jnp.float32),
+            pltpu.SemaphoreType.DMA((len(bounds) - 1,)),
         ],
         compiler_params=pltpu.CompilerParams(vmem_limit_bytes=VMEM_LIMIT),
         name="moments",
@@ -242,7 +252,10 @@
     packed, c_high, c_low, work, gram, cross, rows_in, rows_out, sems,
 ):
     load = pltpu.make_async_copy(e_ref, rows_in, sems.at[0])
+    first_load = pltpu.make_async_copy(start_ref, work, sems.at[2])
+    first_load.start()
     load.start()
+    store = pltpu.make_async_copy(rows_out, scores_ref, sems.at[1])
     pieces, rows, _ = c_ref.shape
     columns, width = start_ref.shape
     blocks = columns // TILE
@@ -267,20 +280,23 @@
         put(j, j, jnp.concatenate([jnp.concatenate(top, 1), bottom], 0))
 
     step_rows = rows_in.shape[0] * BLOCK // width
-    basis = start_ref[...]
+    first_load.wait()
+    basis = work[...]
     for index in range(ITERS):
         current = split2(basis)
-        work[...] = dot3((c_high[...], c_low[...]), current)
+        for t in range(0, columns, TILE):
+            at = slice(t, t + TILE)
+            work[at, :] = dot3((c_high[at, :], c_low[at, :]), current)
         product = split2(work[...])
         gram[...] = dot3(current, product, (0, 0))
         invert_factor(gram)
         inverse = split2(gram[...])
-        summed = split2(dot3(product, inverse, (1, 1)))
+        summed = split2(tall3(product, inverse, (1, 1)))
         cross[...] = self_product(summed)
         if index < ITERS - 1:
             invert_factor(cross)
         else:
-            weights = split2(dot3(current, inverse, (1, 1)) * scale)
+            weights = split2(tall3(current, inverse, (1, 1)) * scale)
             load.wait()
 
             def beside(step):
@@ -288,9 +304,9 @@
                 rows_out[at, :] = dot3(split2(rows_in[at, :]), weights)
 
             invert_factor(cross, beside)
-        basis = dot3(summed, split2(cross[...]), (1, 1))
-    store = pltpu.make_async_copy(rows_out, scores_ref, sems.at[1])
-    store.start()
+        if index == ITERS - 1:
+            store.start()
+        basis = tall3(summed, split2(cross[...]), (1, 1))
     axes_ref[...] = basis * math.sqrt(columns)
     store.wait()
 
@@ -303,7 +319,7 @@
     anywhere = pl.BlockSpec(memory_space=pl.ANY)
     return pl.pallas_call(
         functools.partial(iterate_kernel, scale),
-        in_specs=[pl.BlockSpec(memory_space=pltpu.SMEM), vmem, vmem, anywhere],
+        in_specs=[pl.BlockSpec(memory_space=pltpu.SMEM), vmem, anywhere, anywhere],
         out_specs=[vmem, anywhere],
         out_shape=[
             jax.ShapeDtypeStruct((columns, width), jnp.float32),
@@ -318,7 +334,7 @@
             pltpu.VMEM((width, width), jnp.float32),
             pltpu.VMEM((count, columns), jnp.float32),
             pltpu.VMEM((count, width), jnp.float32),
-            pltpu.SemaphoreType.DMA((2,)),
+            pltpu.SemaphoreType.DMA((3,)),
         ],
         compiler_params=pltpu.CompilerParams(vmem_limit_bytes=VMEM_LIMIT),
         name="iterate",

time: 113 us -> 108 us (0.956)
  Pallas kernels: 50.8 us -> 46.4 us
    pallas_call x1, Pallas kernels: 40.7 us -> 37.1 us  [iterate(): pl.pallas_call(functools.partial(iterate_kernel, scale), in_specs=[pl.Blo...]
where the time goes in v3:
time: 108 us
  Pallas kernels  46.4 us (43%)
  waiting for transfers between devices  41.7 us (39%)
  starting transfers between devices  17.3 us (16%)
  local copies, waits for them, and re-layouts  1.19 us (1%)
    ppermute x14, waiting for transfers between devices, exchange(): return lax.ppermute(x, 'dp', [(d, d ^ flip) for d in range(devices)])  41.7 us
    pallas_call x1, Pallas kernels, iterate(): pl.pallas_call(functools.partial(iterate_kernel, scale), in_specs=[pl.Blo...  37.1 us
    ppermute x14, starting transfers between devices, exchange(): return lax.ppermute(x, 'dp', [(d, d ^ flip) for d in range(devices)])  17.3 us
    pallas_call x1, Pallas kernels, moments(): pl.pallas_call(functools.partial(moments_kernel, bounds), in_specs=[pl.Bl...  9.28 us
  transfers between devices with their start and end apart: 14, of which 12 were waited for; matrix products, arithmetic and copies ran while one was open for 0% of the time, Pallas kernels for 0%

profile of v3, /device:TPU:0, one launch (start us, length us, event | category | flops | bytes accessed | tf_op | source)
XLA Modules:
  0.0 108.1 jit_solution(1473856073428456146)
XLA Ops:
  0.6 9.3 %moments.1 = f32[32,72,256]{2,1,0:T(8,128)S(1)} custom-call(s32[1]{0:T(128)} %bitcast.me_ref, f32[2048,1024]{1,0:T(8,128)} %e_ref.3), custom_call_target="tpu_custom_call" | custom-call | tf_op jit(solution)/shard_map/moments/pallas_call | solution.py:199
  9.9 0.1 slice_bitcast_fusion
  10.0 0.5 collective-permute-start
  10.5 2.5 %collective-permute-done = f32[16,72,256]{2,1,0:T(8,128)S(1)} collective-permute-done((f32[16,72,256]{2,1,0:T(8,128)S(1)}, f32[16,72,256]{2,1,0:T(8,128)S(1)}, u32[]{:S(2)}, u32[]{:S(2)}) %collective-permute-start) | collective-permute-done | bytes 1179680 | tf_op jit(solution)/shard_map/ppermute | solution.py:216
  13.0 0.2 fusion
  13.3 2.9 %collective-permute-start.1 = (f32[4,72,256]{2,1,0:T(8,128)S(1)}, f32[4,72,256]{2,1,0:T(8,128)S(1)}, u32[]{:S(2)}, u32[]{:S(2)}) collective-permute-start(f32[4,72,256]{2,1,0:T(8,128)S(1)} %get-tuple-element.2), channel_id=1, source_target_pairs={{0,2},{1,3},{2,0},{3,1},{4,6},{5,7},{6,4},{7,5},{8,10},{9,11},{10,... | collective-permute-start | bytes 884744 | tf_op jit(solution)/shard_map/ppermute | solution.py:216
  16.3 1.5 %collective-permute-start.2 = (f32[4,72,256]{2,1,0:T(8,128)S(1)}, f32[4,72,256]{2,1,0:T(8,128)S(1)}, u32[]{:S(2)}, u32[]{:S(2)}) collective-permute-start(f32[4,72,256]{2,1,0:T(8,128)S(1)} %get-tuple-element.3), channel_id=1, source_target_pairs={{0,4},{1,5},{2,6},{3,7},{4,0},{5,1},{6,2},{7,3},{8,12},{9,13},{10,... | collective-permute-start | bytes 884744 | tf_op jit(solution)/shard_map/ppermute | solution.py:216
  17.8 6.3 %collective-permute-done.1 = f32[4,72,256]{2,1,0:T(8,128)S(1)} collective-permute-done((f32[4,72,256]{2,1,0:T(8,128)S(1)}, f32[4,72,256]{2,1,0:T(8,128)S(1)}, u32[]{:S(2)}, u32[]{:S(2)}) %collective-permute-start.1) | collective-permute-done | bytes 294944 | tf_op jit(solution)/shard_map/ppermute | solution.py:216
  24.1 7.3 %collective-permute-done.2 = f32[4,72,256]{2,1,0:T(8,128)S(1)} collective-permute-done((f32[4,72,256]{2,1,0:T(8,128)S(1)}, f32[4,72,256]{2,1,0:T(8,128)S(1)}, u32[]{:S(2)}, u32[]{:S(2)}) %collective-permute-start.2) | collective-permute-done | bytes 294944 | tf_op jit(solution)/shard_map/ppermute | solution.py:216
  31.4 0.1 fusion.4
  31.5 1.6 %collective-permute-start.4 = (f32[1,72,256]{2,1,0:T(8,128)S(1)}, f32[1,72,256]{2,1,0:T(8,128)S(1)}, u32[]{:S(2)}, u32[]{:S(2)}) collective-permute-start(f32[1,72,256]{2,1,0:T(8,128)S(1)} %get-tuple-element.7), channel_id=1, source_target_pairs={{0,8},{1,9},{2,10},{3,11},{4,12},{5,13},{6,14},{7,15},{8,0},{9,1},... | collective-permute-start | bytes 221192 | tf_op jit(solution)/shard_map/ppermute | solution.py:216
  33.1 2.5 %collective-permute-start.6 = (f32[1,72,256]{2,1,0:T(8,128)S(1)}, f32[1,72,256]{2,1,0:T(8,128)S(1)}, u32[]{:S(2)}, u32[]{:S(2)}) collective-permute-start(f32[1,72,256]{2,1,0:T(8,128)S(1)} %get-tuple-element.8), channel_id=1, source_target_pairs={{0,24},{1,25},{2,26},{3,27},{4,28},{5,29},{6,30},{7,31},{8,16},{9,... | collective-permute-start | bytes 221192 | tf_op jit(solution)/shard_map/ppermute | solution.py:216
  35.6 0.1 collective-permute-start.5
  35.7 0.2 collective-permute-done.4
  35.9 3.6 %collective-permute-done.6 = f32[1,72,256]{2,1,0:T(8,128)S(1)} collective-permute-done((f32[1,72,256]{2,1,0:T(8,128)S(1)}, f32[1,72,256]{2,1,0:T(8,128)S(1)}, u32[]{:S(2)}, u32[]{:S(2)}) %collective-permute-start.6) | collective-permute-done | bytes 73760 | tf_op jit(solution)/shard_map/ppermute | solution.py:216
  39.5 2.5 %collective-permute-done.5 = f32[1,72,256]{2,1,0:T(8,128)S(1)} collective-permute-done((f32[1,72,256]{2,1,0:T(8,128)S(1)}, f32[1,72,256]{2,1,0:T(8,128)S(1)}, u32[]{:S(2)}, u32[]{:S(2)}) %collective-permute-start.5) | collective-permute-done | bytes 73760 | tf_op jit(solution)/shard_map/ppermute | solution.py:216
  42.0 2.5 %collective-permute-start.9 = (f32[1,72,256]{2,1,0:T(8,128)S(1)}, f32[1,72,256]{2,1,0:T(8,128)S(1)}, u32[]{:S(2)}, u32[]{:S(2)}) collective-permute-start(f32[1,72,256]{2,1,0:T(8,128)S(1)} %fusion.9), channel_id=1, source_target_pairs={{0,24},{1,25},{2,26},{3,27},{4,28},{5,29},{6,30},{7,31},{8,16},{9,... | collective-permute-start | bytes 221192 | tf_op jit(solution)/shard_map/ppermute | solution.py:216
  44.6 1.9 %collective-permute-start.7 = (f32[1,72,256]{2,1,0:T(8,128)S(1)}, f32[1,72,256]{2,1,0:T(8,128)S(1)}, u32[]{:S(2)}, u32[]{:S(2)}) collective-permute-start(f32[1,72,256]{2,1,0:T(8,128)S(1)} %fusion.9), channel_id=1, source_target_pairs={{0,8},{1,9},{2,10},{3,11},{4,12},{5,13},{6,14},{7,15},{8,0},{9,1},... | collective-permute-start | bytes 221192 | tf_op jit(solution)/shard_map/ppermute | solution.py:216
  46.5 2.7 %collective-permute-done.9 = f32[1,72,256]{2,1,0:T(8,128)S(1)} collective-permute-done((f32[1,72,256]{2,1,0:T(8,128)S(1)}, f32[1,72,256]{2,1,0:T(8,128)S(1)}, u32[]{:S(2)}, u32[]{:S(2)}) %collective-permute-start.9) | collective-permute-done | bytes 73760 | tf_op jit(solution)/shard_map/ppermute | solution.py:216
  49.1 1.7 %collective-permute-done.8 = f32[1,72,256]{2,1,0:T(8,128)S(1)} collective-permute-done((f32[1,72,256]{2,1,0:T(8,128)S(1)}, f32[1,72,256]{2,1,0:T(8,128)S(1)}, u32[]{:S(2)}, u32[]{:S(2)}) %collective-permute-start.8) | collective-permute-done | bytes 73760 | tf_op jit(solution)/shard_map/ppermute | solution.py:216
  50.9 1.6 %collective-permute-start.12 = (f32[4,72,256]{2,1,0:T(8,128)S(1)}, f32[4,72,256]{2,1,0:T(8,128)S(1)}, u32[]{:S(2)}, u32[]{:S(2)}) collective-permute-start(f32[4,72,256]{2,1,0:T(8,128)S(1)} %get-tuple-element.6), channel_id=1, source_target_pairs={{0,6},{1,7},{2,4},{3,5},{4,2},{5,3},{6,0},{7,1},{8,14},{9,15},{10,... | collective-permute-start | bytes 884744 | tf_op jit(solution)/shard_map/ppermute | solution.py:216
  52.5 1.4 %collective-permute-start.11 = (f32[4,72,256]{2,1,0:T(8,128)S(1)}, f32[4,72,256]{2,1,0:T(8,128)S(1)}, u32[]{:S(2)}, u32[]{:S(2)}) collective-permute-start(f32[4,72,256]{2,1,0:T(8,128)S(1)} %get-tuple-element.6), channel_id=1, source_target_pairs={{0,4},{1,5},{2,6},{3,7},{4,0},{5,1},{6,2},{7,3},{8,12},{9,13},{10,... | collective-permute-start | bytes 884744 | tf_op jit(solution)/shard_map/ppermute | solution.py:216
  53.9 0.6 collective-permute-start.10
  54.4 7.4 %collective-permute-done.12 = f32[4,72,256]{2,1,0:T(8,128)S(1)} collective-permute-done((f32[4,72,256]{2,1,0:T(8,128)S(1)}, f32[4,72,256]{2,1,0:T(8,128)S(1)}, u32[]{:S(2)}, u32[]{:S(2)}) %collective-permute-start.12) | collective-permute-done | bytes 294944 | tf_op jit(solution)/shard_map/ppermute | solution.py:216
  61.8 4.7 %collective-permute-done.11 = f32[4,72,256]{2,1,0:T(8,128)S(1)} collective-permute-done((f32[4,72,256]{2,1,0:T(8,128)S(1)}, f32[4,72,256]{2,1,0:T(8,128)S(1)}, u32[]{:S(2)}, u32[]{:S(2)}) %collective-permute-start.11) | collective-permute-done | bytes 294944 | tf_op jit(solution)/shard_map/ppermute | solution.py:216
  66.5 0.1 collective-permute-done.10
  66.6 0.1 pad_maximum_fusion.1
  66.7 0.1 collective-permute-start.13
  66.8 2.8 %collective-permute-done.13 = f32[16,72,256]{2,1,0:T(8,128)S(1)} collective-permute-done((f32[16,72,256]{2,1,0:T(8,128)S(1)}, f32[16,72,256]{2,1,0:T(8,128)S(1)}, u32[]{:S(2)}, u32[]{:S(2)}) %collective-permute-start.13) | collective-permute-done | bytes 1179680 | tf_op jit(solution)/shard_map/ppermute | solution.py:216
  69.6 0.2 pad_maximum_fusion
  69.8 1.0 copy-done
  70.8 37.1 %iterate.1 = (f32[1024,256]{1,0:T(8,128)}, f32[2048,256]{1,0:T(8,128)}) custom-call(s32[1]{0:T(128)} %bitcast.me_ref, f32[32,72,256]{2,1,0:T(8,128)S(1)} %bitcast.74, f32[1024,256]{1,0:T(8,128)S(1)} %copy-done, f32[2048,1024]{1,0:T(8,128)} %e_ref.3), custom_call_target="tpu_custom_call" | custom-call | tf_op jit(solution)/shard_map/iterate/pallas_call | solution.py:320
  (9 shorter events, 0.2 us)
Async XLA Ops:
  10.0 3.0 %collective-permute-start = (f32[16,72,256]{2,1,0:T(8,128)S(1)}, f32[16,72,256]{2,1,0:T(8,128)S(1)}, u32[]{:S(2)}, u32[]{:S(2)}) collective-permute-start(f32[16,72,256]{2,1,0:T(8,128)S(1)} %slice_bitcast_fusion), channel_id=1, source_target_pairs={{0,1},{1,0},{2,3},{3,2},{4,5},{5,4},{6,7},{7,6},{8,9},{9,8},{10,11... | collective-permute-start | bytes 3538952 | tf_op jit(solution)/shard_map/ppermute | solution.py:216
  13.3 10.7 %collective-permute-start.1 = (f32[4,72,256]{2,1,0:T(8,128)S(1)}, f32[4,72,256]{2,1,0:T(8,128)S(1)}, u32[]{:S(2)}, u32[]{:S(2)}) collective-permute-start(f32[4,72,256]{2,1,0:T(8,128)S(1)} %get-tuple-element.2), channel_id=1, source_target_pairs={{0,2},{1,3},{2,0},{3,1},{4,6},{5,7},{6,4},{7,5},{8,10},{9,11},{10,... | collective-permute-start | bytes 884744 | tf_op jit(solution)/shard_map/ppermute | solution.py:216
  16.3 15.1 %collective-permute-start.2 = (f32[4,72,256]{2,1,0:T(8,128)S(1)}, f32[4,72,256]{2,1,0:T(8,128)S(1)}, u32[]{:S(2)}, u32[]{:S(2)}) collective-permute-start(f32[4,72,256]{2,1,0:T(8,128)S(1)} %get-tuple-element.3), channel_id=1, source_target_pairs={{0,4},{1,5},{2,6},{3,7},{4,0},{5,1},{6,2},{7,3},{8,12},{9,13},{10,... | collective-permute-start | bytes 884744 | tf_op jit(solution)/shard_map/ppermute | solution.py:216
  17.8 13.6 %collective-permute-start.3 = (f32[4,72,256]{2,1,0:T(8,128)S(1)}, f32[4,72,256]{2,1,0:T(8,128)S(1)}, u32[]{:S(2)}, u32[]{:S(2)}) collective-permute-start(f32[4,72,256]{2,1,0:T(8,128)S(1)} %get-tuple-element.4), channel_id=1, source_target_pairs={{0,6},{1,7},{2,4},{3,5},{4,2},{5,3},{6,0},{7,1},{8,14},{9,15},{10,... | collective-permute-start | bytes 884744 | tf_op jit(solution)/shard_map/ppermute | solution.py:216
  31.5 4.4 %collective-permute-start.4 = (f32[1,72,256]{2,1,0:T(8,128)S(1)}, f32[1,72,256]{2,1,0:T(8,128)S(1)}, u32[]{:S(2)}, u32[]{:S(2)}) collective-permute-start(f32[1,72,256]{2,1,0:T(8,128)S(1)} %get-tuple-element.7), channel_id=1, source_target_pairs={{0,8},{1,9},{2,10},{3,11},{4,12},{5,13},{6,14},{7,15},{8,0},{9,1},... | collective-permute-start | bytes 221192 | tf_op jit(solution)/shard_map/ppermute | solution.py:216
  33.1 6.4 %collective-permute-start.6 = (f32[1,72,256]{2,1,0:T(8,128)S(1)}, f32[1,72,256]{2,1,0:T(8,128)S(1)}, u32[]{:S(2)}, u32[]{:S(2)}) collective-permute-start(f32[1,72,256]{2,1,0:T(8,128)S(1)} %get-tuple-element.8), channel_id=1, source_target_pairs={{0,24},{1,25},{2,26},{3,27},{4,28},{5,29},{6,30},{7,31},{8,16},{9,... | collective-permute-start | bytes 221192 | tf_op jit(solution)/shard_map/ppermute | solution.py:216
  35.6 6.4 %collective-permute-start.5 = (f32[1,72,256]{2,1,0:T(8,128)S(1)}, f32[1,72,256]{2,1,0:T(8,128)S(1)}, u32[]{:S(2)}, u32[]{:S(2)}) collective-permute-start(f32[1,72,256]{2,1,0:T(8,128)S(1)} %get-tuple-element.9), channel_id=1, source_target_pairs={{0,16},{1,17},{2,18},{3,19},{4,20},{5,21},{6,22},{7,23},{8,24},{9,... | collective-permute-start | bytes 221192 | tf_op jit(solution)/shard_map/ppermute | solution.py:216
  42.0 7.1 %collective-permute-start.9 = (f32[1,72,256]{2,1,0:T(8,128)S(1)}, f32[1,72,256]{2,1,0:T(8,128)S(1)}, u32[]{:S(2)}, u32[]{:S(2)}) collective-permute-start(f32[1,72,256]{2,1,0:T(8,128)S(1)} %fusion.9), channel_id=1, source_target_pairs={{0,24},{1,25},{2,26},{3,27},{4,28},{5,29},{6,30},{7,31},{8,16},{9,... | collective-permute-start | bytes 221192 | tf_op jit(solution)/shard_map/ppermute | solution.py:216
  44.6 6.3 %collective-permute-start.8 = (f32[1,72,256]{2,1,0:T(8,128)S(1)}, f32[1,72,256]{2,1,0:T(8,128)S(1)}, u32[]{:S(2)}, u32[]{:S(2)}) collective-permute-start(f32[1,72,256]{2,1,0:T(8,128)S(1)} %fusion.9), channel_id=1, source_target_pairs={{0,16},{1,17},{2,18},{3,19},{4,20},{5,21},{6,22},{7,23},{8,24},{9,... | collective-permute-start | bytes 221192 | tf_op jit(solution)/shard_map/ppermute | solution.py:216
  44.6 6.3 %collective-permute-start.7 = (f32[1,72,256]{2,1,0:T(8,128)S(1)}, f32[1,72,256]{2,1,0:T(8,128)S(1)}, u32[]{:S(2)}, u32[]{:S(2)}) collective-permute-start(f32[1,72,256]{2,1,0:T(8,128)S(1)} %fusion.9), channel_id=1, source_target_pairs={{0,8},{1,9},{2,10},{3,11},{4,12},{5,13},{6,14},{7,15},{8,0},{9,1},... | collective-permute-start | bytes 221192 | tf_op jit(solution)/shard_map/ppermute | solution.py:216
  50.9 11.0 %collective-permute-start.12 = (f32[4,72,256]{2,1,0:T(8,128)S(1)}, f32[4,72,256]{2,1,0:T(8,128)S(1)}, u32[]{:S(2)}, u32[]{:S(2)}) collective-permute-start(f32[4,72,256]{2,1,0:T(8,128)S(1)} %get-tuple-element.6), channel_id=1, source_target_pairs={{0,6},{1,7},{2,4},{3,5},{4,2},{5,3},{6,0},{7,1},{8,14},{9,15},{10,... | collective-permute-start | bytes 884744 | tf_op jit(solution)/shard_map/ppermute | solution.py:216
  52.5 14.1 %collective-permute-start.11 = (f32[4,72,256]{2,1,0:T(8,128)S(1)}, f32[4,72,256]{2,1,0:T(8,128)S(1)}, u32[]{:S(2)}, u32[]{:S(2)}) collective-permute-start(f32[4,72,256]{2,1,0:T(8,128)S(1)} %get-tuple-element.6), channel_id=1, source_target_pairs={{0,4},{1,5},{2,6},{3,7},{4,0},{5,1},{6,2},{7,3},{8,12},{9,13},{10,... | collective-permute-start | bytes 884744 | tf_op jit(solution)/shard_map/ppermute | solution.py:216
  53.9 12.7 %collective-permute-start.10 = (f32[4,72,256]{2,1,0:T(8,128)S(1)}, f32[4,72,256]{2,1,0:T(8,128)S(1)}, u32[]{:S(2)}, u32[]{:S(2)}) collective-permute-start(f32[4,72,256]{2,1,0:T(8,128)S(1)} %get-tuple-element.6), channel_id=1, source_target_pairs={{0,2},{1,3},{2,0},{3,1},{4,6},{5,7},{6,4},{7,5},{8,10},{9,11},{10,... | collective-permute-start | bytes 884744 | tf_op jit(solution)/shard_map/ppermute | solution.py:216
  66.7 2.9 %collective-permute-start.13 = (f32[16,72,256]{2,1,0:T(8,128)S(1)}, f32[16,72,256]{2,1,0:T(8,128)S(1)}, u32[]{:S(2)}, u32[]{:S(2)}) collective-permute-start(f32[16,72,256]{2,1,0:T(8,128)S(1)} %bitcast.77), channel_id=1, source_target_pairs={{0,1},{1,0},{2,3},{3,2},{4,5},{5,4},{6,7},{7,6},{8,9},{9,8},{10,11... | collective-permute-start | bytes 3538952 | tf_op jit(solution)/shard_map/ppermute | solution.py:216
  69.6 1.2 %copy-start = (f32[1024,256]{1,0:T(8,128)S(1)}, f32[1024,256]{1,0:T(8,128)}, u32[]{:S(2)}) copy-start(f32[1024,256]{1,0:T(8,128)} %start_ref.1) | copy-start | bytes 3145732

commit v4 on v3

--- a/solution.py
+++ b/solution.py
@@ -11,6 +11,7 @@
 ITERS = 2
 BLOCK = 32
 SUB = 8
+AHEAD = 2
 LANES = 128
 TILE = 256
 HALF = TILE // 2
@@ -84,65 +85,75 @@
 
     spread_columns(0)
     for tile in range(tiles):
-        if tile + 1 < tiles:
-            spread_columns(tile + 1)
+        first = offset + tile * SUB
+        mine = (lane >= first) & (lane < first + SUB)
+        unit = (lane - first == row).astype(jnp.float32)
+        for i in range(tile, tiles):
+            rows[i][0] = jnp.where(mine, unit if i == tile else 0.0, rows[i][0])
+        scales = jnp.zeros((SUB, LANES), jnp.float32)
         for k in range(SUB):
+            ahead = k >= AHEAD and tile + 1 < tiles
+            if k == AHEAD and ahead:
+                spread_columns(tile + 1)
             j = tile * SUB + k
             column = columns.pop(j)
             pivot = column[tile][k : k + 1]
             inverse = 1.0 / pivot
             mult = {i: column[i] * inverse for i in range(tile, tiles)}
-            for q in range(j + 1, min((tile + 2) * SUB, BLOCK)):
+            for q in range(j + 1, (tile + (2 if ahead else 1)) * SUB):
                 entry = column[q // SUB][q % SUB : q % SUB + 1]
                 for i in range(q // SUB, tiles):
                     columns[q][i] = columns[q][i] - mult[i] * entry
-            scale = lax.rsqrt(pivot)
-            here = lane == offset + j
-            top = [jnp.where(here[:1], 1.0, rows[tile][0][k : k + 1])]
-            top += [group[k : k + 1] for group in rows[tile][1:]]
+            scales = jnp.where(row == k, lax.rsqrt(pivot), scales)
+            mult[tile] = jnp.where(row > k, mult[tile], 0.0)
+            top = [x[k : k + 1] for x in rows[tile]]
             for i in range(tile, tiles):
-                old = rows[i]
-                new = [jnp.where(here, 0.0, old[0])] + old[1:]
-                new = [x - mult[i] * y for x, y in zip(new, top)]
-                if i == tile:
-                    kept = [jnp.where(row == k, y * scale, x) for x, y in zip(old, top)]
-                    new = [jnp.where(row > k, x, y) for x, y in zip(new, kept)]
-                rows[i] = new
+                rows[i] = [x - mult[i] * y for x, y in zip(rows[i], top)]
+        rows[tile] = [x * scales for x in rows[tile]]
+    for tile in range(tiles - 1):
+        right = (lane >= offset + (tile + 1) * SUB) & (lane < offset + BLOCK)
+        rows[tile][0] = jnp.where(right, 0.0, rows[tile][0])
     return rows
 
 
 def invert_factor(a_ref, beside=None):
     n = a_ref.shape[0]
-    lane = lax.broadcasted_iota(jnp.int32, (BLOCK, n), 1)
-    row = lax.broadcasted_iota(jnp.int32, (BLOCK, n), 0)
-    panel = a_ref[0:BLOCK, :]
+    groups = range(n // LANES)
+    lane = lax.broadcasted_iota(jnp.int32, (1, LANES), 1)
+
+    def at(group):
+        return slice(group * LANES, (group + 1) * LANES)
+
+    panel = [a_ref[0:BLOCK, at(g)] for g in groups]
     for start in range(0, n, BLOCK):
         end = start + BLOCK
         if beside is not None:
             beside(start // BLOCK)
-        active = start // LANES
-        order = [active] + [g for g in range(n // LANES) if g != active]
-        rows = [
-            [panel[t : t + SUB, g * LANES : (g + 1) * LANES] for g in order]
-            for t in range(0, BLOCK, SUB)
-        ]
-        rows = eliminate(rows, start % LANES)
-        groups = [jnp.concatenate([tile[order.index(g)] for tile in rows], 0) for g in range(n // LANES)]
-        upper = jnp.concatenate(groups, 1)
-        done = jnp.where((lane < end) & (lane - start > row), 0.0, upper)
-        a_ref[start:end, :] = jnp.where(lane < end, done, 0.0)
+        active, offset = start // LANES, start % LANES
+        order = [active] + [g for g in groups if g != active]
+        rows = [[panel[g][t : t + SUB] for g in order] for t in range(0, BLOCK, SUB)]
+        rows = eliminate(rows, offset)
+        done = [jnp.concatenate([tile[order.index(g)] for tile in rows], 0) for g in groups]
+        for g in groups:
+            kept = done[g] if g < active else jnp.zeros((BLOCK, LANES), jnp.float32)
+            if g == active:
+                kept = jnp.where(lane < offset + BLOCK, done[g], 0.0)
+            a_ref[start:end, at(g)] = kept
         if end == n:
             break
-        left, right = stack_left(upper), stack_right(done)
+        left, right = (stack(jnp.concatenate(done, 1)) for stack in (stack_left, stack_right))
+        gone = (lane >= offset) & (lane < offset + BLOCK)
 
         def updated(first, last):
-            col = lax.broadcasted_iota(jnp.int32, (last - first, n), 1)
-            old = jnp.where((col >= start) & (col < end), 0.0, a_ref[first:last, :])
-            return old - dot(left[:, first:last], right, (0, 0))
+            change = dot(left[:, first:last], right, (0, 0))
+            old = [a_ref[first:last, at(g)] for g in groups]
+            old[active] = jnp.where(gone, 0.0, old[active])
+            return [old[g] - change[:, at(g)] for g in groups]
 
         panel = updated(end, end + BLOCK)
         if end + BLOCK < n:
-            a_ref[end + BLOCK : n, :] = updated(end + BLOCK, n)
+            for g, value in zip(groups, updated(end + BLOCK, n)):
+                a_ref[end + BLOCK : n, at(g)] = value
 
 
 def below_diagonal(blocks):
@@ -153,7 +164,10 @@
     return TILE * len(below_diagonal(blocks)) + HALF * blocks + HALF * blocks // 2
 
 
-def moments_kernel(bounds, me_ref, e_ref, out_ref, rows_in, packed, diagonal, sems):
+def moments_kernel(
+    bounds, me_ref, e_ref, start_ref, out_ref, b_high, b_low,
+    rows_in, start_in, packed, diagonal, sems,
+):
     blocks = e_ref.shape[1] // TILE
     below = below_diagonal(blocks)
     cuts = list(zip(bounds[:-1], bounds[1:]))
@@ -163,6 +177,7 @@
         )
         for index, (first, last) in enumerate(cuts)
     ]
+    loads.append(pltpu.make_async_copy(start_ref, start_in, sems.at[len(cuts)]))
     for load in loads:
         load.start()
     for index, (first, last) in enumerate(cuts):
@@ -177,6 +192,8 @@
             at = slice(place * TILE, (place + 1) * TILE)
             term = dot3(flipped[i], parts[j])
             packed[at, :] = term if index == 0 else packed[at, :] + term
+    loads[-1].wait()
+    b_high[...], b_low[...] = split2(start_in[...])
     lower = TILE * len(below)
     corner = lower + HALF * blocks
     for j in range(blocks):
@@ -190,26 +207,35 @@
         out_ref[piece ^ me_ref[0]] = packed[piece * rows : (piece + 1) * rows, :]
 
 
-def moments(embeddings, me, pieces):
+def moments(embeddings, start_block, me, pieces):
     rows, columns = embeddings.shape
+    width = start_block.shape[1]
     blocks = columns // TILE
     packed = packed_rows(blocks)
     bounds = [0] + [rows // 8 * k for k in (1, 2, 4, 6, 8)]
     shape = (pieces, packed // pieces, TILE)
+    steps = len(bounds) - 1
+    vmem = pl.BlockSpec(memory_space=pltpu.VMEM)
+    anywhere = pl.BlockSpec(memory_space=pl.ANY)
     return pl.pallas_call(
         functools.partial(moments_kernel, bounds),
-        in_specs=[pl.BlockSpec(memory_space=pltpu.SMEM), pl.BlockSpec(memory_space=pl.ANY)],
-        out_specs=pl.BlockSpec(memory_space=pltpu.VMEM),
-        out_shape=jax.ShapeDtypeStruct(shape, jnp.float32),
+        in_specs=[pl.BlockSpec(memory_space=pltpu.SMEM), anywhere, anywhere],
+        out_specs=[vmem, vmem, vmem],
+        out_shape=[
+            jax.ShapeDtypeStruct(shape, jnp.float32),
+            jax.ShapeDtypeStruct((columns, width), jnp.bfloat16),
+            jax.ShapeDtypeStruct((columns, width), jnp.bfloat16),
+        ],
         scratch_shapes=[
             pltpu.VMEM((rows, columns), jnp.float32),
+            pltpu.VMEM((columns, width), jnp.float32),
             pltpu.VMEM((packed, TILE), jnp.float32),
             pltpu.VMEM((blocks, TILE, TILE), jnp.float32),
-            pltpu.SemaphoreType.DMA((len(bounds) - 1,)),
+            pltpu.SemaphoreType.DMA((steps + 1,)),
         ],
         compiler_params=pltpu.CompilerParams(vmem_limit_bytes=VMEM_LIMIT),
         name="moments",
-    )(me, embeddings)
+    )(me, embeddings, start_block)
 
 
 def exchange(x, flip, devices):
@@ -248,16 +274,14 @@
 
 
 def iterate_kernel(
-    scale, me_ref, c_ref, start_ref, e_ref, axes_ref, scores_ref,
+    scale, me_ref, c_ref, b_high, b_low, e_ref, axes_ref, scores_ref,
     packed, c_high, c_low, work, gram, cross, rows_in, rows_out, sems,
 ):
     load = pltpu.make_async_copy(e_ref, rows_in, sems.at[0])
-    first_load = pltpu.make_async_copy(start_ref, work, sems.at[2])
-    first_load.start()
     load.start()
     store = pltpu.make_async_copy(rows_out, scores_ref, sems.at[1])
     pieces, rows, _ = c_ref.shape
-    columns, width = start_ref.shape
+    columns, width = b_high.shape
     blocks = columns // TILE
     for piece in range(pieces):
         packed[piece * rows : (piece + 1) * rows, :] = c_ref[piece ^ me_ref[0]]
@@ -279,11 +303,9 @@
         top = [packed[at : at + HALF, side : side + HALF], bottom[:, :HALF].T]
         put(j, j, jnp.concatenate([jnp.concatenate(top, 1), bottom], 0))
 
-    step_rows = rows_in.shape[0] * BLOCK // width
-    first_load.wait()
-    basis = work[...]
+    step_rows = rows_out.shape[0] * BLOCK // width
     for index in range(ITERS):
-        current = split2(basis)
+        current = split2(basis) if index else (b_high[...], b_low[...])
         for t in range(0, columns, TILE):
             at = slice(t, t + TILE)
             work[at, :] = dot3((c_high[at, :], c_low[at, :]), current)
@@ -311,15 +333,15 @@
     store.wait()
 
 
-def iterate(summed, start_block, embeddings, me, scale):
-    columns, width = start_block.shape
+def iterate(summed, start_parts, embeddings, me, scale):
+    columns, width = start_parts[0].shape
     pieces, rows, _ = summed.shape
     count = embeddings.shape[0]
     vmem = pl.BlockSpec(memory_space=pltpu.VMEM)
     anywhere = pl.BlockSpec(memory_space=pl.ANY)
     return pl.pallas_call(
         functools.partial(iterate_kernel, scale),
-        in_specs=[pl.BlockSpec(memory_space=pltpu.SMEM), vmem, anywhere, anywhere],
+        in_specs=[pl.BlockSpec(memory_space=pltpu.SMEM)] + [vmem] * 3 + [anywhere],
         out_specs=[vmem, anywhere],
         out_shape=[
             jax.ShapeDtypeStruct((columns, width), jnp.float32),
@@ -334,11 +356,11 @@
             pltpu.VMEM((width, width), jnp.float32),
             pltpu.VMEM((count, columns), jnp.float32),
             pltpu.VMEM((count, width), jnp.float32),
-            pltpu.SemaphoreType.DMA((3,)),
+            pltpu.SemaphoreType.DMA((2,)),
         ],
         compiler_params=pltpu.CompilerParams(vmem_limit_bytes=VMEM_LIMIT),
         name="iterate",
-    )(me, summed, start_block, embeddings)
+    )(me, summed, *start_parts, embeddings)
 
 
 def body(embeddings, start_block):
@@ -349,8 +371,10 @@
     scattered = min(bits, ((packed // 8) & -(packed // 8)).bit_length() - 1)
     pieces = 1 << scattered
     me = (lax.axis_index("dp") % pieces).astype(jnp.int32).reshape(1)
-    summed = sum_over_devices(moments(embeddings, me, pieces), devices, scattered)
-    axes, scores = iterate(summed, start_block, embeddings, me, math.sqrt(rows * devices))
+    local, b_high, b_low = moments(embeddings, start_block, me, pieces)
+    summed = sum_over_devices(local, devices, scattered)
+    scale = math.sqrt(rows * devices)
+    axes, scores = iterate(summed, (b_high, b_low), embeddings, me, scale)
     return axes, scores
 
 

time: 108 us -> 107 us (level)
  Pallas kernels: 46.4 us -> 45 us
    pallas_call x1, Pallas kernels: 37.1 us -> 35.3 us  [iterate(): pl.pallas_call(functools.partial(iterate_kernel, scale), in_specs=[pl.Blo...]
where the time goes in v4:
time: 107 us
  Pallas kernels  45 us (42%)
  waiting for transfers between devices  41.7 us (39%)
  starting transfers between devices  17.3 us (16%)
  local copies, waits for them, and re-layouts  1.38 us (1%)
    ppermute x14, waiting for transfers between devices, exchange(): return lax.ppermute(x, 'dp', [(d, d ^ flip) for d in range(devices)])  41.7 us
    pallas_call x1, Pallas kernels, iterate(): pl.pallas_call(functools.partial(iterate_kernel, scale), in_specs=[pl.Blo...  35.3 us
    ppermute x14, starting transfers between devices, exchange(): return lax.ppermute(x, 'dp', [(d, d ^ flip) for d in range(devices)])  17.3 us
    pallas_call x1, Pallas kernels, moments(): pl.pallas_call(functools.partial(moments_kernel, bounds), in_specs=[pl.Bl...  9.77 us
  transfers between devices with their start and end apart: 14, of which 12 were waited for; matrix products, arithmetic and copies ran while one was open for 0% of the time, Pallas kernels for 0%

profile of v4, /device:TPU:0, one launch (start us, length us, event | category | flops | bytes accessed | tf_op | source)
XLA Modules:
  0.0 107.0 jit_solution(12687100208240384824)
XLA Ops:
  0.7 1.2 %copy-done = f32[1024,256]{1,0:T(8,128)S(1)} copy-done((f32[1024,256]{1,0:T(8,128)S(1)}, f32[1024,256]{1,0:T(8,128)}, u32[]{:S(2)}) %copy-start) | copy-done | bytes 1048600
  1.9 9.8 %moments.1 = (f32[32,72,256]{2,1,0:T(8,128)S(1)}, bf16[1024,256]{1,0:T(8,128)(2,1)S(1)}, bf16[1024,256]{1,0:T(8,128)(2,1)S(1)}) custom-call(s32[1]{0:T(128)} %bitcast.me_ref, f32[2048,1024]{1,0:T(8,128)} %e_ref.3, f32[1024,256]{1,0:T(8,128)S(1)} %copy-done), custom_call_target="tpu_custom_call" | custom-call | tf_op jit(solution)/shard_map/moments/pallas_call | solution.py:220
  11.6 0.1 slice_bitcast_fusion
  11.7 0.5 collective-permute-start
  12.2 2.5 %collective-permute-done = f32[16,72,256]{2,1,0:T(8,128)S(1)} collective-permute-done((f32[16,72,256]{2,1,0:T(8,128)S(1)}, f32[16,72,256]{2,1,0:T(8,128)S(1)}, u32[]{:S(2)}, u32[]{:S(2)}) %collective-permute-start) | collective-permute-done | bytes 1179680 | tf_op jit(solution)/shard_map/ppermute | solution.py:242
  14.7 0.2 fusion
  15.0 2.9 %collective-permute-start.1 = (f32[4,72,256]{2,1,0:T(8,128)S(1)}, f32[4,72,256]{2,1,0:T(8,128)S(1)}, u32[]{:S(2)}, u32[]{:S(2)}) collective-permute-start(f32[4,72,256]{2,1,0:T(8,128)S(1)} %get-tuple-element.8), channel_id=1, source_target_pairs={{0,2},{1,3},{2,0},{3,1},{4,6},{5,7},{6,4},{7,5},{8,10},{9,11},{10,... | collective-permute-start | bytes 884744 | tf_op jit(solution)/shard_map/ppermute | solution.py:242
  18.0 1.5 %collective-permute-start.2 = (f32[4,72,256]{2,1,0:T(8,128)S(1)}, f32[4,72,256]{2,1,0:T(8,128)S(1)}, u32[]{:S(2)}, u32[]{:S(2)}) collective-permute-start(f32[4,72,256]{2,1,0:T(8,128)S(1)} %get-tuple-element.9), channel_id=1, source_target_pairs={{0,4},{1,5},{2,6},{3,7},{4,0},{5,1},{6,2},{7,3},{8,12},{9,13},{10,... | collective-permute-start | bytes 884744 | tf_op jit(solution)/shard_map/ppermute | solution.py:242
  19.5 6.3 %collective-permute-done.1 = f32[4,72,256]{2,1,0:T(8,128)S(1)} collective-permute-done((f32[4,72,256]{2,1,0:T(8,128)S(1)}, f32[4,72,256]{2,1,0:T(8,128)S(1)}, u32[]{:S(2)}, u32[]{:S(2)}) %collective-permute-start.1) | collective-permute-done | bytes 294944 | tf_op jit(solution)/shard_map/ppermute | solution.py:242
  25.8 7.3 %collective-permute-done.2 = f32[4,72,256]{2,1,0:T(8,128)S(1)} collective-permute-done((f32[4,72,256]{2,1,0:T(8,128)S(1)}, f32[4,72,256]{2,1,0:T(8,128)S(1)}, u32[]{:S(2)}, u32[]{:S(2)}) %collective-permute-start.2) | collective-permute-done | bytes 294944 | tf_op jit(solution)/shard_map/ppermute | solution.py:242
  33.1 0.1 fusion.4
  33.2 1.6 %collective-permute-start.4 = (f32[1,72,256]{2,1,0:T(8,128)S(1)}, f32[1,72,256]{2,1,0:T(8,128)S(1)}, u32[]{:S(2)}, u32[]{:S(2)}) collective-permute-start(f32[1,72,256]{2,1,0:T(8,128)S(1)} %get-tuple-element.13), channel_id=1, source_target_pairs={{0,8},{1,9},{2,10},{3,11},{4,12},{5,13},{6,14},{7,15},{8,0},{9,1},... | collective-permute-start | bytes 221192 | tf_op jit(solution)/shard_map/ppermute | solution.py:242
  34.8 2.5 %collective-permute-start.6 = (f32[1,72,256]{2,1,0:T(8,128)S(1)}, f32[1,72,256]{2,1,0:T(8,128)S(1)}, u32[]{:S(2)}, u32[]{:S(2)}) collective-permute-start(f32[1,72,256]{2,1,0:T(8,128)S(1)} %get-tuple-element.14), channel_id=1, source_target_pairs={{0,24},{1,25},{2,26},{3,27},{4,28},{5,29},{6,30},{7,31},{8,16},{9,... | collective-permute-start | bytes 221192 | tf_op jit(solution)/shard_map/ppermute | solution.py:242
  37.3 0.1 collective-permute-start.5
  37.4 0.2 collective-permute-done.4
  37.6 3.6 %collective-permute-done.6 = f32[1,72,256]{2,1,0:T(8,128)S(1)} collective-permute-done((f32[1,72,256]{2,1,0:T(8,128)S(1)}, f32[1,72,256]{2,1,0:T(8,128)S(1)}, u32[]{:S(2)}, u32[]{:S(2)}) %collective-permute-start.6) | collective-permute-done | bytes 73760 | tf_op jit(solution)/shard_map/ppermute | solution.py:242
  41.2 2.5 %collective-permute-done.5 = f32[1,72,256]{2,1,0:T(8,128)S(1)} collective-permute-done((f32[1,72,256]{2,1,0:T(8,128)S(1)}, f32[1,72,256]{2,1,0:T(8,128)S(1)}, u32[]{:S(2)}, u32[]{:S(2)}) %collective-permute-start.5) | collective-permute-done | bytes 73760 | tf_op jit(solution)/shard_map/ppermute | solution.py:242
  43.7 2.5 %collective-permute-start.9 = (f32[1,72,256]{2,1,0:T(8,128)S(1)}, f32[1,72,256]{2,1,0:T(8,128)S(1)}, u32[]{:S(2)}, u32[]{:S(2)}) collective-permute-start(f32[1,72,256]{2,1,0:T(8,128)S(1)} %fusion.9), channel_id=1, source_target_pairs={{0,24},{1,25},{2,26},{3,27},{4,28},{5,29},{6,30},{7,31},{8,16},{9,... | collective-permute-start | bytes 221192 | tf_op jit(solution)/shard_map/ppermute | solution.py:242
  46.2 2.0 %collective-permute-start.7 = (f32[1,72,256]{2,1,0:T(8,128)S(1)}, f32[1,72,256]{2,1,0:T(8,128)S(1)}, u32[]{:S(2)}, u32[]{:S(2)}) collective-permute-start(f32[1,72,256]{2,1,0:T(8,128)S(1)} %fusion.9), channel_id=1, source_target_pairs={{0,8},{1,9},{2,10},{3,11},{4,12},{5,13},{6,14},{7,15},{8,0},{9,1},... | collective-permute-start | bytes 221192 | tf_op jit(solution)/shard_map/ppermute | solution.py:242
  48.2 2.7 %collective-permute-done.9 = f32[1,72,256]{2,1,0:T(8,128)S(1)} collective-permute-done((f32[1,72,256]{2,1,0:T(8,128)S(1)}, f32[1,72,256]{2,1,0:T(8,128)S(1)}, u32[]{:S(2)}, u32[]{:S(2)}) %collective-permute-start.9) | collective-permute-done | bytes 73760 | tf_op jit(solution)/shard_map/ppermute | solution.py:242
  50.8 1.7 %collective-permute-done.8 = f32[1,72,256]{2,1,0:T(8,128)S(1)} collective-permute-done((f32[1,72,256]{2,1,0:T(8,128)S(1)}, f32[1,72,256]{2,1,0:T(8,128)S(1)}, u32[]{:S(2)}, u32[]{:S(2)}) %collective-permute-start.8) | collective-permute-done | bytes 73760 | tf_op jit(solution)/shard_map/ppermute | solution.py:242
  52.6 1.6 %collective-permute-start.12 = (f32[4,72,256]{2,1,0:T(8,128)S(1)}, f32[4,72,256]{2,1,0:T(8,128)S(1)}, u32[]{:S(2)}, u32[]{:S(2)}) collective-permute-start(f32[4,72,256]{2,1,0:T(8,128)S(1)} %get-tuple-element.12), channel_id=1, source_target_pairs={{0,6},{1,7},{2,4},{3,5},{4,2},{5,3},{6,0},{7,1},{8,14},{9,15},{10,... | collective-permute-start | bytes 884744 | tf_op jit(solution)/shard_map/ppermute | solution.py:242
  54.2 1.4 %collective-permute-start.11 = (f32[4,72,256]{2,1,0:T(8,128)S(1)}, f32[4,72,256]{2,1,0:T(8,128)S(1)}, u32[]{:S(2)}, u32[]{:S(2)}) collective-permute-start(f32[4,72,256]{2,1,0:T(8,128)S(1)} %get-tuple-element.12), channel_id=1, source_target_pairs={{0,4},{1,5},{2,6},{3,7},{4,0},{5,1},{6,2},{7,3},{8,12},{9,13},{10,... | collective-permute-start | bytes 884744 | tf_op jit(solution)/shard_map/ppermute | solution.py:242
  55.6 0.5 collective-permute-start.10
  56.1 7.4 %collective-permute-done.12 = f32[4,72,256]{2,1,0:T(8,128)S(1)} collective-permute-done((f32[4,72,256]{2,1,0:T(8,128)S(1)}, f32[4,72,256]{2,1,0:T(8,128)S(1)}, u32[]{:S(2)}, u32[]{:S(2)}) %collective-permute-start.12) | collective-permute-done | bytes 294944 | tf_op jit(solution)/shard_map/ppermute | solution.py:242
  63.5 4.7 %collective-permute-done.11 = f32[4,72,256]{2,1,0:T(8,128)S(1)} collective-permute-done((f32[4,72,256]{2,1,0:T(8,128)S(1)}, f32[4,72,256]{2,1,0:T(8,128)S(1)}, u32[]{:S(2)}, u32[]{:S(2)}) %collective-permute-start.11) | collective-permute-done | bytes 294944 | tf_op jit(solution)/shard_map/ppermute | solution.py:242
  68.2 0.1 collective-permute-done.10
  68.3 0.1 pad_maximum_fusion.1
  68.4 0.1 collective-permute-start.13
  68.5 2.8 %collective-permute-done.13 = f32[16,72,256]{2,1,0:T(8,128)S(1)} collective-permute-done((f32[16,72,256]{2,1,0:T(8,128)S(1)}, f32[16,72,256]{2,1,0:T(8,128)S(1)}, u32[]{:S(2)}, u32[]{:S(2)}) %collective-permute-start.13) | collective-permute-done | bytes 1179680 | tf_op jit(solution)/shard_map/ppermute | solution.py:242
  71.3 0.2 pad_maximum_fusion
  71.5 35.3 %iterate.1 = (f32[1024,256]{1,0:T(8,128)}, f32[2048,256]{1,0:T(8,128)}) custom-call(s32[1]{0:T(128)} %bitcast.me_ref, f32[32,72,256]{2,1,0:T(8,128)S(1)} %bitcast.72, bf16[1024,256]{1,0:T(8,128)(2,1)S(1)} %get-tuple-element.6.b_high, bf16[1024,256]{1,0:T(8,128)(2,1)S(1)} %get-tuple-element.7.b_low, f32[2048,1024]{1,0:T(8,128)} %e_ref.3), custom_call_target="tpu_custom_call" | custom-call | tf_op jit(solution)/shard_map/iterate/pallas_call | solution.py:342
  (9 shorter events, 0.2 us)
Async XLA Ops:
  0.6 1.2 %copy-start = (f32[1024,256]{1,0:T(8,128)S(1)}, f32[1024,256]{1,0:T(8,128)}, u32[]{:S(2)}) copy-start(f32[1024,256]{1,0:T(8,128)} %start_ref.1) | copy-start | bytes 3145732
  11.7 3.0 %collective-permute-start = (f32[16,72,256]{2,1,0:T(8,128)S(1)}, f32[16,72,256]{2,1,0:T(8,128)S(1)}, u32[]{:S(2)}, u32[]{:S(2)}) collective-permute-start(f32[16,72,256]{2,1,0:T(8,128)S(1)} %slice_bitcast_fusion), channel_id=1, source_target_pairs={{0,1},{1,0},{2,3},{3,2},{4,5},{5,4},{6,7},{7,6},{8,9},{9,8},{10,11... | collective-permute-start | bytes 3538952 | tf_op jit(solution)/shard_map/ppermute | solution.py:242
  15.0 10.7 %collective-permute-start.1 = (f32[4,72,256]{2,1,0:T(8,128)S(1)}, f32[4,72,256]{2,1,0:T(8,128)S(1)}, u32[]{:S(2)}, u32[]{:S(2)}) collective-permute-start(f32[4,72,256]{2,1,0:T(8,128)S(1)} %get-tuple-element.8), channel_id=1, source_target_pairs={{0,2},{1,3},{2,0},{3,1},{4,6},{5,7},{6,4},{7,5},{8,10},{9,11},{10,... | collective-permute-start | bytes 884744 | tf_op jit(solution)/shard_map/ppermute | solution.py:242
  18.0 15.1 %collective-permute-start.2 = (f32[4,72,256]{2,1,0:T(8,128)S(1)}, f32[4,72,256]{2,1,0:T(8,128)S(1)}, u32[]{:S(2)}, u32[]{:S(2)}) collective-permute-start(f32[4,72,256]{2,1,0:T(8,128)S(1)} %get-tuple-element.9), channel_id=1, source_target_pairs={{0,4},{1,5},{2,6},{3,7},{4,0},{5,1},{6,2},{7,3},{8,12},{9,13},{10,... | collective-permute-start | bytes 884744 | tf_op jit(solution)/shard_map/ppermute | solution.py:242
  19.5 13.6 %collective-permute-start.3 = (f32[4,72,256]{2,1,0:T(8,128)S(1)}, f32[4,72,256]{2,1,0:T(8,128)S(1)}, u32[]{:S(2)}, u32[]{:S(2)}) collective-permute-start(f32[4,72,256]{2,1,0:T(8,128)S(1)} %get-tuple-element.10), channel_id=1, source_target_pairs={{0,6},{1,7},{2,4},{3,5},{4,2},{5,3},{6,0},{7,1},{8,14},{9,15},{10,... | collective-permute-start | bytes 884744 | tf_op jit(solution)/shard_map/ppermute | solution.py:242
  33.2 4.4 %collective-permute-start.4 = (f32[1,72,256]{2,1,0:T(8,128)S(1)}, f32[1,72,256]{2,1,0:T(8,128)S(1)}, u32[]{:S(2)}, u32[]{:S(2)}) collective-permute-start(f32[1,72,256]{2,1,0:T(8,128)S(1)} %get-tuple-element.13), channel_id=1, source_target_pairs={{0,8},{1,9},{2,10},{3,11},{4,12},{5,13},{6,14},{7,15},{8,0},{9,1},... | collective-permute-start | bytes 221192 | tf_op jit(solution)/shard_map/ppermute | solution.py:242
  34.8 6.4 %collective-permute-start.6 = (f32[1,72,256]{2,1,0:T(8,128)S(1)}, f32[1,72,256]{2,1,0:T(8,128)S(1)}, u32[]{:S(2)}, u32[]{:S(2)}) collective-permute-start(f32[1,72,256]{2,1,0:T(8,128)S(1)} %get-tuple-element.14), channel_id=1, source_target_pairs={{0,24},{1,25},{2,26},{3,27},{4,28},{5,29},{6,30},{7,31},{8,16},{9,... | collective-permute-start | bytes 221192 | tf_op jit(solution)/shard_map/ppermute | solution.py:242
  37.3 6.4 %collective-permute-start.5 = (f32[1,72,256]{2,1,0:T(8,128)S(1)}, f32[1,72,256]{2,1,0:T(8,128)S(1)}, u32[]{:S(2)}, u32[]{:S(2)}) collective-permute-start(f32[1,72,256]{2,1,0:T(8,128)S(1)} %get-tuple-element.15), channel_id=1, source_target_pairs={{0,16},{1,17},{2,18},{3,19},{4,20},{5,21},{6,22},{7,23},{8,24},{9,... | collective-permute-start | bytes 221192 | tf_op jit(solution)/shard_map/ppermute | solution.py:242
  43.7 7.1 %collective-permute-start.9 = (f32[1,72,256]{2,1,0:T(8,128)S(1)}, f32[1,72,256]{2,1,0:T(8,128)S(1)}, u32[]{:S(2)}, u32[]{:S(2)}) collective-permute-start(f32[1,72,256]{2,1,0:T(8,128)S(1)} %fusion.9), channel_id=1, source_target_pairs={{0,24},{1,25},{2,26},{3,27},{4,28},{5,29},{6,30},{7,31},{8,16},{9,... | collective-permute-start | bytes 221192 | tf_op jit(solution)/shard_map/ppermute | solution.py:242
  46.2 6.3 %collective-permute-start.8 = (f32[1,72,256]{2,1,0:T(8,128)S(1)}, f32[1,72,256]{2,1,0:T(8,128)S(1)}, u32[]{:S(2)}, u32[]{:S(2)}) collective-permute-start(f32[1,72,256]{2,1,0:T(8,128)S(1)} %fusion.9), channel_id=1, source_target_pairs={{0,16},{1,17},{2,18},{3,19},{4,20},{5,21},{6,22},{7,23},{8,24},{9,... | collective-permute-start | bytes 221192 | tf_op jit(solution)/shard_map/ppermute | solution.py:242
  46.2 6.3 %collective-permute-start.7 = (f32[1,72,256]{2,1,0:T(8,128)S(1)}, f32[1,72,256]{2,1,0:T(8,128)S(1)}, u32[]{:S(2)}, u32[]{:S(2)}) collective-permute-start(f32[1,72,256]{2,1,0:T(8,128)S(1)} %fusion.9), channel_id=1, source_target_pairs={{0,8},{1,9},{2,10},{3,11},{4,12},{5,13},{6,14},{7,15},{8,0},{9,1},... | collective-permute-start | bytes 221192 | tf_op jit(solution)/shard_map/ppermute | solution.py:242
  52.6 11.0 %collective-permute-start.12 = (f32[4,72,256]{2,1,0:T(8,128)S(1)}, f32[4,72,256]{2,1,0:T(8,128)S(1)}, u32[]{:S(2)}, u32[]{:S(2)}) collective-permute-start(f32[4,72,256]{2,1,0:T(8,128)S(1)} %get-tuple-element.12), channel_id=1, source_target_pairs={{0,6},{1,7},{2,4},{3,5},{4,2},{5,3},{6,0},{7,1},{8,14},{9,15},{10,... | collective-permute-start | bytes 884744 | tf_op jit(solution)/shard_map/ppermute | solution.py:242
  54.2 14.1 %collective-permute-start.11 = (f32[4,72,256]{2,1,0:T(8,128)S(1)}, f32[4,72,256]{2,1,0:T(8,128)S(1)}, u32[]{:S(2)}, u32[]{:S(2)}) collective-permute-start(f32[4,72,256]{2,1,0:T(8,128)S(1)} %get-tuple-element.12), channel_id=1, source_target_pairs={{0,4},{1,5},{2,6},{3,7},{4,0},{5,1},{6,2},{7,3},{8,12},{9,13},{10,... | collective-permute-start | bytes 884744 | tf_op jit(solution)/shard_map/ppermute | solution.py:242
  55.6 12.8 %collective-permute-start.10 = (f32[4,72,256]{2,1,0:T(8,128)S(1)}, f32[4,72,256]{2,1,0:T(8,128)S(1)}, u32[]{:S(2)}, u32[]{:S(2)}) collective-permute-start(f32[4,72,256]{2,1,0:T(8,128)S(1)} %get-tuple-element.12), channel_id=1, source_target_pairs={{0,2},{1,3},{2,0},{3,1},{4,6},{5,7},{6,4},{7,5},{8,10},{9,11},{10,... | collective-permute-start | bytes 884744 | tf_op jit(solution)/shard_map/ppermute | solution.py:242
  68.4 2.9 %collective-permute-start.13 = (f32[16,72,256]{2,1,0:T(8,128)S(1)}, f32[16,72,256]{2,1,0:T(8,128)S(1)}, u32[]{:S(2)}, u32[]{:S(2)}) collective-permute-start(f32[16,72,256]{2,1,0:T(8,128)S(1)} %bitcast.77), channel_id=1, source_target_pairs={{0,1},{1,0},{2,3},{3,2},{4,5},{5,4},{6,7},{7,6},{8,9},{9,8},{10,11... | collective-permute-start | bytes 3538952 | tf_op jit(solution)/shard_map/ppermute | solution.py:242

commit v5 on v4

--- a/solution.py
+++ b/solution.py
@@ -161,12 +161,11 @@
 
 
 def packed_rows(blocks):
-    return TILE * len(below_diagonal(blocks)) + HALF * blocks + HALF * blocks // 2
+    return TILE * len(below_diagonal(blocks)) + HALF * blocks
 
 
 def moments_kernel(
-    bounds, me_ref, e_ref, start_ref, out_ref, b_high, b_low,
-    rows_in, start_in, packed, diagonal, sems,
+    bounds, me_ref, e_ref, out_ref, corners, rows_in, packed, diagonal, sems,
 ):
     blocks = e_ref.shape[1] // TILE
     below = below_diagonal(blocks)
@@ -177,7 +176,6 @@
         )
         for index, (first, last) in enumerate(cuts)
     ]
-    loads.append(pltpu.make_async_copy(start_ref, start_in, sems.at[len(cuts)]))
     for load in loads:
         load.start()
     for index, (first, last) in enumerate(cuts):
@@ -192,50 +190,49 @@
             at = slice(place * TILE, (place + 1) * TILE)
             term = dot3(flipped[i], parts[j])
             packed[at, :] = term if index == 0 else packed[at, :] + term
-    loads[-1].wait()
-    b_high[...], b_low[...] = split2(start_in[...])
     lower = TILE * len(below)
-    corner = lower + HALF * blocks
+    row = lax.broadcasted_iota(jnp.int32, (HALF, HALF), 0)
+    col = lax.broadcasted_iota(jnp.int32, (HALF, HALF), 1)
+    corners[...] = jnp.zeros_like(corners)
     for j in range(blocks):
         block = diagonal[j] + diagonal[j].T
-        packed[lower + j * HALF : lower + (j + 1) * HALF, :] = block[HALF:]
-        at = corner + j // 2 * HALF
-        side = j % 2 * HALF
-        packed[at : at + HALF, side : side + HALF] = block[:HALF, :HALF]
+        at = slice(lower + j * HALF, lower + (j + 1) * HALF)
+        packed[at, :HALF] = block[HALF:, :HALF]
+        packed[at, HALF:] = jnp.where(row > col, block[:HALF, :HALF], block[HALF:, HALF:])
+        corners[j : j + 1, :HALF] = jnp.sum(
+            jnp.where(row == col, block[:HALF, :HALF], 0.0), axis=0, keepdims=True
+        )
     pieces, rows, _ = out_ref.shape
     for piece in range(pieces):
         out_ref[piece ^ me_ref[0]] = packed[piece * rows : (piece + 1) * rows, :]
 
 
-def moments(embeddings, start_block, me, pieces):
+def moments(embeddings, me, pieces):
     rows, columns = embeddings.shape
-    width = start_block.shape[1]
     blocks = columns // TILE
     packed = packed_rows(blocks)
     bounds = [0] + [rows // 8 * k for k in (1, 2, 4, 6, 8)]
     shape = (pieces, packed // pieces, TILE)
     steps = len(bounds) - 1
     vmem = pl.BlockSpec(memory_space=pltpu.VMEM)
-    anywhere = pl.BlockSpec(memory_space=pl.ANY)
+    anywhere = pl.BlockSpec(memory_space=pltpu.HBM)
     return pl.pallas_call(
         functools.partial(moments_kernel, bounds),
-        in_specs=[pl.BlockSpec(memory_space=pltpu.SMEM), anywhere, anywhere],
-        out_specs=[vmem, vmem, vmem],
+        in_specs=[pl.BlockSpec(memory_space=pltpu.SMEM), anywhere],
+        out_specs=[vmem] * 2,
         out_shape=[
             jax.ShapeDtypeStruct(shape, jnp.float32),
-            jax.ShapeDtypeStruct((columns, width), jnp.bfloat16),
-            jax.ShapeDtypeStruct((columns, width), jnp.bfloat16),
+            jax.ShapeDtypeStruct((-(-blocks // SUB) * SUB, TILE), jnp.float32),
         ],
         scratch_shapes=[
             pltpu.VMEM((rows, columns), jnp.float32),
-            pltpu.VMEM((columns, width), jnp.float32),
             pltpu.VMEM((packed, TILE), jnp.float32),
             pltpu.VMEM((blocks, TILE, TILE), jnp.float32),
-            pltpu.SemaphoreType.DMA((steps + 1,)),
+            pltpu.SemaphoreType.DMA((steps,)),
         ],
         compiler_params=pltpu.CompilerParams(vmem_limit_bytes=VMEM_LIMIT),
         name="moments",
-    )(me, embeddings, start_block)
+    )(me, embeddings)
 
 
 def exchange(x, flip, devices):
@@ -251,40 +248,54 @@
     return sum(((value >> place) & 1) << bit for place, bit in enumerate(group))
 
 
-def sum_over_devices(x, devices, scattered):
+def pairwise(terms):
+    while len(terms) > 1:
+        terms = [a + b for a, b in zip(terms[::2], terms[1::2])]
+    return terms[0]
+
+
+def sum_over_devices(x, rider, devices, scattered):
     bits = devices.bit_length() - 1
-    pieces, rows, columns = x.shape
+    _, rows, columns = x.shape
+    extra = rider.shape[0]
     for group in phases(scattered):
         size = 1 << len(group)
         x = x.reshape(-1, size, rows, columns)
-        mine = x[:, 0]
-        others = [exchange(x[:, d], spread(d, group), devices) for d in range(1, size)]
-        for other in others:
-            mine = mine + other
-        x = mine
+        count = x.shape[0]
+        mine, riders = x[:, 0], [rider]
+        for d in range(1, size):
+            message = jnp.concatenate([x[:, d].reshape(count * rows, columns), rider], 0)
+            message = exchange(message, spread(d, group), devices)
+            mine = mine + message[:-extra].reshape(count, rows, columns)
+            riders.append(message[-extra:])
+        x, rider = mine, pairwise(riders)
     x = x.reshape(rows, columns)
     for bit in range(scattered, bits):
-        x = x + exchange(x, 1 << bit, devices)
-    x = x[None]
+        message = exchange(jnp.concatenate([x, rider], 0), 1 << bit, devices)
+        x, rider = x + message[:rows], rider + message[rows:]
+    parts = [x[None]]
     for group in reversed(phases(scattered)):
-        size = 1 << len(group)
-        parts = [x] + [exchange(x, spread(d, group), devices) for d in range(1, size)]
         x = jnp.stack(parts, 1).reshape(-1, rows, columns)
-    return x
+        parts = [x] + [exchange(x, spread(d, group), devices) for d in range(1, 1 << len(group))]
+    return parts, rider
 
 
 def iterate_kernel(
-    scale, me_ref, c_ref, b_high, b_low, e_ref, axes_ref, scores_ref,
-    packed, c_high, c_low, work, gram, cross, rows_in, rows_out, sems,
+    scale, halves, me_ref, *refs
 ):
+    c_refs = refs[:halves]
+    corners, b_high, b_low, e_ref, axes_ref, scores_ref = refs[halves : halves + 6]
+    packed, c_high, c_low, work, gram, cross, rows_in, rows_out, sems = refs[halves + 6 :]
     load = pltpu.make_async_copy(e_ref, rows_in, sems.at[0])
     load.start()
     store = pltpu.make_async_copy(rows_out, scores_ref, sems.at[1])
-    pieces, rows, _ = c_ref.shape
+    count, rows, _ = c_refs[0].shape
     columns, width = b_high.shape
     blocks = columns // TILE
-    for piece in range(pieces):
-        packed[piece * rows : (piece + 1) * rows, :] = c_ref[piece ^ me_ref[0]]
+    for part, c_ref in enumerate(c_refs):
+        for index in range(count):
+            piece = (index * halves + part) ^ me_ref[0]
+            packed[pl.ds(pl.multiple_of(piece * rows, SUB), rows), :] = c_ref[index]
 
     def put(i, j, block):
         at_i, at_j = pl.ds(i * TILE, TILE), pl.ds(j * TILE, TILE)
@@ -295,13 +306,16 @@
         put(i, j, block)
         put(j, i, block.T)
     lower = TILE * len(below_diagonal(blocks))
-    corner = lower + HALF * blocks
+    row = lax.broadcasted_iota(jnp.int32, (HALF, HALF), 0)
+    col = lax.broadcasted_iota(jnp.int32, (HALF, HALF), 1)
     for j in range(blocks):
-        bottom = packed[lower + j * HALF : lower + (j + 1) * HALF, :]
-        at = corner + j // 2 * HALF
-        side = j % 2 * HALF
-        top = [packed[at : at + HALF, side : side + HALF], bottom[:, :HALF].T]
-        put(j, j, jnp.concatenate([jnp.concatenate(top, 1), bottom], 0))
+        at = slice(lower + j * HALF, lower + (j + 1) * HALF)
+        quarter, both = packed[at, :HALF], packed[at, HALF:]
+        turned = both.T
+        first = jnp.where(row > col, both, jnp.where(row == col, corners[j : j + 1, :HALF], turned))
+        second = jnp.where(row > col, turned, both)
+        block = [[first, quarter.T], [quarter, second]]
+        put(j, j, jnp.concatenate([jnp.concatenate(halves, 1) for halves in block], 0))
 
     step_rows = rows_out.shape[0] * BLOCK // width
     for index in range(ITERS):
@@ -333,22 +347,22 @@
     store.wait()
 
 
-def iterate(summed, start_parts, embeddings, me, scale):
+def iterate(summed, corners, start_parts, embeddings, me, scale):
     columns, width = start_parts[0].shape
-    pieces, rows, _ = summed.shape
+    pieces, rows, _ = summed[0].shape
     count = embeddings.shape[0]
     vmem = pl.BlockSpec(memory_space=pltpu.VMEM)
-    anywhere = pl.BlockSpec(memory_space=pl.ANY)
+    anywhere = pl.BlockSpec(memory_space=pltpu.HBM)
     return pl.pallas_call(
-        functools.partial(iterate_kernel, scale),
-        in_specs=[pl.BlockSpec(memory_space=pltpu.SMEM)] + [vmem] * 3 + [anywhere],
+        functools.partial(iterate_kernel, scale, len(summed)),
+        in_specs=[pl.BlockSpec(memory_space=pltpu.SMEM)] + [vmem] * (len(summed) + 3) + [anywhere],
         out_specs=[vmem, anywhere],
         out_shape=[
             jax.ShapeDtypeStruct((columns, width), jnp.float32),
             jax.ShapeDtypeStruct((count, width), jnp.float32),
         ],
         scratch_shapes=[
-            pltpu.VMEM((pieces * rows, TILE), jnp.float32),
+            pltpu.VMEM((len(summed) * pieces * rows, TILE), jnp.float32),
             pltpu.VMEM((columns, columns), jnp.bfloat16),
             pltpu.VMEM((columns, columns), jnp.bfloat16),
             pltpu.VMEM((columns, width), jnp.float32),
@@ -360,7 +374,7 @@
         ],
         compiler_params=pltpu.CompilerParams(vmem_limit_bytes=VMEM_LIMIT),
         name="iterate",
-    )(me, summed, *start_parts, embeddings)
+    )(me, *summed, corners, *start_parts, embeddings)
 
 
 def body(embeddings, start_block):
@@ -371,10 +385,13 @@
     scattered = min(bits, ((packed // 8) & -(packed // 8)).bit_length() - 1)
     pieces = 1 << scattered
     me = (lax.axis_index("dp") % pieces).astype(jnp.int32).reshape(1)
-    local, b_high, b_low = moments(embeddings, start_block, me, pieces)
-    summed = sum_over_devices(local, devices, scattered)
+    local, corners = moments(embeddings, me, pieces)
+    summed, corners = sum_over_devices(local, corners, devices, scattered)
+    start, corners = lax.optimization_barrier((start_block, corners))
+    high = lax.reduce_precision(start, 8, 7)
+    start_parts = (high.astype(jnp.bfloat16), (start - high).astype(jnp.bfloat16))
     scale = math.sqrt(rows * devices)
-    axes, scores = iterate(summed, (b_high, b_low), embeddings, me, scale)
+    axes, scores = iterate(summed, corners, start_parts, embeddings, me, scale)
     return axes, scores
 
 

time: 107 us -> 98.7 us (0.922)
  waiting for transfers between devices: 41.7 us -> 33.2 us
    ppermute x14, waiting for transfers between devices: 41.7 us -> 33.2 us  [exchange(): return lax.ppermute(x, 'dp', [(d, d ^ flip) for d in range(devices)])]
  transfers between devices with their start and end apart: 14 -> 14, of which waited for: 12 -> 11; matrix products, arithmetic and copies ran while one was open for 0% -> 0% of each run, Pallas kernels for 0% -> 0%
where the time goes in v5:
time: 98.7 us; the launch traced here: 98.6 us
  Pallas kernels  44.6 us (45%)
  waiting for transfers between devices  33.2 us (34%)
  starting transfers between devices  17.5 us (18%)
  local copies, waits for them, and re-layouts  1.53 us (2%)
  between operations  0.99 us (1%)
    pallas_call x1, Pallas kernels, iterate(): pl.pallas_call(functools.partial(iterate_kernel, scale, len(summed)), in_...  35.4 us
    ppermute x14, waiting for transfers between devices, exchange(): return lax.ppermute(x, 'dp', [(d, d ^ flip) for d in range(devices)])  33.2 us
    ppermute x14, starting transfers between devices, exchange(): return lax.ppermute(x, 'dp', [(d, d ^ flip) for d in range(devices)])  17.5 us
    pallas_call x1, Pallas kernels, moments(): pl.pallas_call(functools.partial(moments_kernel, bounds), in_specs=[pl.Bl...  9.28 us
  transfers between devices with their start and end apart: 14, of which 11 were waited for; matrix products, arithmetic and copies ran while one was open for 0% of the time, Pallas kernels for 0%

profile of v5, /device:TPU:0, one launch (start us, length us, event | category | flops | bytes accessed | tf_op | source)
XLA Modules:
  0.0 98.6 jit_solution(4809887714881589230)
XLA Ops:
  0.6 9.3 %moments.1 = (f32[32,64,256]{2,1,0:T(8,128)S(1)}, f32[8,256]{1,0:T(8,128)S(1)}) custom-call(s32[1]{0:T(128)} %bitcast.me_ref, f32[2048,1024]{1,0:T(8,128)} %refs_5_.1), custom_call_target="tpu_custom_call" | custom-call | tf_op jit(solution)/shard_map/moments/pallas_call | solution.py:219
  9.9 0.2 fusion.8
  10.2 0.1 pad_maximum_fusion
  10.2 0.5 collective-permute-start
  10.7 2.3 %collective-permute-done = f32[1032,256]{1,0:T(8,128)S(1)} collective-permute-done((f32[1032,256]{1,0:T(8,128)S(1)}, f32[1032,256]{1,0:T(8,128)S(1)}, u32[]{:S(2)}, u32[]{:S(2)}) %collective-permute-start) | collective-permute-done | bytes 1056800 | tf_op jit(solution)/shard_map/ppermute | solution.py:239
  13.1 0.1 copy_add_fusion
  13.4 2.9 %collective-permute-start.1 = (f32[264,256]{1,0:T(8,128)S(1)}, f32[264,256]{1,0:T(8,128)S(1)}, u32[]{:S(2)}, u32[]{:S(2)}) collective-permute-start(f32[264,256]{1,0:T(8,128)S(1)} %get-tuple-element.25), channel_id=1, source_target_pairs={{0,2},{1,3},{2,0},{3,1},{4,6},{5,7},{6,4},{7,5},{8,10},{9,11},{10,... | collective-permute-start | bytes 811016 | tf_op jit(solution)/shard_map/ppermute | solution.py:239
  16.3 1.5 %collective-permute-start.2 = (f32[264,256]{1,0:T(8,128)S(1)}, f32[264,256]{1,0:T(8,128)S(1)}, u32[]{:S(2)}, u32[]{:S(2)}) collective-permute-start(f32[264,256]{1,0:T(8,128)S(1)} %get-tuple-element.26), channel_id=1, source_target_pairs={{0,4},{1,5},{2,6},{3,7},{4,0},{5,1},{6,2},{7,3},{8,12},{9,13},{10,... | collective-permute-start | bytes 811016 | tf_op jit(solution)/shard_map/ppermute | solution.py:239
  17.9 5.7 %collective-permute-done.1 = f32[264,256]{1,0:T(8,128)S(1)} collective-permute-done((f32[264,256]{1,0:T(8,128)S(1)}, f32[264,256]{1,0:T(8,128)S(1)}, u32[]{:S(2)}, u32[]{:S(2)}) %collective-permute-start.1) | collective-permute-done | bytes 270368 | tf_op jit(solution)/shard_map/ppermute | solution.py:239
  23.6 6.7 %collective-permute-done.2 = f32[264,256]{1,0:T(8,128)S(1)} collective-permute-done((f32[264,256]{1,0:T(8,128)S(1)}, f32[264,256]{1,0:T(8,128)S(1)}, u32[]{:S(2)}, u32[]{:S(2)}) %collective-permute-start.2) | collective-permute-done | bytes 270368 | tf_op jit(solution)/shard_map/ppermute | solution.py:239
  30.4 0.1 fusion.3
  30.6 1.6 %collective-permute-start.4 = (f32[72,256]{1,0:T(8,128)S(1)}, f32[72,256]{1,0:T(8,128)S(1)}, u32[]{:S(2)}, u32[]{:S(2)}) collective-permute-start(f32[72,256]{1,0:T(8,128)S(1)} %get-tuple-element.22), channel_id=1, source_target_pairs={{0,8},{1,9},{2,10},{3,11},{4,12},{5,13},{6,14},{7,15},{8,0},{9,1},... | collective-permute-start | bytes 221192 | tf_op jit(solution)/shard_map/ppermute | solution.py:239
  32.2 2.6 %collective-permute-start.5 = (f32[72,256]{1,0:T(8,128)S(1)}, f32[72,256]{1,0:T(8,128)S(1)}, u32[]{:S(2)}, u32[]{:S(2)}) collective-permute-start(f32[72,256]{1,0:T(8,128)S(1)} %get-tuple-element.23), channel_id=1, source_target_pairs={{0,16},{1,17},{2,18},{3,19},{4,20},{5,21},{6,22},{7,23},{8,24},{9,... | collective-permute-start | bytes 221192 | tf_op jit(solution)/shard_map/ppermute | solution.py:239
  34.8 0.2 collective-permute-start.6
  35.0 0.7 collective-permute-done.4
  35.7 3.5 %collective-permute-done.5 = f32[72,256]{1,0:T(8,128)S(1)} collective-permute-done((f32[72,256]{1,0:T(8,128)S(1)}, f32[72,256]{1,0:T(8,128)S(1)}, u32[]{:S(2)}, u32[]{:S(2)}) %collective-permute-start.5) | collective-permute-done | bytes 73760 | tf_op jit(solution)/shard_map/ppermute | solution.py:239
  39.2 1.7 %collective-permute-done.6 = f32[72,256]{1,0:T(8,128)S(1)} collective-permute-done((f32[72,256]{1,0:T(8,128)S(1)}, f32[72,256]{1,0:T(8,128)S(1)}, u32[]{:S(2)}, u32[]{:S(2)}) %collective-permute-start.6) | collective-permute-done | bytes 73760 | tf_op jit(solution)/shard_map/ppermute | solution.py:239
  41.0 1.6 %collective-permute-start.9 = (f32[1,64,256]{2,1,0:T(8,128)S(1)}, f32[1,64,256]{2,1,0:T(8,128)S(1)}, u32[]{:S(2)}, u32[]{:S(2)}) collective-permute-start(f32[1,64,256]{2,1,0:T(8,128)S(1)} %bitcast.62), channel_id=1, source_target_pairs={{0,24},{1,25},{2,26},{3,27},{4,28},{5,29},{6,30},{7,31},{8,16},{9,... | collective-permute-start | bytes 196616 | tf_op jit(solution)/shard_map/ppermute | solution.py:239
  42.6 2.8 %collective-permute-start.7 = (f32[1,64,256]{2,1,0:T(8,128)S(1)}, f32[1,64,256]{2,1,0:T(8,128)S(1)}, u32[]{:S(2)}, u32[]{:S(2)}) collective-permute-start(f32[1,64,256]{2,1,0:T(8,128)S(1)} %bitcast.64), channel_id=1, source_target_pairs={{0,8},{1,9},{2,10},{3,11},{4,12},{5,13},{6,14},{7,15},{8,0},{9,1},... | collective-permute-start | bytes 196616 | tf_op jit(solution)/shard_map/ppermute | solution.py:239
  45.4 1.7 %collective-permute-done.9 = f32[1,64,256]{2,1,0:T(8,128)S(1)} collective-permute-done((f32[1,64,256]{2,1,0:T(8,128)S(1)}, f32[1,64,256]{2,1,0:T(8,128)S(1)}, u32[]{:S(2)}, u32[]{:S(2)}) %collective-permute-start.9) | collective-permute-done | bytes 65568 | tf_op jit(solution)/shard_map/ppermute | solution.py:239
  47.1 1.4 %collective-permute-done.8 = f32[1,64,256]{2,1,0:T(8,128)S(1)} collective-permute-done((f32[1,64,256]{2,1,0:T(8,128)S(1)}, f32[1,64,256]{2,1,0:T(8,128)S(1)}, u32[]{:S(2)}, u32[]{:S(2)}) %collective-permute-start.8) | collective-permute-done | bytes 65568 | tf_op jit(solution)/shard_map/ppermute | solution.py:239
  48.6 1.7 %collective-permute-start.12 = (f32[4,64,256]{2,1,0:T(8,128)S(1)}, f32[4,64,256]{2,1,0:T(8,128)S(1)}, u32[]{:S(2)}, u32[]{:S(2)}) collective-permute-start(f32[4,64,256]{2,1,0:T(8,128)S(1)} %get-tuple-element.18), channel_id=1, source_target_pairs={{0,6},{1,7},{2,4},{3,5},{4,2},{5,3},{6,0},{7,1},{8,14},{9,15},{10,... | collective-permute-start | bytes 786440 | tf_op jit(solution)/shard_map/ppermute | solution.py:239
  50.2 1.2 %collective-permute-start.11 = (f32[4,64,256]{2,1,0:T(8,128)S(1)}, f32[4,64,256]{2,1,0:T(8,128)S(1)}, u32[]{:S(2)}, u32[]{:S(2)}) collective-permute-start(f32[4,64,256]{2,1,0:T(8,128)S(1)} %get-tuple-element.18), channel_id=1, source_target_pairs={{0,4},{1,5},{2,6},{3,7},{4,0},{5,1},{6,2},{7,3},{8,12},{9,13},{10,... | collective-permute-start | bytes 786440 | tf_op jit(solution)/shard_map/ppermute | solution.py:239
  51.4 0.7 collective-permute-start.10
  52.1 5.4 %collective-permute-done.12 = f32[4,64,256]{2,1,0:T(8,128)S(1)} collective-permute-done((f32[4,64,256]{2,1,0:T(8,128)S(1)}, f32[4,64,256]{2,1,0:T(8,128)S(1)}, u32[]{:S(2)}, u32[]{:S(2)}) %collective-permute-start.12) | collective-permute-done | bytes 262176 | tf_op jit(solution)/shard_map/ppermute | solution.py:239
  57.5 2.7 %collective-permute-done.11 = f32[4,64,256]{2,1,0:T(8,128)S(1)} collective-permute-done((f32[4,64,256]{2,1,0:T(8,128)S(1)}, f32[4,64,256]{2,1,0:T(8,128)S(1)}, u32[]{:S(2)}, u32[]{:S(2)}) %collective-permute-start.11) | collective-permute-done | bytes 262176 | tf_op jit(solution)/shard_map/ppermute | solution.py:239
  60.1 0.1 pad_maximum_fusion.1
  60.3 0.1 collective-permute-start.13
  60.4 1.0 %copy-done = f32[1024,256]{1,0:T(8,128)S(1)} copy-done((f32[1024,256]{1,0:T(8,128)S(1)}, f32[1024,256]{1,0:T(8,128)}, u32[]{:S(2)}) %copy-start) | copy-done | bytes 1048600
  61.5 0.2 fusion
  61.6 1.4 %collective-permute-done.13.refs_1_ = f32[16,64,256]{2,1,0:T(8,128)S(1)} collective-permute-done((f32[16,64,256]{2,1,0:T(8,128)S(1)}, f32[16,64,256]{2,1,0:T(8,128)S(1)}, u32[]{:S(2)}, u32[]{:S(2)}) %collective-permute-start.13) | collective-permute-done | bytes 1048608 | tf_op jit(solution)/shard_map/ppermute | solution.py:239
  63.1 35.4 %iterate.1 = (f32[1024,256]{1,0:T(8,128)}, f32[2048,256]{1,0:T(8,128)}) custom-call(s32[1]{0:T(128)} %bitcast.me_ref, f32[16,64,256]{2,1,0:T(8,128)S(1)} %bitcast.51, f32[16,64,256]{2,1,0:T(8,128)S(1)} %collective-permute-done.13.refs_1_, f32[8,256]{1,0:T(8,128)S(1)} %fusion.6.refs_2_, bf16[1024,256]{1,0:T(8,128)(2,1)S(1)} %get-tuple-element.13.refs_3_, ...), custom_call_target="tpu_custom_call" | custom-call | tf_op jit(solution)/shard_map/iterate/pallas_call | solution.py:356
  (20 shorter events, 0.5 us)
Async XLA Ops:
  10.2 2.8 %collective-permute-start = (f32[1032,256]{1,0:T(8,128)S(1)}, f32[1032,256]{1,0:T(8,128)S(1)}, u32[]{:S(2)}, u32[]{:S(2)}) collective-permute-start(f32[1032,256]{1,0:T(8,128)S(1)} %pad_maximum_fusion), channel_id=1, source_target_pairs={{0,1},{1,0},{2,3},{3,2},{4,5},{5,4},{6,7},{7,6},{8,9},{9,8},{10,11... | collective-permute-start | bytes 3170312 | tf_op jit(solution)/shard_map/ppermute | solution.py:239
  13.4 10.2 %collective-permute-start.1 = (f32[264,256]{1,0:T(8,128)S(1)}, f32[264,256]{1,0:T(8,128)S(1)}, u32[]{:S(2)}, u32[]{:S(2)}) collective-permute-start(f32[264,256]{1,0:T(8,128)S(1)} %get-tuple-element.25), channel_id=1, source_target_pairs={{0,2},{1,3},{2,0},{3,1},{4,6},{5,7},{6,4},{7,5},{8,10},{9,11},{10,... | collective-permute-start | bytes 811016 | tf_op jit(solution)/shard_map/ppermute | solution.py:239
  16.3 14.0 %collective-permute-start.2 = (f32[264,256]{1,0:T(8,128)S(1)}, f32[264,256]{1,0:T(8,128)S(1)}, u32[]{:S(2)}, u32[]{:S(2)}) collective-permute-start(f32[264,256]{1,0:T(8,128)S(1)} %get-tuple-element.26), channel_id=1, source_target_pairs={{0,4},{1,5},{2,6},{3,7},{4,0},{5,1},{6,2},{7,3},{8,12},{9,13},{10,... | collective-permute-start | bytes 811016 | tf_op jit(solution)/shard_map/ppermute | solution.py:239
  17.9 12.5 %collective-permute-start.3 = (f32[264,256]{1,0:T(8,128)S(1)}, f32[264,256]{1,0:T(8,128)S(1)}, u32[]{:S(2)}, u32[]{:S(2)}) collective-permute-start(f32[264,256]{1,0:T(8,128)S(1)} %get-tuple-element.27), channel_id=1, source_target_pairs={{0,6},{1,7},{2,4},{3,5},{4,2},{5,3},{6,0},{7,1},{8,14},{9,15},{10,... | collective-permute-start | bytes 811016 | tf_op jit(solution)/shard_map/ppermute | solution.py:239
  30.6 5.2 %collective-permute-start.4 = (f32[72,256]{1,0:T(8,128)S(1)}, f32[72,256]{1,0:T(8,128)S(1)}, u32[]{:S(2)}, u32[]{:S(2)}) collective-permute-start(f32[72,256]{1,0:T(8,128)S(1)} %get-tuple-element.22), channel_id=1, source_target_pairs={{0,8},{1,9},{2,10},{3,11},{4,12},{5,13},{6,14},{7,15},{8,0},{9,1},... | collective-permute-start | bytes 221192 | tf_op jit(solution)/shard_map/ppermute | solution.py:239
  32.2 7.0 %collective-permute-start.5 = (f32[72,256]{1,0:T(8,128)S(1)}, f32[72,256]{1,0:T(8,128)S(1)}, u32[]{:S(2)}, u32[]{:S(2)}) collective-permute-start(f32[72,256]{1,0:T(8,128)S(1)} %get-tuple-element.23), channel_id=1, source_target_pairs={{0,16},{1,17},{2,18},{3,19},{4,20},{5,21},{6,22},{7,23},{8,24},{9,... | collective-permute-start | bytes 221192 | tf_op jit(solution)/shard_map/ppermute | solution.py:239
  34.8 6.2 %collective-permute-start.6 = (f32[72,256]{1,0:T(8,128)S(1)}, f32[72,256]{1,0:T(8,128)S(1)}, u32[]{:S(2)}, u32[]{:S(2)}) collective-permute-start(f32[72,256]{1,0:T(8,128)S(1)} %get-tuple-element.24), channel_id=1, source_target_pairs={{0,24},{1,25},{2,26},{3,27},{4,28},{5,29},{6,30},{7,31},{8,16},{9,... | collective-permute-start | bytes 221192 | tf_op jit(solution)/shard_map/ppermute | solution.py:239
  41.0 6.1 %collective-permute-start.9 = (f32[1,64,256]{2,1,0:T(8,128)S(1)}, f32[1,64,256]{2,1,0:T(8,128)S(1)}, u32[]{:S(2)}, u32[]{:S(2)}) collective-permute-start(f32[1,64,256]{2,1,0:T(8,128)S(1)} %bitcast.62), channel_id=1, source_target_pairs={{0,24},{1,25},{2,26},{3,27},{4,28},{5,29},{6,30},{7,31},{8,16},{9,... | collective-permute-start | bytes 196616 | tf_op jit(solution)/shard_map/ppermute | solution.py:239
  42.6 5.9 %collective-permute-start.8 = (f32[1,64,256]{2,1,0:T(8,128)S(1)}, f32[1,64,256]{2,1,0:T(8,128)S(1)}, u32[]{:S(2)}, u32[]{:S(2)}) collective-permute-start(f32[1,64,256]{2,1,0:T(8,128)S(1)} %bitcast.63), channel_id=1, source_target_pairs={{0,16},{1,17},{2,18},{3,19},{4,20},{5,21},{6,22},{7,23},{8,24},{9,... | collective-permute-start | bytes 196616 | tf_op jit(solution)/shard_map/ppermute | solution.py:239
  42.6 5.9 %collective-permute-start.7 = (f32[1,64,256]{2,1,0:T(8,128)S(1)}, f32[1,64,256]{2,1,0:T(8,128)S(1)}, u32[]{:S(2)}, u32[]{:S(2)}) collective-permute-start(f32[1,64,256]{2,1,0:T(8,128)S(1)} %bitcast.64), channel_id=1, source_target_pairs={{0,8},{1,9},{2,10},{3,11},{4,12},{5,13},{6,14},{7,15},{8,0},{9,1},... | collective-permute-start | bytes 196616 | tf_op jit(solution)/shard_map/ppermute | solution.py:239
  48.6 8.9 %collective-permute-start.12 = (f32[4,64,256]{2,1,0:T(8,128)S(1)}, f32[4,64,256]{2,1,0:T(8,128)S(1)}, u32[]{:S(2)}, u32[]{:S(2)}) collective-permute-start(f32[4,64,256]{2,1,0:T(8,128)S(1)} %get-tuple-element.18), channel_id=1, source_target_pairs={{0,6},{1,7},{2,4},{3,5},{4,2},{5,3},{6,0},{7,1},{8,14},{9,15},{10,... | collective-permute-start | bytes 786440 | tf_op jit(solution)/shard_map/ppermute | solution.py:239
  50.2 9.9 %collective-permute-start.11 = (f32[4,64,256]{2,1,0:T(8,128)S(1)}, f32[4,64,256]{2,1,0:T(8,128)S(1)}, u32[]{:S(2)}, u32[]{:S(2)}) collective-permute-start(f32[4,64,256]{2,1,0:T(8,128)S(1)} %get-tuple-element.18), channel_id=1, source_target_pairs={{0,4},{1,5},{2,6},{3,7},{4,0},{5,1},{6,2},{7,3},{8,12},{9,13},{10,... | collective-permute-start | bytes 786440 | tf_op jit(solution)/shard_map/ppermute | solution.py:239
  51.4 8.8 %collective-permute-start.10 = (f32[4,64,256]{2,1,0:T(8,128)S(1)}, f32[4,64,256]{2,1,0:T(8,128)S(1)}, u32[]{:S(2)}, u32[]{:S(2)}) collective-permute-start(f32[4,64,256]{2,1,0:T(8,128)S(1)} %get-tuple-element.18), channel_id=1, source_target_pairs={{0,2},{1,3},{2,0},{3,1},{4,6},{5,7},{6,4},{7,5},{8,10},{9,11},{10,... | collective-permute-start | bytes 786440 | tf_op jit(solution)/shard_map/ppermute | solution.py:239
  60.2 1.2 %copy-start = (f32[1024,256]{1,0:T(8,128)S(1)}, f32[1024,256]{1,0:T(8,128)}, u32[]{:S(2)}) copy-start(f32[1024,256]{1,0:T(8,128)} %param.3) | copy-start | bytes 3145732
  60.3 2.7 %collective-permute-start.13 = (f32[16,64,256]{2,1,0:T(8,128)S(1)}, f32[16,64,256]{2,1,0:T(8,128)S(1)}, u32[]{:S(2)}, u32[]{:S(2)}) collective-permute-start(f32[16,64,256]{2,1,0:T(8,128)S(1)} %bitcast.50), channel_id=1, source_target_pairs={{0,1},{1,0},{2,3},{3,2},{4,5},{5,4},{6,7},{7,6},{8,9},{9,8},{10,11... | collective-permute-start | bytes 3145736 | tf_op jit(solution)/shard_map/ppermute | solution.py:239

commit v6 on v5

--- a/solution.py
+++ b/solution.py
@@ -165,7 +165,7 @@
 
 
 def moments_kernel(
-    bounds, me_ref, e_ref, out_ref, corners, rows_in, packed, diagonal, sems,
+    bounds, me_ref, e_ref, keep, send, corners, rows_in, packed, diagonal, sems,
 ):
     blocks = e_ref.shape[1] // TILE
     below = below_diagonal(blocks)
@@ -202,9 +202,16 @@
         corners[j : j + 1, :HALF] = jnp.sum(
             jnp.where(row == col, block[:HALF, :HALF], 0.0), axis=0, keepdims=True
         )
-    pieces, rows, _ = out_ref.shape
-    for piece in range(pieces):
-        out_ref[piece ^ me_ref[0]] = packed[piece * rows : (piece + 1) * rows, :]
+    count, rows, _ = keep.shape
+
+    def piece(position):
+        start = pl.multiple_of((position ^ me_ref[0]) * rows, SUB)
+        return packed[pl.ds(start, rows), :]
+
+    for index in range(count):
+        keep[index] = piece(2 * index)
+        send[index * rows : (index + 1) * rows, :] = piece(2 * index + 1)
+    send[count * rows :, :] = corners[...]
 
 
 def moments(embeddings, me, pieces):
@@ -212,17 +219,18 @@
     blocks = columns // TILE
     packed = packed_rows(blocks)
     bounds = [0] + [rows // 8 * k for k in (1, 2, 4, 6, 8)]
-    shape = (pieces, packed // pieces, TILE)
+    extra = -(-blocks // SUB) * SUB
     steps = len(bounds) - 1
     vmem = pl.BlockSpec(memory_space=pltpu.VMEM)
     anywhere = pl.BlockSpec(memory_space=pltpu.HBM)
     return pl.pallas_call(
         functools.partial(moments_kernel, bounds),
         in_specs=[pl.BlockSpec(memory_space=pltpu.SMEM), anywhere],
-        out_specs=[vmem] * 2,
+        out_specs=[vmem] * 3,
         out_shape=[
-            jax.ShapeDtypeStruct(shape, jnp.float32),
-            jax.ShapeDtypeStruct((-(-blocks // SUB) * SUB, TILE), jnp.float32),
+            jax.ShapeDtypeStruct((pieces // 2, packed // pieces, TILE), jnp.float32),
+            jax.ShapeDtypeStruct((packed // 2 + extra, TILE), jnp.float32),
+            jax.ShapeDtypeStruct((extra, TILE), jnp.float32),
         ],
         scratch_shapes=[
             pltpu.VMEM((rows, columns), jnp.float32),
@@ -254,20 +262,23 @@
     return terms[0]
 
 
-def sum_over_devices(x, rider, devices, scattered):
+def sum_over_devices(keep, send, rider, devices, scattered):
     bits = devices.bit_length() - 1
-    _, rows, columns = x.shape
+    _, rows, columns = keep.shape
     extra = rider.shape[0]
-    for group in phases(scattered):
+    message = exchange(send, 1, devices)
+    x = keep + message[:-extra].reshape(keep.shape)
+    rider = rider + message[-extra:]
+    for group in phases(scattered)[1:]:
         size = 1 << len(group)
         x = x.reshape(-1, size, rows, columns)
         count = x.shape[0]
-        mine, riders = x[:, 0], [rider]
-        for d in range(1, size):
+        mine, riders = x[:, 0], [rider] * size
+        for d in reversed(range(1, size)):
             message = jnp.concatenate([x[:, d].reshape(count * rows, columns), rider], 0)
             message = exchange(message, spread(d, group), devices)
             mine = mine + message[:-extra].reshape(count, rows, columns)
-            riders.append(message[-extra:])
+            riders[d] = message[-extra:]
         x, rider = mine, pairwise(riders)
     x = x.reshape(rows, columns)
     for bit in range(scattered, bits):
@@ -288,7 +299,7 @@
     packed, c_high, c_low, work, gram, cross, rows_in, rows_out, sems = refs[halves + 6 :]
     load = pltpu.make_async_copy(e_ref, rows_in, sems.at[0])
     load.start()
-    store = pltpu.make_async_copy(rows_out, scores_ref, sems.at[1])
+    stores = []
     count, rows, _ = c_refs[0].shape
     columns, width = b_high.shape
     blocks = columns // TILE
@@ -338,13 +349,17 @@
             def beside(step):
                 at = slice(step * step_rows, (step + 1) * step_rows)
                 rows_out[at, :] = dot3(split2(rows_in[at, :]), weights)
+                store = pltpu.make_async_copy(
+                    rows_out.at[at, :], scores_ref.at[at, :], sems.at[1 + step]
+                )
+                store.start()
+                stores.append(store)
 
             invert_factor(cross, beside)
-        if index == ITERS - 1:
-            store.start()
         basis = tall3(summed, split2(cross[...]), (1, 1))
     axes_ref[...] = basis * math.sqrt(columns)
-    store.wait()
+    for store in stores:
+        store.wait()
 
 
 def iterate(summed, corners, start_parts, embeddings, me, scale):
@@ -370,7 +385,7 @@
             pltpu.VMEM((width, width), jnp.float32),
             pltpu.VMEM((count, columns), jnp.float32),
             pltpu.VMEM((count, width), jnp.float32),
-            pltpu.SemaphoreType.DMA((2,)),
+            pltpu.SemaphoreType.DMA((1 + width // BLOCK,)),
         ],
         compiler_params=pltpu.CompilerParams(vmem_limit_bytes=VMEM_LIMIT),
         name="iterate",
@@ -385,8 +400,8 @@
     scattered = min(bits, ((packed // 8) & -(packed // 8)).bit_length() - 1)
     pieces = 1 << scattered
     me = (lax.axis_index("dp") % pieces).astype(jnp.int32).reshape(1)
-    local, corners = moments(embeddings, me, pieces)
-    summed, corners = sum_over_devices(local, corners, devices, scattered)
+    keep, send, corners = moments(embeddings, me, pieces)
+    summed, corners = sum_over_devices(keep, send, corners, devices, scattered)
     start, corners = lax.optimization_barrier((start_block, corners))
     high = lax.reduce_precision(start, 8, 7)
     start_parts = (high.astype(jnp.bfloat16), (start - high).astype(jnp.bfloat16))

time: 98.7 us -> 98 us (level)
  no operation moved by 1% of the time
where the time goes in v6:
time: 98 us; the launch traced here: 97.9 us
  Pallas kernels  44.3 us (45%)
  waiting for transfers between devices  33.2 us (34%)
  starting transfers between devices  17.5 us (18%)
  local copies, waits for them, and re-layouts  1.31 us (1%)
  between operations  0.98 us (1%)
    pallas_call x1, Pallas kernels, iterate(): pl.pallas_call(functools.partial(iterate_kernel, scale, len(summed)), in_...  34.9 us
    ppermute x14, waiting for transfers between devices, exchange(): return lax.ppermute(x, 'dp', [(d, d ^ flip) for d in range(devices)])  33.2 us
    ppermute x14, starting transfers between devices, exchange(): return lax.ppermute(x, 'dp', [(d, d ^ flip) for d in range(devices)])  17.5 us
    pallas_call x1, Pallas kernels, moments(): pl.pallas_call(functools.partial(moments_kernel, bounds), in_specs=[pl.Bl...  9.36 us
  transfers between devices with their start and end apart: 14, of which 11 were waited for; matrix products, arithmetic and copies ran while one was open for 0% of the time, Pallas kernels for 0%

profile of v6, /device:TPU:0, one launch (start us, length us, event | category | flops | bytes accessed | tf_op | source)
XLA Modules:
  0.0 97.9 jit_solution(18004442216636550733)
XLA Ops:
  0.6 9.4 %moments.1 = (f32[16,64,256]{2,1,0:T(8,128)S(1)}, f32[1032,256]{1,0:T(8,128)S(1)}, f32[8,256]{1,0:T(8,128)S(1)}) custom-call(s32[1]{0:T(128)} %bitcast.me_ref, f32[2048,1024]{1,0:T(8,128)} %refs_5_.1), custom_call_target="tpu_custom_call" | custom-call | tf_op jit(solution)/shard_map/moments/pallas_call | solution.py:226
  10.0 0.5 collective-permute-start
  10.5 2.3 %collective-permute-done = f32[1032,256]{1,0:T(8,128)S(1)} collective-permute-done((f32[1032,256]{1,0:T(8,128)S(1)}, f32[1032,256]{1,0:T(8,128)S(1)}, u32[]{:S(2)}, u32[]{:S(2)}) %collective-permute-start) | collective-permute-done | bytes 1056800 | tf_op jit(solution)/shard_map/ppermute | solution.py:247
  12.8 0.1 slice.88
  12.9 0.1 add.73
  13.1 0.1 pad_maximum_fusion.1
  13.2 2.9 %collective-permute-start.3 = (f32[264,256]{1,0:T(8,128)S(1)}, f32[264,256]{1,0:T(8,128)S(1)}, u32[]{:S(2)}, u32[]{:S(2)}) collective-permute-start(f32[264,256]{1,0:T(8,128)S(1)} %get-tuple-element.25), channel_id=1, source_target_pairs={{0,2},{1,3},{2,0},{3,1},{4,6},{5,7},{6,4},{7,5},{8,10},{9,11},{10,... | collective-permute-start | bytes 811016 | tf_op jit(solution)/shard_map/ppermute | solution.py:247
  16.1 1.5 %collective-permute-start.2 = (f32[264,256]{1,0:T(8,128)S(1)}, f32[264,256]{1,0:T(8,128)S(1)}, u32[]{:S(2)}, u32[]{:S(2)}) collective-permute-start(f32[264,256]{1,0:T(8,128)S(1)} %get-tuple-element.26), channel_id=1, source_target_pairs={{0,4},{1,5},{2,6},{3,7},{4,0},{5,1},{6,2},{7,3},{8,12},{9,13},{10,... | collective-permute-start | bytes 811016 | tf_op jit(solution)/shard_map/ppermute | solution.py:247
  17.7 5.7 %collective-permute-done.3 = f32[264,256]{1,0:T(8,128)S(1)} collective-permute-done((f32[264,256]{1,0:T(8,128)S(1)}, f32[264,256]{1,0:T(8,128)S(1)}, u32[]{:S(2)}, u32[]{:S(2)}) %collective-permute-start.3) | collective-permute-done | bytes 270368 | tf_op jit(solution)/shard_map/ppermute | solution.py:247
  23.4 6.7 %collective-permute-done.2 = f32[264,256]{1,0:T(8,128)S(1)} collective-permute-done((f32[264,256]{1,0:T(8,128)S(1)}, f32[264,256]{1,0:T(8,128)S(1)}, u32[]{:S(2)}, u32[]{:S(2)}) %collective-permute-start.2) | collective-permute-done | bytes 270368 | tf_op jit(solution)/shard_map/ppermute | solution.py:247
  30.2 0.1 fusion.3
  30.3 3.7 %collective-permute-start.4 = (f32[72,256]{1,0:T(8,128)S(1)}, f32[72,256]{1,0:T(8,128)S(1)}, u32[]{:S(2)}, u32[]{:S(2)}) collective-permute-start(f32[72,256]{1,0:T(8,128)S(1)} %get-tuple-element.22), channel_id=1, source_target_pairs={{0,24},{1,25},{2,26},{3,27},{4,28},{5,29},{6,30},{7,31},{8,16},{9,... | collective-permute-start | bytes 221192 | tf_op jit(solution)/shard_map/ppermute | solution.py:247
  34.0 0.8 collective-permute-start.6
  34.8 2.2 %collective-permute-done.4 = f32[72,256]{1,0:T(8,128)S(1)} collective-permute-done((f32[72,256]{1,0:T(8,128)S(1)}, f32[72,256]{1,0:T(8,128)S(1)}, u32[]{:S(2)}, u32[]{:S(2)}) %collective-permute-start.4) | collective-permute-done | bytes 73760 | tf_op jit(solution)/shard_map/ppermute | solution.py:247
  37.0 2.8 %collective-permute-done.5 = f32[72,256]{1,0:T(8,128)S(1)} collective-permute-done((f32[72,256]{1,0:T(8,128)S(1)}, f32[72,256]{1,0:T(8,128)S(1)}, u32[]{:S(2)}, u32[]{:S(2)}) %collective-permute-start.5) | collective-permute-done | bytes 73760 | tf_op jit(solution)/shard_map/ppermute | solution.py:247
  39.8 2.5 %collective-permute-start.9 = (f32[1,64,256]{2,1,0:T(8,128)S(1)}, f32[1,64,256]{2,1,0:T(8,128)S(1)}, u32[]{:S(2)}, u32[]{:S(2)}) collective-permute-start(f32[1,64,256]{2,1,0:T(8,128)S(1)} %bitcast.53), channel_id=1, source_target_pairs={{0,24},{1,25},{2,26},{3,27},{4,28},{5,29},{6,30},{7,31},{8,16},{9,... | collective-permute-start | bytes 196616 | tf_op jit(solution)/shard_map/ppermute | solution.py:247
  42.3 1.9 %collective-permute-start.7 = (f32[1,64,256]{2,1,0:T(8,128)S(1)}, f32[1,64,256]{2,1,0:T(8,128)S(1)}, u32[]{:S(2)}, u32[]{:S(2)}) collective-permute-start(f32[1,64,256]{2,1,0:T(8,128)S(1)} %bitcast.55), channel_id=1, source_target_pairs={{0,8},{1,9},{2,10},{3,11},{4,12},{5,13},{6,14},{7,15},{8,0},{9,1},... | collective-permute-start | bytes 196616 | tf_op jit(solution)/shard_map/ppermute | solution.py:247
  44.2 2.4 %collective-permute-done.9 = f32[1,64,256]{2,1,0:T(8,128)S(1)} collective-permute-done((f32[1,64,256]{2,1,0:T(8,128)S(1)}, f32[1,64,256]{2,1,0:T(8,128)S(1)}, u32[]{:S(2)}, u32[]{:S(2)}) %collective-permute-start.9) | collective-permute-done | bytes 65568 | tf_op jit(solution)/shard_map/ppermute | solution.py:247
  46.6 1.3 %collective-permute-done.8 = f32[1,64,256]{2,1,0:T(8,128)S(1)} collective-permute-done((f32[1,64,256]{2,1,0:T(8,128)S(1)}, f32[1,64,256]{2,1,0:T(8,128)S(1)}, u32[]{:S(2)}, u32[]{:S(2)}) %collective-permute-start.8) | collective-permute-done | bytes 65568 | tf_op jit(solution)/shard_map/ppermute | solution.py:247
  48.0 1.5 %collective-permute-start.12 = (f32[4,64,256]{2,1,0:T(8,128)S(1)}, f32[4,64,256]{2,1,0:T(8,128)S(1)}, u32[]{:S(2)}, u32[]{:S(2)}) collective-permute-start(f32[4,64,256]{2,1,0:T(8,128)S(1)} %get-tuple-element.18), channel_id=1, source_target_pairs={{0,6},{1,7},{2,4},{3,5},{4,2},{5,3},{6,0},{7,1},{8,14},{9,15},{10,... | collective-permute-start | bytes 786440 | tf_op jit(solution)/shard_map/ppermute | solution.py:247
  49.5 1.3 %collective-permute-start.11 = (f32[4,64,256]{2,1,0:T(8,128)S(1)}, f32[4,64,256]{2,1,0:T(8,128)S(1)}, u32[]{:S(2)}, u32[]{:S(2)}) collective-permute-start(f32[4,64,256]{2,1,0:T(8,128)S(1)} %get-tuple-element.18), channel_id=1, source_target_pairs={{0,4},{1,5},{2,6},{3,7},{4,0},{5,1},{6,2},{7,3},{8,12},{9,13},{10,... | collective-permute-start | bytes 786440 | tf_op jit(solution)/shard_map/ppermute | solution.py:247
  50.8 0.8 collective-permute-start.10
  51.5 5.6 %collective-permute-done.12 = f32[4,64,256]{2,1,0:T(8,128)S(1)} collective-permute-done((f32[4,64,256]{2,1,0:T(8,128)S(1)}, f32[4,64,256]{2,1,0:T(8,128)S(1)}, u32[]{:S(2)}, u32[]{:S(2)}) %collective-permute-start.12) | collective-permute-done | bytes 262176 | tf_op jit(solution)/shard_map/ppermute | solution.py:247
  57.1 2.7 %collective-permute-done.11 = f32[4,64,256]{2,1,0:T(8,128)S(1)} collective-permute-done((f32[4,64,256]{2,1,0:T(8,128)S(1)}, f32[4,64,256]{2,1,0:T(8,128)S(1)}, u32[]{:S(2)}, u32[]{:S(2)}) %collective-permute-start.11) | collective-permute-done | bytes 262176 | tf_op jit(solution)/shard_map/ppermute | solution.py:247
  59.8 0.1 collective-permute-done.10
  59.9 0.1 pad_maximum_fusion
  60.0 0.1 copy.5
  60.1 0.1 collective-permute-start.13
  60.2 1.0 %copy-done = f32[1024,256]{1,0:T(8,128)S(1)} copy-done((f32[1024,256]{1,0:T(8,128)S(1)}, f32[1024,256]{1,0:T(8,128)}, u32[]{:S(2)}) %copy-start) | copy-done | bytes 1048600
  61.2 0.2 fusion
  61.4 1.4 %collective-permute-done.13.refs_1_ = f32[16,64,256]{2,1,0:T(8,128)S(1)} collective-permute-done((f32[16,64,256]{2,1,0:T(8,128)S(1)}, f32[16,64,256]{2,1,0:T(8,128)S(1)}, u32[]{:S(2)}, u32[]{:S(2)}) %collective-permute-start.13) | collective-permute-done | bytes 1048608 | tf_op jit(solution)/shard_map/ppermute | solution.py:247
  62.8 34.9 %iterate.1 = (f32[1024,256]{1,0:T(8,128)}, f32[2048,256]{1,0:T(8,128)}) custom-call(s32[1]{0:T(128)} %bitcast.me_ref, f32[16,64,256]{2,1,0:T(8,128)S(1)} %bitcast.43, f32[16,64,256]{2,1,0:T(8,128)S(1)} %collective-permute-done.13.refs_1_, f32[8,256]{1,0:T(8,128)S(1)} %fusion.6.refs_2_, bf16[1024,256]{1,0:T(8,128)(2,1)S(1)} %get-tuple-element.13.refs_3_, ...), custom_call_target="tpu_custom_call" | custom-call | tf_op jit(solution)/shard_map/iterate/pallas_call | solution.py:371
  (18 shorter events, 0.3 us)
Async XLA Ops:
  10.0 2.8 %collective-permute-start = (f32[1032,256]{1,0:T(8,128)S(1)}, f32[1032,256]{1,0:T(8,128)S(1)}, u32[]{:S(2)}, u32[]{:S(2)}) collective-permute-start(f32[1032,256]{1,0:T(8,128)S(1)} %get-tuple-element.8), channel_id=1, source_target_pairs={{0,1},{1,0},{2,3},{3,2},{4,5},{5,4},{6,7},{7,6},{8,9},{9,8},{10,11... | collective-permute-start | bytes 3170312 | tf_op jit(solution)/shard_map/ppermute | solution.py:247
  13.2 10.2 %collective-permute-start.3 = (f32[264,256]{1,0:T(8,128)S(1)}, f32[264,256]{1,0:T(8,128)S(1)}, u32[]{:S(2)}, u32[]{:S(2)}) collective-permute-start(f32[264,256]{1,0:T(8,128)S(1)} %get-tuple-element.25), channel_id=1, source_target_pairs={{0,2},{1,3},{2,0},{3,1},{4,6},{5,7},{6,4},{7,5},{8,10},{9,11},{10,... | collective-permute-start | bytes 811016 | tf_op jit(solution)/shard_map/ppermute | solution.py:247
  16.1 14.0 %collective-permute-start.2 = (f32[264,256]{1,0:T(8,128)S(1)}, f32[264,256]{1,0:T(8,128)S(1)}, u32[]{:S(2)}, u32[]{:S(2)}) collective-permute-start(f32[264,256]{1,0:T(8,128)S(1)} %get-tuple-element.26), channel_id=1, source_target_pairs={{0,4},{1,5},{2,6},{3,7},{4,0},{5,1},{6,2},{7,3},{8,12},{9,13},{10,... | collective-permute-start | bytes 811016 | tf_op jit(solution)/shard_map/ppermute | solution.py:247
  17.6 12.5 %collective-permute-start.1 = (f32[264,256]{1,0:T(8,128)S(1)}, f32[264,256]{1,0:T(8,128)S(1)}, u32[]{:S(2)}, u32[]{:S(2)}) collective-permute-start(f32[264,256]{1,0:T(8,128)S(1)} %get-tuple-element.27), channel_id=1, source_target_pairs={{0,6},{1,7},{2,4},{3,5},{4,2},{5,3},{6,0},{7,1},{8,14},{9,15},{10,... | collective-permute-start | bytes 811016 | tf_op jit(solution)/shard_map/ppermute | solution.py:247
  30.3 6.6 %collective-permute-start.4 = (f32[72,256]{1,0:T(8,128)S(1)}, f32[72,256]{1,0:T(8,128)S(1)}, u32[]{:S(2)}, u32[]{:S(2)}) collective-permute-start(f32[72,256]{1,0:T(8,128)S(1)} %get-tuple-element.22), channel_id=1, source_target_pairs={{0,24},{1,25},{2,26},{3,27},{4,28},{5,29},{6,30},{7,31},{8,16},{9,... | collective-permute-start | bytes 221192 | tf_op jit(solution)/shard_map/ppermute | solution.py:247
  34.0 5.7 %collective-permute-start.5 = (f32[72,256]{1,0:T(8,128)S(1)}, f32[72,256]{1,0:T(8,128)S(1)}, u32[]{:S(2)}, u32[]{:S(2)}) collective-permute-start(f32[72,256]{1,0:T(8,128)S(1)} %get-tuple-element.23), channel_id=1, source_target_pairs={{0,16},{1,17},{2,18},{3,19},{4,20},{5,21},{6,22},{7,23},{8,24},{9,... | collective-permute-start | bytes 221192 | tf_op jit(solution)/shard_map/ppermute | solution.py:247
  34.0 5.7 %collective-permute-start.6 = (f32[72,256]{1,0:T(8,128)S(1)}, f32[72,256]{1,0:T(8,128)S(1)}, u32[]{:S(2)}, u32[]{:S(2)}) collective-permute-start(f32[72,256]{1,0:T(8,128)S(1)} %get-tuple-element.24), channel_id=1, source_target_pairs={{0,8},{1,9},{2,10},{3,11},{4,12},{5,13},{6,14},{7,15},{8,0},{9,1},... | collective-permute-start | bytes 221192 | tf_op jit(solution)/shard_map/ppermute | solution.py:247
  39.8 6.9 %collective-permute-start.9 = (f32[1,64,256]{2,1,0:T(8,128)S(1)}, f32[1,64,256]{2,1,0:T(8,128)S(1)}, u32[]{:S(2)}, u32[]{:S(2)}) collective-permute-start(f32[1,64,256]{2,1,0:T(8,128)S(1)} %bitcast.53), channel_id=1, source_target_pairs={{0,24},{1,25},{2,26},{3,27},{4,28},{5,29},{6,30},{7,31},{8,16},{9,... | collective-permute-start | bytes 196616 | tf_op jit(solution)/shard_map/ppermute | solution.py:247
  42.3 5.6 %collective-permute-start.8 = (f32[1,64,256]{2,1,0:T(8,128)S(1)}, f32[1,64,256]{2,1,0:T(8,128)S(1)}, u32[]{:S(2)}, u32[]{:S(2)}) collective-permute-start(f32[1,64,256]{2,1,0:T(8,128)S(1)} %bitcast.54), channel_id=1, source_target_pairs={{0,16},{1,17},{2,18},{3,19},{4,20},{5,21},{6,22},{7,23},{8,24},{9,... | collective-permute-start | bytes 196616 | tf_op jit(solution)/shard_map/ppermute | solution.py:247
  42.3 5.6 %collective-permute-start.7 = (f32[1,64,256]{2,1,0:T(8,128)S(1)}, f32[1,64,256]{2,1,0:T(8,128)S(1)}, u32[]{:S(2)}, u32[]{:S(2)}) collective-permute-start(f32[1,64,256]{2,1,0:T(8,128)S(1)} %bitcast.55), channel_id=1, source_target_pairs={{0,8},{1,9},{2,10},{3,11},{4,12},{5,13},{6,14},{7,15},{8,0},{9,1},... | collective-permute-start | bytes 196616 | tf_op jit(solution)/shard_map/ppermute | solution.py:247
  48.0 9.2 %collective-permute-start.12 = (f32[4,64,256]{2,1,0:T(8,128)S(1)}, f32[4,64,256]{2,1,0:T(8,128)S(1)}, u32[]{:S(2)}, u32[]{:S(2)}) collective-permute-start(f32[4,64,256]{2,1,0:T(8,128)S(1)} %get-tuple-element.18), channel_id=1, source_target_pairs={{0,6},{1,7},{2,4},{3,5},{4,2},{5,3},{6,0},{7,1},{8,14},{9,15},{10,... | collective-permute-start | bytes 786440 | tf_op jit(solution)/shard_map/ppermute | solution.py:247
  49.5 10.4 %collective-permute-start.11 = (f32[4,64,256]{2,1,0:T(8,128)S(1)}, f32[4,64,256]{2,1,0:T(8,128)S(1)}, u32[]{:S(2)}, u32[]{:S(2)}) collective-permute-start(f32[4,64,256]{2,1,0:T(8,128)S(1)} %get-tuple-element.18), channel_id=1, source_target_pairs={{0,4},{1,5},{2,6},{3,7},{4,0},{5,1},{6,2},{7,3},{8,12},{9,13},{10,... | collective-permute-start | bytes 786440 | tf_op jit(solution)/shard_map/ppermute | solution.py:247
  50.8 9.1 %collective-permute-start.10 = (f32[4,64,256]{2,1,0:T(8,128)S(1)}, f32[4,64,256]{2,1,0:T(8,128)S(1)}, u32[]{:S(2)}, u32[]{:S(2)}) collective-permute-start(f32[4,64,256]{2,1,0:T(8,128)S(1)} %get-tuple-element.18), channel_id=1, source_target_pairs={{0,2},{1,3},{2,0},{3,1},{4,6},{5,7},{6,4},{7,5},{8,10},{9,11},{10,... | collective-permute-start | bytes 786440 | tf_op jit(solution)/shard_map/ppermute | solution.py:247
  60.0 1.2 %copy-start = (f32[1024,256]{1,0:T(8,128)S(1)}, f32[1024,256]{1,0:T(8,128)}, u32[]{:S(2)}) copy-start(f32[1024,256]{1,0:T(8,128)} %param.3) | copy-start | bytes 3145732
  60.1 2.7 %collective-permute-start.13 = (f32[16,64,256]{2,1,0:T(8,128)S(1)}, f32[16,64,256]{2,1,0:T(8,128)S(1)}, u32[]{:S(2)}, u32[]{:S(2)}) collective-permute-start(f32[16,64,256]{2,1,0:T(8,128)S(1)} %bitcast.42), channel_id=1, source_target_pairs={{0,1},{1,0},{2,3},{3,2},{4,5},{5,4},{6,7},{7,6},{8,9},{9,8},{10,11... | collective-permute-start | bytes 3145736 | tf_op jit(solution)/shard_map/ppermute | solution.py:247

commit v7 on v6

--- a/solution.py
+++ b/solution.py
@@ -247,9 +247,9 @@
     return lax.ppermute(x, "dp", [(d, d ^ flip) for d in range(devices)])
 
 
-def phases(bits):
+def phases(bits, width):
     groups = [[0]] if bits else []
-    return groups + [list(range(b, min(b + 2, bits))) for b in range(1, bits, 2)]
+    return groups + [list(range(b, min(b + width, bits))) for b in range(1, bits, width)]
 
 
 def spread(value, group):
@@ -269,7 +269,7 @@
     message = exchange(send, 1, devices)
     x = keep + message[:-extra].reshape(keep.shape)
     rider = rider + message[-extra:]
-    for group in phases(scattered)[1:]:
+    for group in phases(scattered, 3)[1:]:
         size = 1 << len(group)
         x = x.reshape(-1, size, rows, columns)
         count = x.shape[0]
@@ -285,7 +285,7 @@
         message = exchange(jnp.concatenate([x, rider], 0), 1 << bit, devices)
         x, rider = x + message[:rows], rider + message[rows:]
     parts = [x[None]]
-    for group in reversed(phases(scattered)):
+    for group in reversed(phases(scattered, 2)):
         x = jnp.stack(parts, 1).reshape(-1, rows, columns)
         parts = [x] + [exchange(x, spread(d, group), devices) for d in range(1, 1 << len(group))]
     return parts, rider

time: 98 us -> 96.6 us (0.986)
  waiting for transfers between devices: 33.2 us -> 24.8 us
  starting transfers between devices: 17.5 us -> 24.4 us
    ppermute x14 -> x16, waiting for transfers between devices: 33.2 us -> 24.8 us  [exchange(): return lax.ppermute(x, 'dp', [(d, d ^ flip) for d in range(devices)])]
    ppermute x14 -> x16, starting transfers between devices: 17.5 us -> 24.4 us  [exchange(): return lax.ppermute(x, 'dp', [(d, d ^ flip) for d in range(devices)])]
  transfers between devices with their start and end apart: 14 -> 16, of which waited for: 11 -> 9; matrix products, arithmetic and copies ran while one was open for 0% -> 0% of each run, Pallas kernels for 0% -> 0%
where the time goes in v7:
time: 96.6 us; the launch traced here: 96.4 us
  Pallas kernels  44.3 us (46%)
  waiting for transfers between devices  24.8 us (26%)
  starting transfers between devices  24.4 us (25%)
  local copies, waits for them, and re-layouts  1.33 us (1%)
  between operations  1.02 us (1%)
    pallas_call x1, Pallas kernels, iterate(): pl.pallas_call(functools.partial(iterate_kernel, scale, len(summed)), in_...  34.9 us
    ppermute x16, waiting for transfers between devices, exchange(): return lax.ppermute(x, 'dp', [(d, d ^ flip) for d in range(devices)])  24.8 us
    ppermute x16, starting transfers between devices, exchange(): return lax.ppermute(x, 'dp', [(d, d ^ flip) for d in range(devices)])  24.4 us
    pallas_call x1, Pallas kernels, moments(): pl.pallas_call(functools.partial(moments_kernel, bounds), in_specs=[pl.Bl...  9.36 us
  transfers between devices with their start and end apart: 16, of which 9 were waited for; matrix products, arithmetic and copies ran while one was open for 0% of the time, Pallas kernels for 0%

profile of v7, /device:TPU:0, one launch (start us, length us, event | category | flops | bytes accessed | tf_op | source)
XLA Modules:
  0.0 96.4 jit_solution(9958835148857757944)
XLA Ops:
  0.6 9.4 %moments.1 = (f32[16,64,256]{2,1,0:T(8,128)S(1)}, f32[1032,256]{1,0:T(8,128)S(1)}, f32[8,256]{1,0:T(8,128)S(1)}) custom-call(s32[1]{0:T(128)} %bitcast.me_ref, f32[2048,1024]{1,0:T(8,128)} %refs_5_.1), custom_call_target="tpu_custom_call" | custom-call | tf_op jit(solution)/shard_map/moments/pallas_call | solution.py:226
  10.0 0.5 collective-permute-start
  10.5 2.3 %collective-permute-done = f32[1032,256]{1,0:T(8,128)S(1)} collective-permute-done((f32[1032,256]{1,0:T(8,128)S(1)}, f32[1032,256]{1,0:T(8,128)S(1)}, u32[]{:S(2)}, u32[]{:S(2)}) %collective-permute-start) | collective-permute-done | bytes 1056800 | tf_op jit(solution)/shard_map/ppermute | solution.py:247
  12.9 0.1 add.111
  13.1 0.1 pad_maximum_fusion.1
  13.2 2.9 %collective-permute-start.7 = (f32[136,256]{1,0:T(8,128)S(1)}, f32[136,256]{1,0:T(8,128)S(1)}, u32[]{:S(2)}, u32[]{:S(2)}) collective-permute-start(f32[136,256]{1,0:T(8,128)S(1)} %get-tuple-element.25), channel_id=1, source_target_pairs={{0,2},{1,3},{2,0},{3,1},{4,6},{5,7},{6,4},{7,5},{8,10},{9,11},{10,... | collective-permute-start | bytes 417800 | tf_op jit(solution)/shard_map/ppermute | solution.py:247
  16.1 2.5 %collective-permute-start.2 = (f32[136,256]{1,0:T(8,128)S(1)}, f32[136,256]{1,0:T(8,128)S(1)}, u32[]{:S(2)}, u32[]{:S(2)}) collective-permute-start(f32[136,256]{1,0:T(8,128)S(1)} %get-tuple-element.26), channel_id=1, source_target_pairs={{0,12},{1,13},{2,14},{3,15},{4,8},{5,9},{6,10},{7,11},{8,4},{9,5},... | collective-permute-start | bytes 417800 | tf_op jit(solution)/shard_map/ppermute | solution.py:247
  18.7 0.4 collective-permute-start.3
  19.1 1.6 %collective-permute-start.4 = (f32[136,256]{1,0:T(8,128)S(1)}, f32[136,256]{1,0:T(8,128)S(1)}, u32[]{:S(2)}, u32[]{:S(2)}) collective-permute-start(f32[136,256]{1,0:T(8,128)S(1)} %get-tuple-element.28), channel_id=1, source_target_pairs={{0,8},{1,9},{2,10},{3,11},{4,12},{5,13},{6,14},{7,15},{8,0},{9,1},... | collective-permute-start | bytes 417800 | tf_op jit(solution)/shard_map/ppermute | solution.py:247
  20.7 1.4 %collective-permute-start.5 = (f32[136,256]{1,0:T(8,128)S(1)}, f32[136,256]{1,0:T(8,128)S(1)}, u32[]{:S(2)}, u32[]{:S(2)}) collective-permute-start(f32[136,256]{1,0:T(8,128)S(1)} %get-tuple-element.29), channel_id=1, source_target_pairs={{0,6},{1,7},{2,4},{3,5},{4,2},{5,3},{6,0},{7,1},{8,14},{9,15},{10,... | collective-permute-start | bytes 417800 | tf_op jit(solution)/shard_map/ppermute | solution.py:247
  22.1 1.5 %collective-permute-start.6 = (f32[136,256]{1,0:T(8,128)S(1)}, f32[136,256]{1,0:T(8,128)S(1)}, u32[]{:S(2)}, u32[]{:S(2)}) collective-permute-start(f32[136,256]{1,0:T(8,128)S(1)} %get-tuple-element.30), channel_id=1, source_target_pairs={{0,4},{1,5},{2,6},{3,7},{4,0},{5,1},{6,2},{7,3},{8,12},{9,13},{10,... | collective-permute-start | bytes 417800 | tf_op jit(solution)/shard_map/ppermute | solution.py:247
  23.7 2.6 %collective-permute-start.1 = (f32[136,256]{1,0:T(8,128)S(1)}, f32[136,256]{1,0:T(8,128)S(1)}, u32[]{:S(2)}, u32[]{:S(2)}) collective-permute-start(f32[136,256]{1,0:T(8,128)S(1)} %get-tuple-element.31), channel_id=1, source_target_pairs={{0,14},{1,15},{2,12},{3,13},{4,10},{5,11},{6,8},{7,9},{8,6},{9,7},... | collective-permute-start | bytes 417800 | tf_op jit(solution)/shard_map/ppermute | solution.py:247
  26.4 3.3 %collective-permute-done.4 = f32[136,256]{1,0:T(8,128)S(1)} collective-permute-done((f32[136,256]{1,0:T(8,128)S(1)}, f32[136,256]{1,0:T(8,128)S(1)}, u32[]{:S(2)}, u32[]{:S(2)}) %collective-permute-start.4) | collective-permute-done | bytes 139296 | tf_op jit(solution)/shard_map/ppermute | solution.py:247
  29.7 2.9 %collective-permute-done.6 = f32[136,256]{1,0:T(8,128)S(1)} collective-permute-done((f32[136,256]{1,0:T(8,128)S(1)}, f32[136,256]{1,0:T(8,128)S(1)}, u32[]{:S(2)}, u32[]{:S(2)}) %collective-permute-start.6) | collective-permute-done | bytes 139296 | tf_op jit(solution)/shard_map/ppermute | solution.py:247
  32.7 2.7 %collective-permute-start.8 = (f32[72,256]{1,0:T(8,128)S(1)}, f32[72,256]{1,0:T(8,128)S(1)}, u32[]{:S(2)}, u32[]{:S(2)}) collective-permute-start(f32[72,256]{1,0:T(8,128)S(1)} %pad_maximum_fusion.9), channel_id=1, source_target_pairs={{0,16},{1,17},{2,18},{3,19},{4,20},{5,21},{6,22},{7,23},{8,24},{9,... | collective-permute-start | bytes 221192 | tf_op jit(solution)/shard_map/ppermute | solution.py:247
  35.4 3.4 %collective-permute-done.8 = f32[72,256]{1,0:T(8,128)S(1)} collective-permute-done((f32[72,256]{1,0:T(8,128)S(1)}, f32[72,256]{1,0:T(8,128)S(1)}, u32[]{:S(2)}, u32[]{:S(2)}) %collective-permute-start.8) | collective-permute-done | bytes 73760 | tf_op jit(solution)/shard_map/ppermute | solution.py:247
  38.9 2.1 %collective-permute-start.11 = (f32[1,64,256]{2,1,0:T(8,128)S(1)}, f32[1,64,256]{2,1,0:T(8,128)S(1)}, u32[]{:S(2)}, u32[]{:S(2)}) collective-permute-start(f32[1,64,256]{2,1,0:T(8,128)S(1)} %get-tuple-element.24), channel_id=1, source_target_pairs={{0,24},{1,25},{2,26},{3,27},{4,28},{5,29},{6,30},{7,31},{8,16},{9,... | collective-permute-start | bytes 196616 | tf_op jit(solution)/shard_map/ppermute | solution.py:247
  41.0 2.3 %collective-permute-start.9 = (f32[1,64,256]{2,1,0:T(8,128)S(1)}, f32[1,64,256]{2,1,0:T(8,128)S(1)}, u32[]{:S(2)}, u32[]{:S(2)}) collective-permute-start(f32[1,64,256]{2,1,0:T(8,128)S(1)} %get-tuple-element.24), channel_id=1, source_target_pairs={{0,8},{1,9},{2,10},{3,11},{4,12},{5,13},{6,14},{7,15},{8,0},{9,1},... | collective-permute-start | bytes 196616 | tf_op jit(solution)/shard_map/ppermute | solution.py:247
  43.3 1.7 %collective-permute-done.11 = f32[1,64,256]{2,1,0:T(8,128)S(1)} collective-permute-done((f32[1,64,256]{2,1,0:T(8,128)S(1)}, f32[1,64,256]{2,1,0:T(8,128)S(1)}, u32[]{:S(2)}, u32[]{:S(2)}) %collective-permute-start.11) | collective-permute-done | bytes 65568 | tf_op jit(solution)/shard_map/ppermute | solution.py:247
  45.0 1.7 %collective-permute-done.10 = f32[1,64,256]{2,1,0:T(8,128)S(1)} collective-permute-done((f32[1,64,256]{2,1,0:T(8,128)S(1)}, f32[1,64,256]{2,1,0:T(8,128)S(1)}, u32[]{:S(2)}, u32[]{:S(2)}) %collective-permute-start.10) | collective-permute-done | bytes 65568 | tf_op jit(solution)/shard_map/ppermute | solution.py:247
  46.8 2.3 %collective-permute-start.14 = (f32[4,64,256]{2,1,0:T(8,128)S(1)}, f32[4,64,256]{2,1,0:T(8,128)S(1)}, u32[]{:S(2)}, u32[]{:S(2)}) collective-permute-start(f32[4,64,256]{2,1,0:T(8,128)S(1)} %get-tuple-element.22), channel_id=1, source_target_pairs={{0,6},{1,7},{2,4},{3,5},{4,2},{5,3},{6,0},{7,1},{8,14},{9,15},{10,... | collective-permute-start | bytes 786440 | tf_op jit(solution)/shard_map/ppermute | solution.py:247
  49.1 0.7 collective-permute-start.13
  49.9 0.5 collective-permute-start.12
  50.3 5.4 %collective-permute-done.14 = f32[4,64,256]{2,1,0:T(8,128)S(1)} collective-permute-done((f32[4,64,256]{2,1,0:T(8,128)S(1)}, f32[4,64,256]{2,1,0:T(8,128)S(1)}, u32[]{:S(2)}, u32[]{:S(2)}) %collective-permute-start.14) | collective-permute-done | bytes 262176 | tf_op jit(solution)/shard_map/ppermute | solution.py:247
  55.7 2.7 %collective-permute-done.13 = f32[4,64,256]{2,1,0:T(8,128)S(1)} collective-permute-done((f32[4,64,256]{2,1,0:T(8,128)S(1)}, f32[4,64,256]{2,1,0:T(8,128)S(1)}, u32[]{:S(2)}, u32[]{:S(2)}) %collective-permute-start.13) | collective-permute-done | bytes 262176 | tf_op jit(solution)/shard_map/ppermute | solution.py:247
  58.4 0.1 pad_maximum_fusion
  58.5 0.1 copy.5
  58.6 0.1 collective-permute-start.15
  58.7 1.0 %copy-done = f32[1024,256]{1,0:T(8,128)S(1)} copy-done((f32[1024,256]{1,0:T(8,128)S(1)}, f32[1024,256]{1,0:T(8,128)}, u32[]{:S(2)}) %copy-start) | copy-done | bytes 1048600
  59.7 0.2 fusion
  59.9 1.4 %collective-permute-done.15.refs_1_ = f32[16,64,256]{2,1,0:T(8,128)S(1)} collective-permute-done((f32[16,64,256]{2,1,0:T(8,128)S(1)}, f32[16,64,256]{2,1,0:T(8,128)S(1)}, u32[]{:S(2)}, u32[]{:S(2)}) %collective-permute-start.15) | collective-permute-done | bytes 1048608 | tf_op jit(solution)/shard_map/ppermute | solution.py:247
  61.3 34.9 %iterate.1 = (f32[1024,256]{1,0:T(8,128)}, f32[2048,256]{1,0:T(8,128)}) custom-call(s32[1]{0:T(128)} %bitcast.me_ref, f32[16,64,256]{2,1,0:T(8,128)S(1)} %bitcast.61, f32[16,64,256]{2,1,0:T(8,128)S(1)} %collective-permute-done.15.refs_1_, f32[8,256]{1,0:T(8,128)S(1)} %slice_add_fusion.1.refs_2_, bf16[1024,256]{1,0:T(8,128)(2,1)S(1)} %get-tuple-element.13.refs_3_, ...), custom_call_target="tpu_custom_call" | custom-call | tf_op jit(solution)/shard_map/iterate/pallas_call | solution.py:371
  (26 shorter events, 0.4 us)
Async XLA Ops:
  10.0 2.8 %collective-permute-start = (f32[1032,256]{1,0:T(8,128)S(1)}, f32[1032,256]{1,0:T(8,128)S(1)}, u32[]{:S(2)}, u32[]{:S(2)}) collective-permute-start(f32[1032,256]{1,0:T(8,128)S(1)} %get-tuple-element.8), channel_id=1, source_target_pairs={{0,1},{1,0},{2,3},{3,2},{4,5},{5,4},{6,7},{7,6},{8,9},{9,8},{10,11... | collective-permute-start | bytes 3170312 | tf_op jit(solution)/shard_map/ppermute | solution.py:247
  13.2 8.9 %collective-permute-start.7 = (f32[136,256]{1,0:T(8,128)S(1)}, f32[136,256]{1,0:T(8,128)S(1)}, u32[]{:S(2)}, u32[]{:S(2)}) collective-permute-start(f32[136,256]{1,0:T(8,128)S(1)} %get-tuple-element.25), channel_id=1, source_target_pairs={{0,2},{1,3},{2,0},{3,1},{4,6},{5,7},{6,4},{7,5},{8,10},{9,11},{10,... | collective-permute-start | bytes 417800 | tf_op jit(solution)/shard_map/ppermute | solution.py:247
  16.1 7.5 %collective-permute-start.2 = (f32[136,256]{1,0:T(8,128)S(1)}, f32[136,256]{1,0:T(8,128)S(1)}, u32[]{:S(2)}, u32[]{:S(2)}) collective-permute-start(f32[136,256]{1,0:T(8,128)S(1)} %get-tuple-element.26), channel_id=1, source_target_pairs={{0,12},{1,13},{2,14},{3,15},{4,8},{5,9},{6,10},{7,11},{8,4},{9,5},... | collective-permute-start | bytes 417800 | tf_op jit(solution)/shard_map/ppermute | solution.py:247
  18.7 7.7 %collective-permute-start.3 = (f32[136,256]{1,0:T(8,128)S(1)}, f32[136,256]{1,0:T(8,128)S(1)}, u32[]{:S(2)}, u32[]{:S(2)}) collective-permute-start(f32[136,256]{1,0:T(8,128)S(1)} %get-tuple-element.27), channel_id=1, source_target_pairs={{0,10},{1,11},{2,8},{3,9},{4,14},{5,15},{6,12},{7,13},{8,2},{9,3},... | collective-permute-start | bytes 417800 | tf_op jit(solution)/shard_map/ppermute | solution.py:247
  19.1 10.5 %collective-permute-start.4 = (f32[136,256]{1,0:T(8,128)S(1)}, f32[136,256]{1,0:T(8,128)S(1)}, u32[]{:S(2)}, u32[]{:S(2)}) collective-permute-start(f32[136,256]{1,0:T(8,128)S(1)} %get-tuple-element.28), channel_id=1, source_target_pairs={{0,8},{1,9},{2,10},{3,11},{4,12},{5,13},{6,14},{7,15},{8,0},{9,1},... | collective-permute-start | bytes 417800 | tf_op jit(solution)/shard_map/ppermute | solution.py:247
  20.7 9.0 %collective-permute-start.5 = (f32[136,256]{1,0:T(8,128)S(1)}, f32[136,256]{1,0:T(8,128)S(1)}, u32[]{:S(2)}, u32[]{:S(2)}) collective-permute-start(f32[136,256]{1,0:T(8,128)S(1)} %get-tuple-element.29), channel_id=1, source_target_pairs={{0,6},{1,7},{2,4},{3,5},{4,2},{5,3},{6,0},{7,1},{8,14},{9,15},{10,... | collective-permute-start | bytes 417800 | tf_op jit(solution)/shard_map/ppermute | solution.py:247
  22.1 10.4 %collective-permute-start.6 = (f32[136,256]{1,0:T(8,128)S(1)}, f32[136,256]{1,0:T(8,128)S(1)}, u32[]{:S(2)}, u32[]{:S(2)}) collective-permute-start(f32[136,256]{1,0:T(8,128)S(1)} %get-tuple-element.30), channel_id=1, source_target_pairs={{0,4},{1,5},{2,6},{3,7},{4,0},{5,1},{6,2},{7,3},{8,12},{9,13},{10,... | collective-permute-start | bytes 417800 | tf_op jit(solution)/shard_map/ppermute | solution.py:247
  23.7 8.9 %collective-permute-start.1 = (f32[136,256]{1,0:T(8,128)S(1)}, f32[136,256]{1,0:T(8,128)S(1)}, u32[]{:S(2)}, u32[]{:S(2)}) collective-permute-start(f32[136,256]{1,0:T(8,128)S(1)} %get-tuple-element.31), channel_id=1, source_target_pairs={{0,14},{1,15},{2,12},{3,13},{4,10},{5,11},{6,8},{7,9},{8,6},{9,7},... | collective-permute-start | bytes 417800 | tf_op jit(solution)/shard_map/ppermute | solution.py:247
  32.7 6.1 %collective-permute-start.8 = (f32[72,256]{1,0:T(8,128)S(1)}, f32[72,256]{1,0:T(8,128)S(1)}, u32[]{:S(2)}, u32[]{:S(2)}) collective-permute-start(f32[72,256]{1,0:T(8,128)S(1)} %pad_maximum_fusion.9), channel_id=1, source_target_pairs={{0,16},{1,17},{2,18},{3,19},{4,20},{5,21},{6,22},{7,23},{8,24},{9,... | collective-permute-start | bytes 221192 | tf_op jit(solution)/shard_map/ppermute | solution.py:247
  38.9 6.1 %collective-permute-start.11 = (f32[1,64,256]{2,1,0:T(8,128)S(1)}, f32[1,64,256]{2,1,0:T(8,128)S(1)}, u32[]{:S(2)}, u32[]{:S(2)}) collective-permute-start(f32[1,64,256]{2,1,0:T(8,128)S(1)} %get-tuple-element.24), channel_id=1, source_target_pairs={{0,24},{1,25},{2,26},{3,27},{4,28},{5,29},{6,30},{7,31},{8,16},{9,... | collective-permute-start | bytes 196616 | tf_op jit(solution)/shard_map/ppermute | solution.py:247
  41.0 5.8 %collective-permute-start.10 = (f32[1,64,256]{2,1,0:T(8,128)S(1)}, f32[1,64,256]{2,1,0:T(8,128)S(1)}, u32[]{:S(2)}, u32[]{:S(2)}) collective-permute-start(f32[1,64,256]{2,1,0:T(8,128)S(1)} %get-tuple-element.24), channel_id=1, source_target_pairs={{0,16},{1,17},{2,18},{3,19},{4,20},{5,21},{6,22},{7,23},{8,24},{9,... | collective-permute-start | bytes 196616 | tf_op jit(solution)/shard_map/ppermute | solution.py:247
  41.0 5.8 %collective-permute-start.9 = (f32[1,64,256]{2,1,0:T(8,128)S(1)}, f32[1,64,256]{2,1,0:T(8,128)S(1)}, u32[]{:S(2)}, u32[]{:S(2)}) collective-permute-start(f32[1,64,256]{2,1,0:T(8,128)S(1)} %get-tuple-element.24), channel_id=1, source_target_pairs={{0,8},{1,9},{2,10},{3,11},{4,12},{5,13},{6,14},{7,15},{8,0},{9,1},... | collective-permute-start | bytes 196616 | tf_op jit(solution)/shard_map/ppermute | solution.py:247
  46.8 9.0 %collective-permute-start.14 = (f32[4,64,256]{2,1,0:T(8,128)S(1)}, f32[4,64,256]{2,1,0:T(8,128)S(1)}, u32[]{:S(2)}, u32[]{:S(2)}) collective-permute-start(f32[4,64,256]{2,1,0:T(8,128)S(1)} %get-tuple-element.22), channel_id=1, source_target_pairs={{0,6},{1,7},{2,4},{3,5},{4,2},{5,3},{6,0},{7,1},{8,14},{9,15},{10,... | collective-permute-start | bytes 786440 | tf_op jit(solution)/shard_map/ppermute | solution.py:247
  49.1 9.3 %collective-permute-start.13 = (f32[4,64,256]{2,1,0:T(8,128)S(1)}, f32[4,64,256]{2,1,0:T(8,128)S(1)}, u32[]{:S(2)}, u32[]{:S(2)}) collective-permute-start(f32[4,64,256]{2,1,0:T(8,128)S(1)} %get-tuple-element.22), channel_id=1, source_target_pairs={{0,4},{1,5},{2,6},{3,7},{4,0},{5,1},{6,2},{7,3},{8,12},{9,13},{10,... | collective-permute-start | bytes 786440 | tf_op jit(solution)/shard_map/ppermute | solution.py:247
  49.9 8.6 %collective-permute-start.12 = (f32[4,64,256]{2,1,0:T(8,128)S(1)}, f32[4,64,256]{2,1,0:T(8,128)S(1)}, u32[]{:S(2)}, u32[]{:S(2)}) collective-permute-start(f32[4,64,256]{2,1,0:T(8,128)S(1)} %get-tuple-element.22), channel_id=1, source_target_pairs={{0,2},{1,3},{2,0},{3,1},{4,6},{5,7},{6,4},{7,5},{8,10},{9,11},{10,... | collective-permute-start | bytes 786440 | tf_op jit(solution)/shard_map/ppermute | solution.py:247
  58.5 1.2 %copy-start = (f32[1024,256]{1,0:T(8,128)S(1)}, f32[1024,256]{1,0:T(8,128)}, u32[]{:S(2)}) copy-start(f32[1024,256]{1,0:T(8,128)} %param.3) | copy-start | bytes 3145732
  58.6 2.7 %collective-permute-start.15 = (f32[16,64,256]{2,1,0:T(8,128)S(1)}, f32[16,64,256]{2,1,0:T(8,128)S(1)}, u32[]{:S(2)}, u32[]{:S(2)}) collective-permute-start(f32[16,64,256]{2,1,0:T(8,128)S(1)} %bitcast.60), channel_id=1, source_target_pairs={{0,1},{1,0},{2,3},{3,2},{4,5},{5,4},{6,7},{7,6},{8,9},{9,8},{10,11... | collective-permute-start | bytes 3145736 | tf_op jit(solution)/shard_map/ppermute | solution.py:247
